TPU v7x, 32 devices: a whole 2x2x4 slice. The times are simulated.
32 devices in a mesh: blk: 8 (over y, x, core), uly: 4 (over z).
Axes of the slice: x: 2, y: 2, z: 4, core: 2. Of those that a mesh axis runs over, the one named last changes fastest.
Arguments:
- tokens: bfloat16 [2, 4096, 2048], P(None, ('blk', 'uly')), may hold values from -6 to 6
- retain_gain: bfloat16 [2048], P('blk'), may hold values from 0.5 to 1.5
- query_weight: bfloat16 [2048, 2048], P('blk', 'uly'), may hold values from -0.125 to 0.125
- key_weight: bfloat16 [2048, 2048], P('blk', 'uly'), may hold values from -0.125 to 0.125
- value_weight: bfloat16 [2048, 4096], P('blk', 'uly'), may hold values from -0.125 to 0.125
- gate_matrix: bfloat16 [2048, 4096], P('blk', 'uly'), may hold values from -0.125 to 0.125
- output_weight: bfloat16 [4096, 2048], P('uly', 'blk'), may hold values from -0.125 to 0.125
- feed_gain: bfloat16 [2048], P('blk'), may hold values from 0.5 to 1.5
- up_weight: bfloat16 [2048, 4096], P('blk', 'uly'), may hold values from -0.125 to 0.125
- down_weight: bfloat16 [4096, 2048], P('uly', 'blk'), may hold values from -0.125 to 0.125
- decay_rate: float32 [8], replicated, may hold values from 0.00025 to 0.04
- lengths: int32 [2, 2], replicated, may hold values from 1024 to 3072, as said below
- out_grad: bfloat16 [2, 4096, 2048], P(None, ('blk', 'uly')), may hold values from -6 to 6
Outputs:
- block_out: bfloat16 [2, 4096, 2048], P(None, ('blk', 'uly'))
- input_grad: float32 [2, 4096, 2048], P(None, ('blk', 'uly'))
- retain_gain_grad: float32 [2048], P('blk')
- query_grad: float32 [2048, 2048], P('blk', 'uly')
- key_grad: float32 [2048, 2048], P('blk', 'uly')
- value_grad: float32 [2048, 4096], P('blk', 'uly')
- gate_grad: float32 [2048, 4096], P('blk', 'uly')
- output_grad: float32 [4096, 2048], P('uly', 'blk')
- feed_gain_grad: float32 [2048], P('blk')
- up_grad: float32 [2048, 4096], P('blk', 'uly')
- down_grad: float32 [4096, 2048], P('uly', 'blk')
Inputs may be any that keep to these rules, and one draw needn't show every extreme that they name: Each row holds 2 sequence lengths that sum to 4096; every one is at least 1024 and the longest of each row is exactly 3072.
All inputs are finite; a program needn't handle non-finite values.
Results may differ from a plain program's by a relative error of at most 0.015.
The roundings to bfloat16 on the way count: a program that leaves them out, or rounds other values in their place, can miss the bound.
Values may be sent and summed in bfloat16 or wider, within the bound.
A program may use at most 320 MiB of HBM per device.

v0:
```python
from functools import partial

import jax
import jax.numpy as jnp
from jax import lax
from jax.sharding import PartitionSpec as P

EPSILON = 1e-05
TOP_PRECISION = lax.Precision.HIGHEST


def prefix(part, axis, combine, identity):
    place = lax.axis_index(axis)
    gathered = jax.tree.map(lambda a: lax.all_gather(a, axis), part)
    state = jax.tree.map(lambda a, e: jnp.zeros_like(a) + jnp.asarray(e, a.dtype), part, identity)

    def prefix_one(lap, state):
        return combine(
            state, jax.tree.map(lambda a: lax.dynamic_index_in_dim(a, lap, 0, False), gathered)
        )

    return lax.fori_loop(0, place, prefix_one, state)


def carried_in(shard, axis, join, neutral):
    count = lax.axis_size(axis)
    place = lax.axis_index(axis)
    ahead = count - 1 - place
    gathered = jax.tree.map(
        lambda a, kind: lax.all_gather(a.astype(kind), axis),
        shard,
        jax.tree.map(lambda a: jnp.bfloat16 if a.dtype == jnp.float32 else a.dtype, shard),
    )
    state = jax.tree.map(lambda a, e: jnp.zeros_like(a) + jnp.asarray(e, a.dtype), shard, neutral)

    def carried_one(lap, state):
        source = count - 1 - lap
        return join(
            state,
            jax.tree.map(
                lambda a, own: lax.dynamic_index_in_dim(a, source, 0, False).astype(own.dtype),
                gathered,
                shard,
            ),
        )

    return lax.fori_loop(0, ahead, carried_one, state)


def layer_norm(values, gain_row):
    center = values - jnp.mean(values, axis=-1, keepdims=True)
    spread = jnp.mean(center * center, axis=-1, keepdims=True)
    return center * lax.rsqrt(spread + EPSILON) * gain_row


def group_norm(values):
    center = values - jnp.mean(values, axis=-1, keepdims=True)
    spread = jnp.mean(center * center, axis=-1, keepdims=True)
    return center * lax.rsqrt(spread + EPSILON)


def swish(values):
    return values * jax.nn.sigmoid(values)


def gelu_tanh(values):
    return jax.nn.gelu(values, approximate=True)


def segment_ids(positions, lengths_row):
    bounds = jnp.cumsum(lengths_row) - lengths_row
    return jnp.sum((bounds[None, :] <= positions[:, None]).astype(jnp.int32), axis=1)


def retention_parts(rate_row, seg_local, seg_prev, length):
    places = jnp.arange(length).astype(rate_row.dtype)
    offset = places[:, None] - places[None, :]
    causal = (offset >= 0) & (seg_local[:, None] == seg_local[None, :])
    decay_table = jnp.exp(-rate_row[:, None, None] * jnp.maximum(offset, 0.0)[None])
    inner_width = jnp.where(causal[None], decay_table, 0.0)
    carry_in = (seg_local == seg_prev).astype(rate_row.dtype)
    entry = carry_in[None, :] * jnp.exp(-rate_row[:, None] * (places[None, :] + 1.0))
    carry_out = (seg_local == seg_local[length - 1]).astype(rate_row.dtype)
    leave = carry_out[None, :] * jnp.exp(-rate_row[:, None] * (length - 1.0 - places[None, :]))
    through = (seg_local[length - 1] == seg_prev).astype(rate_row.dtype) * jnp.exp(
        -rate_row * length
    )
    return (inner_width, entry, leave, through)


def state_local(leave, head_keys, value_heads):
    return jnp.einsum(
        "hld,hle->hde", head_keys * leave[:, :, None], value_heads, precision=TOP_PRECISION
    )


def read_out(inner_width, entry, head_queries, head_keys, value_heads, state_in):
    score_matrix = (
        jnp.einsum("eng,ekg->enk", head_queries, head_keys, precision=TOP_PRECISION) * inner_width
    )
    local_part = jnp.einsum("hlm,hme->hle", score_matrix, value_heads, precision=TOP_PRECISION)
    carried = jnp.einsum("hld,hde->hle", head_queries, state_in, precision=TOP_PRECISION)
    return local_part + entry[:, :, None] * carried


def to_heads(row_block, head_count):
    return row_block.reshape(row_block.shape[0], head_count, -1).transpose(1, 0, 2)


def from_heads(head_block):
    return head_block.transpose(1, 0, 2).reshape(head_block.shape[1], -1)


def gate_mix(gate_rows, retained):
    return swish(gate_rows) * from_heads(group_norm(retained))


def chain(earlier, later):
    return (earlier[0] * later[0], later[1] + later[0][:, None, None] * earlier[1])


def matmul(left_side, right_side):
    return jnp.dot(left_side, right_side, preferred_element_type=jnp.float32)


def inner_rows(left_side, right_side):
    return lax.dot_general(
        left_side, right_side, (((0,), (0,)), ((), ())), preferred_element_type=jnp.float32
    )


def outer_cols(left_side, right_side):
    return lax.dot_general(
        left_side, right_side, (((1,), (1,)), ((), ())), preferred_element_type=jnp.float32
    )


def spread(row_block):
    return lax.all_gather(row_block, "uly", axis=0, tiled=True)


def collect(partial_rows):
    return lax.psum_scatter(partial_rows, "uly", scatter_dimension=0, tiled=True)


def fetch(shards):
    front_set = (
        lax.all_gather(shards[0], "blk", axis=0, tiled=True),
        lax.all_gather(shards[1], "blk", axis=0, tiled=True),
        lax.all_gather(shards[2], "blk", axis=0, tiled=True),
        lax.all_gather(shards[3], "blk", axis=0, tiled=True),
        lax.all_gather(shards[4], "blk", axis=0, tiled=True),
        lax.all_gather(shards[6], "blk", axis=0, tiled=True),
        lax.all_gather(shards[7], "blk", axis=0, tiled=True),
    )
    back_set = (
        lax.all_gather(shards[5], "blk", axis=1, tiled=True),
        lax.all_gather(shards[8], "blk", axis=1, tiled=True),
    )
    return (
        front_set[0].astype(jnp.float32),
        front_set[1],
        front_set[2],
        front_set[3],
        front_set[4],
        back_set[0],
        front_set[5].astype(jnp.float32),
        front_set[6],
        back_set[1],
    )


def reduce_grads(grad_set):
    front_set = (
        lax.psum_scatter(
            grad_set[0].astype(jnp.bfloat16), "blk", scatter_dimension=0, tiled=True
        ).astype(jnp.float32),
        lax.psum_scatter(
            grad_set[1].astype(jnp.bfloat16), "blk", scatter_dimension=0, tiled=True
        ).astype(jnp.float32),
        lax.psum_scatter(
            grad_set[2].astype(jnp.bfloat16), "blk", scatter_dimension=0, tiled=True
        ).astype(jnp.float32),
        lax.psum_scatter(
            grad_set[3].astype(jnp.bfloat16), "blk", scatter_dimension=0, tiled=True
        ).astype(jnp.float32),
        lax.psum_scatter(
            grad_set[4].astype(jnp.bfloat16), "blk", scatter_dimension=0, tiled=True
        ).astype(jnp.float32),
        lax.psum_scatter(
            grad_set[6].astype(jnp.bfloat16), "blk", scatter_dimension=0, tiled=True
        ).astype(jnp.float32),
        lax.psum_scatter(
            grad_set[7].astype(jnp.bfloat16), "blk", scatter_dimension=0, tiled=True
        ).astype(jnp.float32),
    )
    back_set = (
        lax.psum_scatter(
            grad_set[5].astype(jnp.bfloat16), "blk", scatter_dimension=1, tiled=True
        ).astype(jnp.float32),
        lax.psum_scatter(
            grad_set[8].astype(jnp.bfloat16), "blk", scatter_dimension=1, tiled=True
        ).astype(jnp.float32),
    )
    gain_pair = lax.psum((front_set[0], front_set[5]), "uly")
    return (
        gain_pair[0],
        front_set[1],
        front_set[2],
        front_set[3],
        front_set[4],
        back_set[0],
        gain_pair[1],
        front_set[6],
        back_set[1],
    )


def forward_pass(row_block, rate_row, lengths_row, weights):
    (
        gain_one,
        query_full,
        key_full,
        value_full,
        gate_full,
        output_full,
        gain_two,
        up_full,
        down_full,
    ) = weights
    head_count = rate_row.shape[0]
    inputs = row_block.astype(jnp.float32)
    norm_one, norm_one_back = jax.vjp(layer_norm, inputs, gain_one)
    wide_one = spread(norm_one.astype(jnp.bfloat16))
    length = wide_one.shape[0]
    query_rows = matmul(wide_one, query_full).astype(jnp.bfloat16)
    key_rows = matmul(wide_one, key_full).astype(jnp.bfloat16)
    value_rows = matmul(wide_one, value_full).astype(jnp.bfloat16)
    gate_rows = matmul(wide_one, gate_full)
    positions = lax.axis_index("blk") * length + jnp.arange(length, dtype=jnp.int32)
    seg_local = segment_ids(positions, lengths_row)
    seg_prev = segment_ids(positions[:1] - 1, lengths_row)[0]
    inner_width, entry, leave, through = retention_parts(rate_row, seg_local, seg_prev, length)
    head_queries = to_heads(query_rows, head_count).astype(jnp.float32)
    head_keys = to_heads(key_rows, head_count).astype(jnp.float32)
    value_heads = to_heads(value_rows, head_count).astype(jnp.float32)
    state_out, state_back = jax.vjp(partial(state_local, leave), head_keys, value_heads)
    start_set = (jnp.ones_like(through), jnp.zeros_like(state_out))
    state_in = prefix((through, state_out), "blk", chain, start_set)[1]
    retained, read_back = jax.vjp(
        partial(read_out, inner_width, entry), head_queries, head_keys, value_heads, state_in
    )
    mixed_exact, mix_back = jax.vjp(gate_mix, gate_rows, retained)
    mixed_rows = mixed_exact.astype(jnp.bfloat16)
    hidden = inputs + collect(matmul(mixed_rows, output_full))
    norm_two, norm_two_back = jax.vjp(layer_norm, hidden, gain_two)
    wide_two = spread(norm_two.astype(jnp.bfloat16))
    gelu_out, gelu_back = jax.vjp(gelu_tanh, matmul(wide_two, up_full))
    activated = gelu_out.astype(jnp.bfloat16)
    block_rows = (hidden + collect(matmul(activated, down_full))).astype(jnp.bfloat16)
    saved = (
        norm_one_back,
        wide_one,
        through,
        state_back,
        read_back,
        mix_back,
        mixed_rows,
        norm_two_back,
        wide_two,
        gelu_back,
        activated,
    )
    return (block_rows, saved)


def backward_pass(saved, cotangent, weights):
    (
        gain_one,
        query_full,
        key_full,
        value_full,
        gate_full,
        output_full,
        gain_two,
        up_full,
        down_full,
    ) = weights
    (
        norm_one_back,
        wide_one,
        through,
        state_back,
        read_back,
        mix_back,
        mixed_rows,
        norm_two_back,
        wide_two,
        gelu_back,
        activated,
    ) = saved
    out_wide = spread(cotangent)
    down_part = inner_rows(activated, out_wide)
    grad_activated = outer_cols(out_wide, down_full)
    grad_upward = gelu_back(grad_activated)[0].astype(jnp.bfloat16)
    up_part = inner_rows(wide_two, grad_upward)
    grad_norm_two = collect(outer_cols(grad_upward, up_full))
    hidden_part, gain_two_part = norm_two_back(grad_norm_two)
    grad_hidden = cotangent.astype(jnp.float32) + hidden_part
    attended_wide = spread(grad_hidden.astype(jnp.bfloat16))
    output_part = inner_rows(mixed_rows, attended_wide)
    grad_mixed = outer_cols(attended_wide, output_full)
    gate_exact, grad_retained = mix_back(grad_mixed)
    grad_gate = gate_exact.astype(jnp.bfloat16)
    query_exact, key_exact, value_exact, grad_state_in = read_back(grad_retained)
    start_set = (jnp.ones_like(through), jnp.zeros_like(grad_state_in))
    grad_state_out = carried_in((through, grad_state_in), "blk", chain, start_set)[1]
    key_extra, value_extra = state_back(grad_state_out)
    grad_queries = from_heads(query_exact).astype(jnp.bfloat16)
    grad_keys = from_heads(key_exact + key_extra).astype(jnp.bfloat16)
    grad_values = from_heads(value_exact + value_extra).astype(jnp.bfloat16)
    query_slice = inner_rows(wide_one, grad_queries)
    key_part = inner_rows(wide_one, grad_keys)
    value_part = inner_rows(wide_one, grad_values)
    gate_part = inner_rows(wide_one, grad_gate)
    partial_norm = outer_cols(grad_queries, query_full) + outer_cols(grad_keys, key_full)
    partial_norm = (
        partial_norm + outer_cols(grad_values, value_full) + outer_cols(grad_gate, gate_full)
    )
    grad_norm_one = collect(partial_norm)
    input_part, gain_one_part = norm_one_back(grad_norm_one)
    input_rows = grad_hidden + input_part
    grad_set = (
        gain_one_part,
        query_slice,
        key_part,
        value_part,
        gate_part,
        output_part,
        gain_two_part,
        up_part,
        down_part,
    )
    return (input_rows, grad_set)


def body(
    tokens,
    retain_gain,
    query_weight,
    key_weight,
    value_weight,
    gate_matrix,
    output_weight,
    feed_gain,
    up_weight,
    down_weight,
    decay_rate,
    lengths,
    out_grad,
):
    shards = (
        retain_gain,
        query_weight,
        key_weight,
        value_weight,
        gate_matrix,
        output_weight,
        feed_gain,
        up_weight,
        down_weight,
    )
    heads_here = decay_rate.shape[0] // lax.axis_size("uly")
    rate_row = lax.dynamic_slice_in_dim(decay_rate, lax.axis_index("uly") * heads_here, heads_here)
    outputs = []
    input_grads = []
    totals = None
    for micro_step in range(tokens.shape[0]):
        weights = fetch(shards)
        block_rows, saved = forward_pass(tokens[micro_step], rate_row, lengths[micro_step], weights)
        back_weights = fetch(shards)
        input_rows, grad_set = backward_pass(saved, out_grad[micro_step], back_weights)
        grad_set = reduce_grads(grad_set)
        totals = grad_set if totals is None else jax.tree.map(jnp.add, totals, grad_set)
        outputs.append(block_rows)
        input_grads.append(input_rows)
    return (
        jnp.stack(outputs),
        jnp.stack(input_grads),
        totals[0],
        totals[1],
        totals[2],
        totals[3],
        totals[4],
        totals[5],
        totals[6],
        totals[7],
        totals[8],
    )


def solution(mesh):
    placed = (
        P(None, ("blk", "uly"), None),
        P("blk"),
        P("blk", "uly"),
        P("blk", "uly"),
        P("blk", "uly"),
        P("blk", "uly"),
        P("uly", "blk"),
        P("blk"),
        P("blk", "uly"),
        P("uly", "blk"),
        P(),
        P(),
        P(None, ("blk", "uly"), None),
    )
    return jax.shard_map(
        body,
        mesh=mesh,
        in_specs=placed,
        out_specs=(
            P(None, ("blk", "uly"), None),
            P(None, ("blk", "uly"), None),
            P("blk"),
            P("blk", "uly"),
            P("blk", "uly"),
            P("blk", "uly"),
            P("blk", "uly"),
            P("uly", "blk"),
            P("blk"),
            P("blk", "uly"),
            P("uly", "blk"),
        ),
        check_vma=False,
    )
```

profile of v0, /device:TPU:0, one launch (start us, length us, event | category | flops | bytes accessed | tf_op | source)
XLA Modules:
  0.0 2296.7 jit_solution(9851383608554440304)
XLA Ops:
  34.3 35.6 %all-gather.50.cloned.1.call-done = bf16[512,2048]{1,0:T(8,128)(2,1)} async-done(((bf16[128,2048]{1,0:T(8,128)(2,1)}), bf16[512,2048]{1,0:T(8,128)(2,1)}) %all-gather.50.cloned.1.call-update) | async-done | bytes 2097168 | tf_op jit(solution)/shard_map/all_gather | solution.py:139
  102.2 34.9 %all-gather.40.cloned.1.call-done = bf16[2048,1024]{1,0:T(8,128)(2,1)} async-done(((bf16[256,1024]{1,0:T(8,128)(2,1)}), bf16[2048,1024]{1,0:T(8,128)(2,1)}) %all-gather.40.cloned.1.call-update) | async-done | bytes 4194320 | tf_op jit(solution)/shard_map/all_gather | solution.py:151
  147.1 37.9 %all-gather.32.cloned.1.call-done = bf16[512,2048]{1,0:T(8,128)(2,1)} async-done(((bf16[128,2048]{1,0:T(8,128)(2,1)}), bf16[512,2048]{1,0:T(8,128)(2,1)}) %all-gather.32.cloned.1.call-update) | async-done | bytes 2097168 | tf_op jit(solution)/shard_map/all_gather | solution.py:139
  223.2 47.1 %all-gather.60.cloned.1.call-done = f32[16,256,512]{2,1,0:T(8,128)} async-done(((f32[2,256,512]{2,1,0:T(8,128)}), f32[16,256,512]{2,1,0:T(8,128)}) %all-gather.60.cloned.1.call-update) | async-done | bytes 8388624 | tf_op jit(solution)/shard_map/all_gather | solution.py:14
  362.2 43.0 %all-gather.58.cloned.1.call-done = f32[16,256,512]{2,1,0:T(8,128)} async-done(((f32[2,256,512]{2,1,0:T(8,128)}), f32[16,256,512]{2,1,0:T(8,128)}) %all-gather.58.cloned.1.call-update) | async-done | bytes 8388624 | tf_op jit(solution)/shard_map/all_gather | solution.py:14
  445.9 38.2 %reduce-scatter.27.cloned.1.call-done = f32[128,2048]{1,0:T(8,128)} async-done(((f32[512,2048]{1,0:T(8,128)}), f32[128,2048]{1,0:T(8,128)}) %reduce-scatter.27.cloned.1.call-update) | async-done | bytes 1048592 | tf_op jit(solution)/shard_map/reduce_scatter | solution.py:143
  484.1 79.7 %reduce-scatter.23.cloned.1.call-done = f32[128,2048]{1,0:T(8,128)} async-done(((f32[512,2048]{1,0:T(8,128)}), f32[128,2048]{1,0:T(8,128)}) %reduce-scatter.23.cloned.1.call-update) | async-done | bytes 1048592 | tf_op jit(solution)/shard_map/reduce_scatter | solution.py:143
  602.8 48.1 %all-gather.44.cloned.1.call-done = bf16[512,2048]{1,0:T(8,128)(2,1)} async-done(((bf16[128,2048]{1,0:T(8,128)(2,1)}), bf16[512,2048]{1,0:T(8,128)(2,1)}) %all-gather.44.cloned.1.call-update) | async-done | bytes 2097168 | tf_op jit(solution)/shard_map/all_gather | solution.py:139
  657.4 39.7 %all-gather.62.cloned.1.call-done = bf16[1,512,2048]{2,1,0:T(8,128)(2,1)} async-done(((bf16[1,128,2048]{2,1,0:T(8,128)(2,1)}), bf16[1,512,2048]{2,1,0:T(8,128)(2,1)}) %all-gather.62.cloned.1.call-update) | async-done | bytes 2097168 | tf_op jit(solution)/shard_map/all_gather | solution.py:139
  697.0 37.9 %all-gather.48.cloned.1.call-done = bf16[1024,2048]{1,0:T(8,128)(2,1)} async-done(((bf16[1024,256]{1,0:T(8,128)(2,1)}), bf16[1024,2048]{1,0:T(8,128)(2,1)}) %all-gather.48.cloned.1.call-update) | async-done | bytes 4194320 | tf_op jit(solution)/shard_map/all_gather | solution.py:158
  755.4 68.0 %reduce-scatter.31.cloned.1.call-done = f32[128,2048]{1,0:T(8,128)} async-done(((f32[512,2048]{1,0:T(8,128)}), f32[128,2048]{1,0:T(8,128)}) %reduce-scatter.31.cloned.1.call-update) | async-done | bytes 1048592 | tf_op jit(solution)/shard_map/reduce_scatter | solution.py:143
  825.6 77.3 %reduce-scatter.25.cloned.1.call-done = f32[128,2048]{1,0:T(8,128)} async-done(((f32[512,2048]{1,0:T(8,128)}), f32[128,2048]{1,0:T(8,128)}) %reduce-scatter.25.cloned.1.call-update) | async-done | bytes 1048592 | tf_op jit(solution)/shard_map/reduce_scatter | solution.py:143
  907.2 45.6 %all-gather.52.cloned.1.call-done = bf16[512,2048]{1,0:T(8,128)(2,1)} async-done(((bf16[128,2048]{1,0:T(8,128)(2,1)}), bf16[512,2048]{1,0:T(8,128)(2,1)}) %all-gather.52.cloned.1.call-update) | async-done | bytes 2097168 | tf_op jit(solution)/shard_map/all_gather | solution.py:139
  959.3 39.8 %all-gather.66.cloned.1.call-done = bf16[1,512,2048]{2,1,0:T(8,128)(2,1)} async-done(((bf16[1,128,2048]{2,1,0:T(8,128)(2,1)}), bf16[1,512,2048]{2,1,0:T(8,128)(2,1)}) %all-gather.66.cloned.1.call-update) | async-done | bytes 2097168 | tf_op jit(solution)/shard_map/all_gather | solution.py:139
  1018.0 68.2 %reduce-scatter.35.cloned.1.call-done = f32[128,2048]{1,0:T(8,128)} async-done(((f32[512,2048]{1,0:T(8,128)}), f32[128,2048]{1,0:T(8,128)}) %reduce-scatter.35.cloned.1.call-update) | async-done | bytes 1048592 | tf_op jit(solution)/shard_map/reduce_scatter | solution.py:143
  1088.4 77.5 %reduce-scatter.29.cloned.1.call-done = f32[128,2048]{1,0:T(8,128)} async-done(((f32[512,2048]{1,0:T(8,128)}), f32[128,2048]{1,0:T(8,128)}) %reduce-scatter.29.cloned.1.call-update) | async-done | bytes 1048592 | tf_op jit(solution)/shard_map/reduce_scatter | solution.py:143
  1171.2 45.4 %all-gather.54.cloned.1.call-done = bf16[512,2048]{1,0:T(8,128)(2,1)} async-done(((bf16[128,2048]{1,0:T(8,128)(2,1)}), bf16[512,2048]{1,0:T(8,128)(2,1)}) %all-gather.54.cloned.1.call-update) | async-done | bytes 2097168 | tf_op jit(solution)/shard_map/all_gather | solution.py:139
  1228.4 34.5 %all-gather.56.cloned.1.call-done = bf16[512,2048]{1,0:T(8,128)(2,1)} async-done(((bf16[128,2048]{1,0:T(8,128)(2,1)}), bf16[512,2048]{1,0:T(8,128)(2,1)}) %all-gather.56.cloned.1.call-update) | async-done | bytes 2097168 | tf_op jit(solution)/shard_map/all_gather | solution.py:139
  1479.5 45.0 %reduce-scatter.59.cloned.1.call-done = bf16[256,1024]{1,0:T(8,128)(2,1)} async-done(((bf16[2048,1024]{1,0:T(8,128)(2,1)}), bf16[256,1024]{1,0:T(8,128)(2,1)}) %reduce-scatter.59.cloned.1.call-update) | async-done | bytes 524304 | tf_op jit(solution)/shard_map/reduce_scatter | solution.py:193
  1524.5 55.1 %reduce-scatter.61.cloned.1.call-done = bf16[256,1024]{1,0:T(8,128)(2,1)} async-done(((bf16[2048,1024]{1,0:T(8,128)(2,1)}), bf16[256,1024]{1,0:T(8,128)(2,1)}) %reduce-scatter.61.cloned.1.call-update) | async-done | bytes 524304 | tf_op jit(solution)/shard_map/reduce_scatter | solution.py:193
  1583.1 41.0 %reduce-scatter.39.cloned.1.call-done = bf16[256,512]{1,0:T(8,128)(2,1)} async-done(((bf16[2048,512]{1,0:T(8,128)(2,1)}), bf16[256,512]{1,0:T(8,128)(2,1)}) %reduce-scatter.39.cloned.1.call-update) | async-done | bytes 262160 | tf_op jit(solution)/shard_map/reduce_scatter | solution.py:178
  1624.0 44.9 %reduce-scatter.41.cloned.1.call-done = bf16[256,512]{1,0:T(8,128)(2,1)} async-done(((bf16[2048,512]{1,0:T(8,128)(2,1)}), bf16[256,512]{1,0:T(8,128)(2,1)}) %reduce-scatter.41.cloned.1.call-update) | async-done | bytes 262160 | tf_op jit(solution)/shard_map/reduce_scatter | solution.py:178
  1670.8 52.8 %reduce-scatter.57.cloned.1.call-done = bf16[1024,256]{1,0:T(8,128)(2,1)} async-done(((bf16[1024,2048]{1,0:T(8,128)(2,1)}), bf16[1024,256]{1,0:T(8,128)(2,1)}) %reduce-scatter.57.cloned.1.call-update) | async-done | bytes 524304 | tf_op jit(solution)/shard_map/reduce_scatter | solution.py:198
  1723.6 54.9 %reduce-scatter.55.cloned.1.call-done = bf16[1024,256]{1,0:T(8,128)(2,1)} async-done(((bf16[1024,2048]{1,0:T(8,128)(2,1)}), bf16[1024,256]{1,0:T(8,128)(2,1)}) %reduce-scatter.55.cloned.1.call-update) | async-done | bytes 524304 | tf_op jit(solution)/shard_map/reduce_scatter | solution.py:198
  1780.9 52.4 %reduce-scatter.51.cloned.1.call-done = bf16[256,1024]{1,0:T(8,128)(2,1)} async-done(((bf16[2048,1024]{1,0:T(8,128)(2,1)}), bf16[256,1024]{1,0:T(8,128)(2,1)}) %reduce-scatter.51.cloned.1.call-update) | async-done | bytes 524304 | tf_op jit(solution)/shard_map/reduce_scatter | solution.py:187
  1833.3 55.1 %reduce-scatter.53.cloned.1.call-done = bf16[256,1024]{1,0:T(8,128)(2,1)} async-done(((bf16[2048,1024]{1,0:T(8,128)(2,1)}), bf16[256,1024]{1,0:T(8,128)(2,1)}) %reduce-scatter.53.cloned.1.call-update) | async-done | bytes 524304 | tf_op jit(solution)/shard_map/reduce_scatter | solution.py:187
  1890.7 42.0 %reduce-scatter.43.cloned.1.call-done = bf16[256,512]{1,0:T(8,128)(2,1)} async-done(((bf16[2048,512]{1,0:T(8,128)(2,1)}), bf16[256,512]{1,0:T(8,128)(2,1)}) %reduce-scatter.43.cloned.1.call-update) | async-done | bytes 262160 | tf_op jit(solution)/shard_map/reduce_scatter | solution.py:181
  1932.7 44.7 %reduce-scatter.45.cloned.1.call-done = bf16[256,512]{1,0:T(8,128)(2,1)} async-done(((bf16[2048,512]{1,0:T(8,128)(2,1)}), bf16[256,512]{1,0:T(8,128)(2,1)}) %reduce-scatter.45.cloned.1.call-update) | async-done | bytes 262160 | tf_op jit(solution)/shard_map/reduce_scatter | solution.py:181
  1979.4 52.8 %reduce-scatter.47.cloned.1.call-done = bf16[256,1024]{1,0:T(8,128)(2,1)} async-done(((bf16[2048,1024]{1,0:T(8,128)(2,1)}), bf16[256,1024]{1,0:T(8,128)(2,1)}) %reduce-scatter.47.cloned.1.call-update) | async-done | bytes 524304 | tf_op jit(solution)/shard_map/reduce_scatter | solution.py:184
  2032.2 54.9 %reduce-scatter.49.cloned.1.call-done = bf16[256,1024]{1,0:T(8,128)(2,1)} async-done(((bf16[2048,1024]{1,0:T(8,128)(2,1)}), bf16[256,1024]{1,0:T(8,128)(2,1)}) %reduce-scatter.49.cloned.1.call-update) | async-done | bytes 524304 | tf_op jit(solution)/shard_map/reduce_scatter | solution.py:184
  2089.5 76.7 %reduce-scatter.33.cloned.1.call-done = f32[128,2048]{1,0:T(8,128)} async-done(((f32[512,2048]{1,0:T(8,128)}), f32[128,2048]{1,0:T(8,128)}) %reduce-scatter.33.cloned.1.call-update) | async-done | bytes 1048592 | tf_op jit(solution)/shard_map/reduce_scatter | solution.py:143
  2166.2 79.7 %reduce-scatter.37.cloned.1.call-done = f32[128,2048]{1,0:T(8,128)} async-done(((f32[512,2048]{1,0:T(8,128)}), f32[128,2048]{1,0:T(8,128)}) %reduce-scatter.37.cloned.1.call-update) | async-done | bytes 1048592 | tf_op jit(solution)/shard_map/reduce_scatter | solution.py:143
  (557 shorter events, 644.5 us)
Async XLA Ops:
  25.0 160.1 %all-gather.32.cloned.1.call-start = ((), (), s32[]{:S(2)}) async-start(), calls=%async_computation.22 | async-start | bytes 2621440 | tf_op jit(solution)/shard_map/all_gather | solution.py:139
  25.6 190.7 %all-gather.36.cloned.1.call-start = ((), (), s32[]{:S(2)}) async-start(), calls=%async_computation.24 | async-start | bytes 2359296 | tf_op jit(solution)/shard_map/all_gather | solution.py:149
  26.1 244.2 %all-gather.60.cloned.1.call-start = ((), (), s32[]{:S(2)}) async-start(), calls=%async_computation.58 | async-start | bytes 9437184 | tf_op jit(solution)/shard_map/all_gather | solution.py:14
  145.6 163.4 %all-gather.34.cloned.1.call-start = ((), (), s32[]{:S(2)}) async-start(), calls=%async_computation.23 | async-start | bytes 4718592 | tf_op jit(solution)/shard_map/all_gather | solution.py:152
  146.3 202.0 %all-gather.42.cloned.1.call-start = ((), (), s32[]{:S(2)}) async-start(), calls=%async_computation.27 | async-start | bytes 4718592 | tf_op jit(solution)/shard_map/all_gather | solution.py:157
  147.1 258.1 %all-gather.58.cloned.1.call-start = ((), (), s32[]{:S(2)}) async-start(), calls=%async_computation.57 | async-start | bytes 9437184 | tf_op jit(solution)/shard_map/all_gather | solution.py:14
  197.5 286.6 %reduce-scatter.27.cloned.1.call-start = ((), (), s32[]{:S(2)}) async-start(), calls=%async_computation.34 | async-start | bytes 5242880 | tf_op jit(solution)/shard_map/reduce_scatter | solution.py:143
  354.9 208.9 %reduce-scatter.23.cloned.1.call-start = ((), (), s32[]{:S(2)}) async-start(), calls=%async_computation.28 | async-start | bytes 5242880 | tf_op jit(solution)/shard_map/reduce_scatter | solution.py:143
  426.5 176.3 %all-gather.46.cloned.1.call-start = ((), (), s32[]{:S(2)}) async-start(), calls=%async_computation.30 | async-start | bytes 4718592 | tf_op jit(solution)/shard_map/all_gather | solution.py:154
  427.1 223.8 %all-gather.44.cloned.1.call-start = ((), (), s32[]{:S(2)}) async-start(), calls=%async_computation.29 | async-start | bytes 2621440 | tf_op jit(solution)/shard_map/all_gather | solution.py:139
  569.0 165.9 %all-gather.48.cloned.1.call-start = ((), (), s32[]{:S(2)}) async-start(), calls=%async_computation.31 | async-start | bytes 4718592 | tf_op jit(solution)/shard_map/all_gather | solution.py:158
  569.6 253.8 %reduce-scatter.31.cloned.1.call-start = ((), (), s32[]{:S(2)}) async-start(), calls=%async_computation.37 | async-start | bytes 5242880 | tf_op jit(solution)/shard_map/reduce_scatter | solution.py:143
  754.0 198.8 %all-gather.52.cloned.1.call-start = ((), (), s32[]{:S(2)}) async-start(), calls=%async_computation.35 | async-start | bytes 2621440 | tf_op jit(solution)/shard_map/all_gather | solution.py:139
  907.0 179.2 %reduce-scatter.35.cloned.1.call-start = ((), (), s32[]{:S(2)}) async-start(), calls=%async_computation.40 | async-start | bytes 5242880 | tf_op jit(solution)/shard_map/reduce_scatter | solution.py:143
  1017.9 198.7 %all-gather.54.cloned.1.call-start = ((), (), s32[]{:S(2)}) async-start(), calls=%async_computation.38 | async-start | bytes 2621440 | tf_op jit(solution)/shard_map/all_gather | solution.py:139
  1170.8 216.8 %all-gather.64.cloned.1.call-start = ((), (), s32[]{:S(2)}) async-start(), calls=%async_computation.60 | async-start | bytes 4718592 | tf_op jit(solution)/shard_map/all_gather | solution.py:30
  1289.3 187.8 %reduce-scatter.63.cloned.1.call-start = ((), (), s32[]{:S(2)}) async-start(), calls=%async_computation.55 | async-start | bytes 4718592 | tf_op jit(solution)/shard_map/reduce_scatter | solution.py:201
  1296.5 180.7 %reduce-scatter.65.cloned.1.call-start = ((), (), s32[]{:S(2)}) async-start(), calls=%async_computation.56 | async-start | bytes 4718592 | tf_op jit(solution)/shard_map/reduce_scatter | solution.py:201
  1303.4 221.2 %reduce-scatter.59.cloned.1.call-start = ((), (), s32[]{:S(2)}) async-start(), calls=%async_computation.53 | async-start | bytes 4718592 | tf_op jit(solution)/shard_map/reduce_scatter | solution.py:193
  1309.7 270.0 %reduce-scatter.61.cloned.1.call-start = ((), (), s32[]{:S(2)}) async-start(), calls=%async_computation.54 | async-start | bytes 4718592 | tf_op jit(solution)/shard_map/reduce_scatter | solution.py:193
  1316.1 307.9 %reduce-scatter.39.cloned.1.call-start = ((), (), s32[]{:S(2)}) async-start(), calls=%async_computation.43 | async-start | bytes 2359296 | tf_op jit(solution)/shard_map/reduce_scatter | solution.py:178
  1331.2 337.7 %reduce-scatter.41.cloned.1.call-start = ((), (), s32[]{:S(2)}) async-start(), calls=%async_computation.44 | async-start | bytes 2359296 | tf_op jit(solution)/shard_map/reduce_scatter | solution.py:178
  1345.6 378.0 %reduce-scatter.57.cloned.1.call-start = ((), (), s32[]{:S(2)}) async-start(), calls=%async_computation.52 | async-start | bytes 4718592 | tf_op jit(solution)/shard_map/reduce_scatter | solution.py:198
  1351.6 427.0 %reduce-scatter.55.cloned.1.call-start = ((), (), s32[]{:S(2)}) async-start(), calls=%async_computation.51 | async-start | bytes 4718592 | tf_op jit(solution)/shard_map/reduce_scatter | solution.py:198
  1357.9 475.4 %reduce-scatter.51.cloned.1.call-start = ((), (), s32[]{:S(2)}) async-start(), calls=%async_computation.49 | async-start | bytes 4718592 | tf_op jit(solution)/shard_map/reduce_scatter | solution.py:187
  1364.1 524.3 %reduce-scatter.53.cloned.1.call-start = ((), (), s32[]{:S(2)}) async-start(), calls=%async_computation.50 | async-start | bytes 4718592 | tf_op jit(solution)/shard_map/reduce_scatter | solution.py:187
  1370.3 562.5 %reduce-scatter.43.cloned.1.call-start = ((), (), s32[]{:S(2)}) async-start(), calls=%async_computation.45 | async-start | bytes 2359296 | tf_op jit(solution)/shard_map/reduce_scatter | solution.py:181
  1402.3 575.2 %reduce-scatter.45.cloned.1.call-start = ((), (), s32[]{:S(2)}) async-start(), calls=%async_computation.46 | async-start | bytes 2359296 | tf_op jit(solution)/shard_map/reduce_scatter | solution.py:181
  1423.1 609.1 %reduce-scatter.47.cloned.1.call-start = ((), (), s32[]{:S(2)}) async-start(), calls=%async_computation.47 | async-start | bytes 4718592 | tf_op jit(solution)/shard_map/reduce_scatter | solution.py:184
  1436.9 650.2 %reduce-scatter.49.cloned.1.call-start = ((), (), s32[]{:S(2)}) async-start(), calls=%async_computation.48 | async-start | bytes 4718592 | tf_op jit(solution)/shard_map/reduce_scatter | solution.py:184
  1451.4 714.8 %reduce-scatter.33.cloned.1.call-start = ((), (), s32[]{:S(2)}) async-start(), calls=%async_computation.39 | async-start | bytes 5242880 | tf_op jit(solution)/shard_map/reduce_scatter | solution.py:143
  1463.9 782.0 %reduce-scatter.37.cloned.1.call-start = ((), (), s32[]{:S(2)}) async-start(), calls=%async_computation.42 | async-start | bytes 5242880 | tf_op jit(solution)/shard_map/reduce_scatter | solution.py:143
  (138 other events, 5205.7 us)
Sparse Core Ops, SparseCore 0:
  23.6 46.2 all-gather.49
  139.1 45.9 all-gather.31
  215.9 54.3 all-gather.59
  350.8 54.3 all-gather.57
  407.3 76.7 reduce-scatter.26
  486.5 77.2 reduce-scatter.22
  605.0 45.9 all-gather.43
  652.3 44.6 all-gather.61
  746.6 76.7 reduce-scatter.30
  825.7 77.2 reduce-scatter.24
  906.3 46.4 all-gather.51
  954.4 44.6 all-gather.65
  1010.6 75.4 reduce-scatter.34
  1088.6 77.2 reduce-scatter.28
  1170.2 46.4 all-gather.53
  1218.2 44.6 all-gather.55
  1363.5 51.3 reduce-scatter.62
  1418.5 51.3 reduce-scatter.64
  1473.2 51.3 reduce-scatter.58
  1528.3 51.3 reduce-scatter.60
  1582.8 41.1 reduce-scatter.38
  1627.7 41.2 reduce-scatter.40
  1672.3 51.3 reduce-scatter.56
  1727.2 51.3 reduce-scatter.54
  1781.9 51.3 reduce-scatter.50
  1837.0 51.3 reduce-scatter.52
  1891.5 41.1 reduce-scatter.42
  1936.2 41.2 reduce-scatter.44
  1980.8 51.3 reduce-scatter.46
  2035.8 51.3 reduce-scatter.48
  2089.4 76.7 reduce-scatter.32
  2168.6 77.2 reduce-scatter.36
  (9 shorter events, 309.2 us)
where the time goes:
time: 2310 us; the launch traced here: 2300 us
  waiting for transfers between devices  1780 us (77%)
  matrix products  272 us (12%)
  blocking collectives  92.9 us (4%)
  other arithmetic  79.9 us (3%)
  local copies, waits for them, and re-layouts  46.2 us (2%)
    reduce_scatter x8, waiting for transfers between devices, collect(): lax.psum_scatter(partial_rows, 'uly', scatter_dimension=0, tiled=True)  565 us
    all_gather x8, waiting for transfers between devices, spread(): return lax.all_gather(row_block, 'uly', axis=0, tiled=True)  327 us
    reduce_scatter x2, waiting for transfers between devices, reduce_grads(): lax.psum_scatter(grad_set[3].astype(jnp.bfloat16), 'blk', scatter_dimensi...  108 us
    reduce_scatter x2, waiting for transfers between devices, reduce_grads(): lax.psum_scatter(grad_set[5].astype(jnp.bfloat16), 'blk', scatter_dimensi...  108 us
    reduce_scatter x2, waiting for transfers between devices, reduce_grads(): lax.psum_scatter(grad_set[4].astype(jnp.bfloat16), 'blk', scatter_dimensi...  108 us
    reduce_scatter x2, waiting for transfers between devices, reduce_grads(): lax.psum_scatter(grad_set[7].astype(jnp.bfloat16), 'blk', scatter_dimensi...  100 us
    all_gather x2, waiting for transfers between devices, prefix(): gathered = jax.tree.map(lambda a: lax.all_gather(a, axis), part)  90.1 us
    reduce_scatter x2, waiting for transfers between devices, reduce_grads(): lax.psum_scatter(grad_set[2].astype(jnp.bfloat16), 'blk', scatter_dimensi...  86.8 us
  transfers between devices with their start and end apart: 41, of which 36 were waited for; matrix products, arithmetic and copies ran while one was open for 13% of the time, Pallas kernels for 0%

commit v1 on v0

v1 whole, which is shorter than its diff:
```python
import jax
import jax.numpy as jnp
from jax import lax
from jax.sharding import PartitionSpec as P

EPSILON = 1e-05
BF = jnp.bfloat16
F32 = jnp.float32


def dot_nn(left, right, kind=F32):
    return jnp.dot(left, right, preferred_element_type=F32).astype(kind)


def dot_tn(left, right, kind=F32):
    return lax.dot_general(
        left, right, (((0,), (0,)), ((), ())), preferred_element_type=F32
    ).astype(kind)


def dot_nt(left, right, kind=F32):
    return lax.dot_general(
        left, right, (((1,), (1,)), ((), ())), preferred_element_type=F32
    ).astype(kind)


def swap(array, mask):
    count = lax.axis_size("blk")
    return lax.ppermute(array, "blk", [(b, b ^ mask) for b in range(count)])


def shift(array, step):
    count = lax.axis_size("uly")
    return lax.ppermute(array, "uly", [(z, (z + step) % count) for z in range(count)])


def is_cube():
    return lax.axis_size("blk") == 8


def masks():
    return [2 * k + j for j in range(2) for k in range(4)]


def arrange(array):
    if not is_cube():
        return array
    me = lax.axis_index("blk")
    width = array.shape[-1] // 8
    parts = [
        lax.dynamic_slice_in_dim(array, (me ^ m) * width, width, array.ndim - 1) for m in masks()
    ]
    return jnp.concatenate(parts, axis=-1)


def restore(array):
    if not is_cube():
        return array
    me = lax.axis_index("blk")
    width = array.shape[-1] // 8
    parts = []
    for b in range(8):
        m = me ^ b
        place = (m & 1) * 4 + (m >> 1)
        parts.append(lax.dynamic_slice_in_dim(array, place * width, width, array.ndim - 1))
    return jnp.concatenate(parts, axis=-1)


def mirror(array):
    if not is_cube():
        return array
    half = array.shape[-1] // 2
    return jnp.concatenate([array[..., half:], array[..., :half]], axis=-1)


def plane_gather(first, second):
    first_x = swap(first, 2)
    second_y = swap(second, 4)
    first_y, first_xy = swap(first, 4), swap(first_x, 4)
    second_x, second_xy = swap(second, 2), swap(second_y, 2)
    return [first, first_x, first_y, first_xy], [second, second_x, second_y, second_xy]


def block_gather(first, second, dim):
    if not is_cube():
        return (
            lax.all_gather(first, "blk", axis=dim, tiled=True),
            lax.all_gather(second, "blk", axis=dim, tiled=True),
        )
    out = []
    for pieces in plane_gather(first, second):
        out.append(jnp.concatenate(pieces + [swap(p, 1) for p in pieces], axis=dim))
    return out


def both(own, came):
    return (own.astype(F32) + came.astype(F32)).astype(BF)


def plane_reduce(first, second):
    first = [both(first[k], swap(first[k + 2], 4)) for k in range(2)]
    second = [both(second[k], swap(second[k + 1], 2)) for k in (0, 2)]
    return both(first[0], swap(first[1], 2)), both(second[0], swap(second[1], 4))


def block_reduce(first, second, dim):
    if not is_cube():
        return (
            lax.psum_scatter(first.astype(BF), "blk", scatter_dimension=dim, tiled=True),
            lax.psum_scatter(second.astype(BF), "blk", scatter_dimension=dim, tiled=True),
        )
    sums = []
    for array in (first, second):
        parts = jnp.split(array.astype(BF), 8, axis=dim)
        sums.append([both(parts[k], swap(parts[4 + k], 1)) for k in range(4)])
    return plane_reduce(*sums)


def cube_all(array):
    if not is_cube():
        return lax.all_gather(array, "blk")
    array = array[None]
    for mask in (2, 4, 1):
        array = jnp.concatenate([array, swap(array, mask)], axis=0)
    return array


def cube_sum(array):
    if not is_cube():
        return lax.psum_scatter(array, "blk", scatter_dimension=array.ndim - 1, tiled=True)
    for mask in (1, 4, 2):
        half = array.shape[-1] // 2
        array = array[..., :half] + swap(array[..., half:], mask)
    return array


def spread(rows):
    count = lax.axis_size("uly")
    place = lax.axis_index("uly")
    came = [rows] + [shift(rows, s) for s in range(1, count)]
    window = came[:0:-1] + came[:1] + came[:0:-1]
    length = rows.shape[0]
    return lax.dynamic_slice_in_dim(
        jnp.concatenate(window, axis=0), (count - 1 - place) * length, count * length, 0
    )


def collect(partial):
    count = lax.axis_size("uly")
    place = lax.axis_index("uly")
    length = partial.shape[0] // count

    def rows_of(step):
        return lax.dynamic_slice_in_dim(partial, ((place + step) % count) * length, length, 0)

    total = rows_of(0)
    for s in range(1, count):
        total = total + shift(rows_of(s).astype(BF), s).astype(F32)
    return total


def normed(values):
    center = values - jnp.mean(values, axis=-1, keepdims=True)
    scale = lax.rsqrt(jnp.mean(center * center, axis=-1, keepdims=True) + EPSILON)
    return center * scale, scale


def norm_back(grad, hat, scale):
    return scale * (
        grad
        - jnp.mean(grad, axis=-1, keepdims=True)
        - hat * jnp.mean(grad * hat, axis=-1, keepdims=True)
    )


GELU_A = 0.7978845608028654
GELU_B = 0.044715


def gelu_pair(u):
    square = u * u
    tanh = jnp.tanh(GELU_A * u * (1.0 + GELU_B * square))
    slope = 0.5 * (1.0 + tanh) + 0.5 * u * (1.0 - tanh * tanh) * GELU_A * (
        1.0 + 3.0 * GELU_B * square
    )
    return 0.5 * u * (1.0 + tanh), slope


def segment_ids(positions, lengths_row):
    count = lengths_row.shape[0]
    before = jnp.arange(count)[None, :] < jnp.arange(count)[:, None]
    bounds = jnp.sum(jnp.where(before, lengths_row[None, :], 0), axis=1)
    return jnp.sum((bounds[None, :] <= positions[:, None]).astype(jnp.int32), axis=1)


def decay_parts(rates, lengths_row, length):
    me = lax.axis_index("blk")
    count = lax.axis_size("blk")
    places = jnp.arange(length, dtype=jnp.int32)
    seg = segment_ids(me * length + places, lengths_row)
    ends = segment_ids((jnp.arange(count, dtype=jnp.int32) + 1) * length - 1, lengths_row)
    seg_prev = segment_ids(jnp.reshape(me * length - 1, (1,)), lengths_row)[0]
    offset = places[:, None] - places[None, :]
    causal = (offset >= 0) & (seg[:, None] == seg[None, :])
    far = jnp.maximum(offset, 0).astype(F32)
    inner = jnp.where(causal[None], jnp.exp(-rates[:, None, None] * far[None]), 0.0)
    at = places.astype(F32)
    entry = jnp.where(seg == seg_prev, jnp.exp(-rates[:, None] * (at + 1.0)), 0.0)
    leave = jnp.where(seg == seg[length - 1], jnp.exp(-rates[:, None] * (length - 1.0 - at)), 0.0)
    if is_cube():
        source = me ^ jnp.asarray(masks(), jnp.int32)
    else:
        source = jnp.arange(count, dtype=jnp.int32)
    end_of = ends[source]
    end_before = jnp.where(source > 0, ends[jnp.maximum(source - 1, 0)], 0)
    past = jnp.maximum(me - 1 - source, 0).astype(F32)
    ahead = jnp.maximum(source - 1 - me, 0).astype(F32)
    from_past = jnp.where(
        (source < me) & (end_of == seg_prev), jnp.exp(-rates[:, None] * (length * past)), 0.0
    )
    from_ahead = jnp.where(
        (source > me) & (end_before == ends[me]), jnp.exp(-rates[:, None] * (length * ahead)), 0.0
    )
    return inner, entry[:, :, None], leave[:, :, None], from_past, from_ahead


def state_sum(weights, states):
    return jnp.einsum("hb,bhde->hde", weights, states.astype(F32))


def retention_state(heads, leave):
    return jnp.stack(
        [
            dot_tn((k.astype(F32) * leave[h]).astype(BF), v, BF)
            for h, (q, k, v) in enumerate(heads)
        ]
    )


def retention(heads, parts, state):
    inner, entry = parts[0], parts[1]
    out = []
    for h, (q, k, v) in enumerate(heads):
        scores = (dot_nt(q, k) * inner[h]).astype(BF)
        out.append(dot_nn(scores, v) + entry[h] * dot_nn(q, state[h].astype(BF)))
    return out


def mix(gate, retained):
    out = []
    for h, r in enumerate(retained):
        g = gate[:, h * r.shape[1] : (h + 1) * r.shape[1]]
        out.append((g * jax.nn.sigmoid(g) * normed(r)[0]).astype(BF))
    return jnp.concatenate(out, axis=1)


def mix_back(gate, retained, grad_mixed):
    grad_gate, grad_retained = [], []
    for h, r in enumerate(retained):
        cols = slice(h * r.shape[1], (h + 1) * r.shape[1])
        g, gm = gate[:, cols], grad_mixed[:, cols]
        sigma = jax.nn.sigmoid(g)
        hat, scale = normed(r)
        grad_gate.append((gm * hat * (sigma + g * sigma * (1.0 - sigma))).astype(BF))
        grad_retained.append(norm_back(gm * g * sigma, hat, scale).astype(BF))
    return jnp.concatenate(grad_gate, axis=1), grad_retained


def retention_back(heads, parts, state, grad_retained, grad_state):
    inner, entry, leave = parts[0], parts[1], parts[2]
    grads = []
    for h, (q, k, v) in enumerate(heads):
        gr = grad_retained[h]
        scores = (dot_nt(q, k) * inner[h]).astype(BF)
        pulls = (dot_nt(gr, v) * inner[h]).astype(BF)
        gs, st = grad_state[h].astype(BF), state[h].astype(BF)
        gq = dot_nn(pulls, k) + entry[h] * dot_nt(gr, st)
        gk = dot_tn(pulls, q) + leave[h] * dot_nt(v, gs)
        gv = dot_tn(scores, gr) + leave[h] * dot_nn(k, gs)
        grads.append((gq.astype(BF), gk.astype(BF), gv.astype(BF)))
    return grads


def core_cut(array, dim):
    core = lax.axis_index("blk") % 2
    half = array.shape[dim] // 2
    own = lax.dynamic_slice_in_dim(array, core * half, half, dim)
    other = lax.dynamic_slice_in_dim(array, (1 - core) * half, half, dim)
    return own, other


def core_order(own, other, dim):
    if is_cube():
        return jnp.concatenate([own, other], axis=dim)
    return core_join(own, other, dim)


def core_join(own, other, dim):
    first = lax.axis_index("blk") % 2 == 0
    return jnp.concatenate([jnp.where(first, own, other), jnp.where(first, other, own)], axis=dim)


def core_groups():
    count = lax.axis_size("blk")
    return [list(range(0, count, 2)), list(range(1, count, 2))]


def feed_weights(up_shard, down_shard):
    own, other = core_cut(up_shard, 1)
    up = core_order(own, swap(other, 1), 0)
    own, other = core_cut(down_shard, 0)
    down = core_order(own, swap(other, 1), 1)
    ups, downs = [], []
    for s in range(lax.axis_size("uly")):
        up_s = up if s == 0 else shift(up, s)
        down_s = down if s == 0 else shift(down, s)
        if is_cube():
            up_k, down_k = plane_gather(up_s, down_s)
            half = up.shape[0] // 2
            ups.append(
                jnp.concatenate([u[:half] for u in up_k] + [u[half:] for u in up_k], axis=0)
            )
            downs.append(
                jnp.concatenate([d[:, :half] for d in down_k] + [d[:, half:] for d in down_k], axis=1)
            )
        else:
            groups = core_groups()
            ups.append(lax.all_gather(up_s, "blk", axis=0, tiled=True, axis_index_groups=groups))
            downs.append(lax.all_gather(down_s, "blk", axis=1, tiled=True, axis_index_groups=groups))
    return jnp.concatenate(ups, axis=1), jnp.concatenate(downs, axis=0)


def feed_reduce(up_grad, down_grad):
    count = lax.axis_size("uly")
    depth = up_grad.shape[0]
    wide = up_grad.shape[1] // count
    up_sum, down_sum = None, None
    for s in range(count):
        up_s = up_grad[:, s * wide : (s + 1) * wide]
        down_s = down_grad[s * wide : (s + 1) * wide]
        if is_cube():
            c = depth // 8
            up_k = [
                jnp.concatenate(
                    [up_s[k * c : (k + 1) * c], up_s[(4 + k) * c : (5 + k) * c]], axis=0
                )
                for k in range(4)
            ]
            down_k = [
                jnp.concatenate(
                    [down_s[:, k * c : (k + 1) * c], down_s[:, (4 + k) * c : (5 + k) * c]], axis=1
                )
                for k in range(4)
            ]
            up_s, down_s = plane_reduce(up_k, down_k)
        else:
            groups = core_groups()
            up_s = lax.psum_scatter(
                up_s, "blk", scatter_dimension=0, tiled=True, axis_index_groups=groups
            )
            down_s = lax.psum_scatter(
                down_s, "blk", scatter_dimension=1, tiled=True, axis_index_groups=groups
            )
        if s:
            up_s, down_s = shift(up_s, -s), shift(down_s, -s)
        up_s, down_s = up_s.astype(F32), down_s.astype(F32)
        up_sum = up_s if up_sum is None else up_sum + up_s
        down_sum = down_s if down_sum is None else down_sum + down_s
    half = up_sum.shape[0] // 2
    core = lax.axis_index("blk") % 2
    first = 0 if is_cube() else core * half
    second = half if is_cube() else (1 - core) * half
    up_own = lax.dynamic_slice_in_dim(up_sum, first, half, 0)
    up_other = lax.dynamic_slice_in_dim(up_sum, second, half, 0)
    down_own = lax.dynamic_slice_in_dim(down_sum, first, half, 1)
    down_other = lax.dynamic_slice_in_dim(down_sum, second, half, 1)
    return (
        core_join(up_own, swap(up_other.astype(BF), 1).astype(F32), 1),
        core_join(down_own, swap(down_other.astype(BF), 1).astype(F32), 0),
    )


def feed(norm_two, out_rows, up, down):
    upward = dot_nn(norm_two, up)
    act, slope = gelu_pair(upward)
    act = act.astype(BF)
    grad_act = dot_nt(out_rows, down)
    grad_up = (grad_act * slope).astype(BF)
    return (
        dot_nn(act, down),
        dot_nt(grad_up, up),
        dot_tn(norm_two, grad_up, BF),
        dot_tn(act, out_rows, BF),
    )


def body(
    tokens,
    retain_gain,
    query_weight,
    key_weight,
    value_weight,
    gate_matrix,
    output_weight,
    feed_gain,
    up_weight,
    down_weight,
    decay_rate,
    lengths,
    out_grad,
):
    micro, rows, width = tokens.shape
    heads_here = decay_rate.shape[0] // lax.axis_size("uly")
    rates = lax.dynamic_slice_in_dim(decay_rate, lax.axis_index("uly") * heads_here, heads_here)
    hd = query_weight.shape[1] // heads_here
    vd = value_weight.shape[1] // heads_here
    cut_v = value_weight.shape[1] // 2
    cut_o = output_weight.shape[0] // 2

    tokens = arrange(tokens)
    wide_tokens = [spread(tokens[m]) for m in range(micro)]
    gains = cube_all(jnp.stack([retain_gain, feed_gain]))
    gain_one = gains[:, 0].reshape(-1).astype(F32)
    gain_two = gains[:, 1].reshape(-1).astype(F32)

    first = jnp.concatenate([query_weight, key_weight, value_weight[:, :cut_v]], axis=1)
    second = jnp.concatenate([value_weight[:, cut_v:], gate_matrix], axis=1)
    w_first, w_second = block_gather(first, second, 0)
    w_out = jnp.concatenate(
        block_gather(output_weight[:cut_o], output_weight[cut_o:], 1), axis=0
    )
    up, down = feed_weights(up_weight, down_weight)

    outs = arrange(out_grad)
    outs_other = swap(mirror(outs), 1)

    length = wide_tokens[0].shape[0]
    qk = query_weight.shape[1]

    wide_hat, wide_one, sets, gates, parts, states = [], [], [], [], [], []
    for m in range(micro):
        hat, _ = normed(wide_tokens[m].astype(F32))
        one = (hat * gain_one).astype(BF)
        a = dot_nn(one, w_first, BF)
        v_high = dot_nn(one, w_second[:, :cut_v], BF)
        gate = dot_nn(one, w_second[:, cut_v:])
        values = jnp.concatenate([a[:, 2 * qk :], v_high], axis=1)
        heads = [
            (
                a[:, h * hd : (h + 1) * hd],
                a[:, qk + h * hd : qk + (h + 1) * hd],
                values[:, h * vd : (h + 1) * vd],
            )
            for h in range(heads_here)
        ]
        part = decay_parts(rates, lengths[m], length)
        states.append(retention_state(heads, part[2]))
        wide_one.append(one)
        sets.append(heads)
        gates.append(gate)
        parts.append(part)

    def exchange(pieces):
        if not is_cube():
            return [lax.all_gather(p, "blk") for p in pieces]
        half = len(pieces) // 2
        a, b = plane_gather(jnp.stack(pieces[:half]), jnp.stack(pieces[half:]))
        got = []
        for four in (a, b):
            full = jnp.stack(four + [swap(p, 1) for p in four])
            got += [full[:, i] for i in range(full.shape[1])]
        return got

    all_states = exchange(states)
    state_in, retained, mixed, hidden, hats, scales, norm_two = [], [], [], [], [], [], []
    for m in range(micro):
        state = state_sum(parts[m][3], all_states[m])
        kept = retention(sets[m], parts[m], state)
        mx = mix(gates[m], kept)
        hid = tokens[m].astype(F32) + collect(dot_nn(mx, w_out))
        hat, scale = normed(hid)
        state_in.append(state)
        retained.append(kept)
        mixed.append(mx)
        hidden.append(hid)
        hats.append(hat)
        scales.append(scale)
        norm_two.append((hat * gain_two).astype(BF))

    two = jnp.concatenate(norm_two, axis=0)
    two_both = jnp.concatenate([two, swap(mirror(two), 1)], axis=0)
    flat = outs.reshape(micro * rows, width)
    out_both = jnp.concatenate([flat, outs_other.reshape(micro * rows, width)], axis=0)
    down_rows, grad_two, up_part, down_part = feed(two_both, out_both, up, down)
    own = micro * rows
    back_sum = swap(mirror(grad_two[own:].astype(BF)), 1)
    down_sum = swap(mirror(down_rows[own:].astype(BF)), 1)
    grad_two = grad_two[:own] + back_sum.astype(F32)
    down_rows = down_rows[:own] + down_sum.astype(F32)
    up_grad, down_grad = feed_reduce(up_part, down_part)

    block_out = restore(
        (jnp.stack(hidden) + down_rows.reshape(micro, rows, width)).astype(BF)
    )

    grad_hidden, wide_att = [], []
    gain_two_part = jnp.zeros((width,), F32)
    for m in range(micro):
        g2 = grad_two[m * rows : (m + 1) * rows]
        gain_two_part = gain_two_part + jnp.sum(g2 * hats[m], axis=0)
        gh = outs[m].astype(F32) + norm_back(g2 * gain_two, hats[m], scales[m])
        grad_hidden.append(gh)
        wide_att.append(spread(gh.astype(BF)))

    grad_gates, grad_rets, grad_states = [], [], []
    for m in range(micro):
        grad_mixed = dot_nt(wide_att[m], w_out)
        gg, gr = mix_back(gates[m], retained[m], grad_mixed)
        grad_gates.append(gg)
        grad_rets.append(gr)
        grad_states.append(
            jnp.stack(
                [
                    dot_tn((q.astype(F32) * parts[m][1][h]).astype(BF), gr[h], BF)
                    for h, (q, k, v) in enumerate(sets[m])
                ]
            )
        )
    all_back = exchange(grad_states)
    out_part = dot_tn(
        jnp.concatenate(mixed, axis=0), jnp.concatenate(wide_att, axis=0), BF
    )

    first_grads, second_grads, input_grads = [], [], []
    gain_one_part = jnp.zeros((width,), F32)
    for m in range(micro):
        back = state_sum(parts[m][4], all_back[m])
        grads = retention_back(sets[m], parts[m], state_in[m], grad_rets[m], back)
        gq = jnp.concatenate([g[0] for g in grads], axis=1)
        gk = jnp.concatenate([g[1] for g in grads], axis=1)
        gv = jnp.concatenate([g[2] for g in grads], axis=1)
        ga = jnp.concatenate([gq, gk, gv[:, :cut_v]], axis=1)
        gb = jnp.concatenate([gv[:, cut_v:], grad_gates[m]], axis=1)
        first_grads.append(ga)
        second_grads.append(gb)
        partial = dot_nt(ga, w_first) + dot_nt(gb, w_second)
        wide_hat, _ = normed(wide_tokens[m].astype(F32))
        gain_one_part = gain_one_part + jnp.sum(partial * wide_hat, axis=0)
        grad_one = collect(partial)
        hat, scale = normed(tokens[m].astype(F32))
        input_grads.append(grad_hidden[m] + norm_back(grad_one * gain_one, hat, scale))

    one_all = jnp.concatenate(wide_one, axis=0)
    first_part = dot_tn(one_all, jnp.concatenate(first_grads, axis=0), BF)
    second_part = dot_tn(one_all, jnp.concatenate(second_grads, axis=0), BF)
    out_first, out_second = block_reduce(out_part[:cut_o], out_part[cut_o:], 1)
    first_sum, second_sum = block_reduce(first_part, second_part, 0)
    first_sum, second_sum = first_sum.astype(F32), second_sum.astype(F32)
    output_grad = jnp.concatenate([out_first, out_second], axis=0).astype(F32)

    gain_pair = cube_sum(jnp.stack([gain_one_part, gain_two_part]))
    total = gain_pair
    for s in range(1, lax.axis_size("uly")):
        total = total + shift(gain_pair, s)

    return (
        block_out,
        restore(jnp.stack(input_grads)),
        total[0],
        first_sum[:, :qk],
        first_sum[:, qk : 2 * qk],
        jnp.concatenate([first_sum[:, 2 * qk :], second_sum[:, :cut_v]], axis=1),
        second_sum[:, cut_v:],
        output_grad,
        total[1],
        up_grad,
        down_grad,
    )


def solution(mesh):
    rows = P(None, ("blk", "uly"), None)
    gain, wide, tall = P("blk"), P("blk", "uly"), P("uly", "blk")
    return jax.shard_map(
        body,
        mesh=mesh,
        in_specs=(rows, gain, wide, wide, wide, wide, tall, gain, wide, tall, P(), P(), rows),
        out_specs=(rows, rows, gain, wide, wide, wide, wide, tall, gain, wide, tall),
        check_vma=False,
    )
```

time: 2310 us -> 1330 us (0.58)
  waiting for transfers between devices: 1780 us -> 717 us
  starting transfers between devices: 4.62 us -> 215 us
  blocking collectives: 92.9 us -> 0 us
  matrix products: 272 us -> 199 us
  local copies, waits for them, and re-layouts: 46.2 us -> 118 us
    reduce_scatter x22 -> x0, waiting for transfers between devices: 1160 us -> none  [the longest x8 565 us: collect(): lax.psum_scatter(partial_rows, 'uly', scatter_dimension=0, tiled=True)]
    ppermute x0 -> x185, waiting for transfers between devices: none -> 717 us  [the longest x146 377 us: swap(): return lax.ppermute(array, 'blk', [(b, b ^ mask) for b in range(count)])]
    all_gather x19 -> x0, waiting for transfers between devices: 612 us -> none  [the longest x8 327 us: spread(): return lax.all_gather(row_block, 'uly', axis=0, tiled=True)]
    ppermute x0 -> x185, starting transfers between devices: none -> 215 us  [the longest x146 114 us: swap(): return lax.ppermute(array, 'blk', [(b, b ^ mask) for b in range(count)])]
    dot_general x66 -> x75, matrix products: 272 us -> 199 us  [the longest x24 75.2 us: dot_nt(): lax.dot_general(left, right, (((1,), (1,)), ((), ())), preferred_element_...]
    unnamed x3 -> x0, blocking collectives: 52.1 us -> none
    unnamed x267 -> x605, local copies, waits for them, and re-layouts: 30.4 us -> 75 us
    add x25 -> x11, other arithmetic: 35 us -> 3.41 us  [the longest x1 2.22 us: feed_reduce(): up_sum = up_s if up_sum is None else up_sum + up_s]
  transfers between devices with their start and end apart: 41 -> 185, of which waited for: 36 -> 77; matrix products, arithmetic and copies ran while one was open for 13% -> 19% of each run, Pallas kernels for 0% -> 0%
where the time goes in v1:
time: 1330 us
  waiting for transfers between devices  717 us (54%)
  starting transfers between devices  215 us (16%)
  matrix products  199 us (15%)
  local copies, waits for them, and re-layouts  118 us (9%)
  other arithmetic  70.4 us (5%)
    ppermute x146, waiting for transfers between devices, swap(): return lax.ppermute(array, 'blk', [(b, b ^ mask) for b in range(count)])  377 us
    ppermute x39, waiting for transfers between devices, shift(): lax.ppermute(array, 'uly', [(z, (z + step) % count) for z in range(count)])  340 us
    ppermute x146, starting transfers between devices, swap(): return lax.ppermute(array, 'blk', [(b, b ^ mask) for b in range(count)])  114 us
    ppermute x39, starting transfers between devices, shift(): lax.ppermute(array, 'uly', [(z, (z + step) % count) for z in range(count)])  101 us
    dot_general x24, matrix products, dot_nt(): lax.dot_general(left, right, (((1,), (1,)), ((), ())), preferred_element_...  75.2 us
    unnamed x605, local copies, waits for them, and re-layouts  75 us
    dot_general x21, matrix products, dot_tn(): lax.dot_general(left, right, (((0,), (0,)), ((), ())), preferred_element_...  58.8 us
    dot_general x26, matrix products, dot_nn(): return jnp.dot(left, right, preferred_element_type=F32).astype(kind)  53.8 us
  transfers between devices with their start and end apart: 185, of which 77 were waited for; matrix products, arithmetic and copies ran while one was open for 19% of the time, Pallas kernels for 0%

profile of v1, /device:TPU:0, one launch (start us, length us, event | category | flops | bytes accessed | tf_op | source)
XLA Modules:
  0.0 1325.8 jit_solution(12991646787156057203)
XLA Ops:
  81.7 13.4 %collective-permute-done.2 = bf16[128,2048]{1,0:T(8,128)(2,1)S(1)} collective-permute-done((bf16[128,2048]{1,0:T(8,128)(2,1)}, bf16[128,2048]{1,0:T(8,128)(2,1)S(1)}, u32[]{:S(2)}, u32[]{:S(2)}) %collective-permute-start.2) | collective-permute-done | bytes 524320 | tf_op jit(solution)/shard_map/ppermute | solution.py:34
  96.7 29.2 %collective-permute-done.45 = bf16[128,2048]{1,0:T(8,128)(2,1)S(1)} collective-permute-done((bf16[128,2048]{1,0:T(8,128)(2,1)S(1)}, bf16[128,2048]{1,0:T(8,128)(2,1)S(1)}, u32[]{:S(2)}, u32[]{:S(2)}) %collective-permute-start.45) | collective-permute-done | bytes 524320 | tf_op jit(solution)/shard_map/ppermute | solution.py:34
  158.9 36.6 %collective-permute-done.82 = bf16[512,512]{1,0:T(8,128)(2,1)S(1)} collective-permute-done((bf16[512,512]{1,0:T(8,128)(2,1)S(1)}, bf16[512,512]{1,0:T(8,128)(2,1)S(1)}, u32[]{:S(2)}, u32[]{:S(2)}) %collective-permute-start.82) | collective-permute-done | bytes 524320 | tf_op jit(solution)/shard_map/ppermute | solution.py:34
  195.6 12.2 collective-permute-start.62
  209.3 28.3 %collective-permute-done.66 = bf16[512,512]{1,0:T(8,128)(2,1)S(1)} collective-permute-done((bf16[512,512]{1,0:T(8,128)(2,1)S(1)}, bf16[512,512]{1,0:T(8,128)(2,1)S(1)}, u32[]{:S(2)}, u32[]{:S(2)}) %collective-permute-start.66) | collective-permute-done | bytes 524320 | tf_op jit(solution)/shard_map/ppermute | solution.py:34
  242.1 10.4 collective-permute-done.76
  271.8 12.2 collective-permute-done.14
  373.3 13.0 collective-permute-done.15
  444.9 11.5 collective-permute-done.47
  457.5 10.5 collective-permute-done.22
  470.4 12.1 collective-permute-done.49
  511.3 29.9 %collective-permute-done.42 = bf16[128,2048]{1,0:T(8,128)(2,1)S(1)} collective-permute-done((bf16[128,2048]{1,0:T(8,128)(2,1)S(1)}, bf16[128,2048]{1,0:T(8,128)(2,1)S(1)}, u32[]{:S(2)}, u32[]{:S(2)}) %collective-permute-start.42) | collective-permute-done | bytes 524320 | tf_op jit(solution)/shard_map/ppermute | solution.py:34
  542.8 42.8 %collective-permute-done.55 = bf16[128,2048]{1,0:T(8,128)(2,1)S(1)} collective-permute-done((bf16[128,2048]{1,0:T(8,128)(2,1)S(1)}, bf16[128,2048]{1,0:T(8,128)(2,1)S(1)}, u32[]{:S(2)}, u32[]{:S(2)}) %collective-permute-start.55) | collective-permute-done | bytes 524320 | tf_op jit(solution)/shard_map/ppermute | solution.py:34
  599.7 10.8 fusion.291
  610.5 13.7 %multiply_convert_fusion = bf16[512,2048]{1,0:T(8,128)(2,1)} fusion(f32[512,2048]{1,0:T(8,128)} %fusion.75, bf16[512,2048]{1,0:T(8,128)(2,1)} %constant_dynamic-update-slice_fusion.110, bf16[512,2048]{1,0:T(8,128)(2,1)} %constant_dynamic-update-slice_fusion.102, bf16[512,2048]{1,0:T(8,128)(2,1)} %copy-done.172, ...), kind=kOutput, calls=%fused_computation.58 | convolution fusion | flops 4351590400 | bytes 16777216 | tf_op jit(solution)/shard_map/dot_general | solution.py:22
  643.1 10.5 convolution_convert_fusion.1
  677.7 10.6 collective-permute-done.161
  713.8 11.0 collective-permute-done.173
  815.4 45.0 %collective-permute-done.107 = bf16[128,2048]{1,0:T(8,128)(2,1)S(1)} collective-permute-done((bf16[128,2048]{1,0:T(8,128)(2,1)S(1)}, bf16[128,2048]{1,0:T(8,128)(2,1)S(1)}, u32[]{:S(2)}, u32[]{:S(2)}) %collective-permute-start.107) | collective-permute-done | bytes 524320 | tf_op jit(solution)/shard_map/ppermute | solution.py:34
  871.2 17.8 %collective-permute-start.167 = (bf16[512,512]{1,0:T(8,128)(2,1)}, bf16[512,512]{1,0:T(8,128)(2,1)}, u32[]{:S(2)}, u32[]{:S(2)}) collective-permute-start(bf16[512,512]{1,0:T(8,128)(2,1)} %add_convert_fusion.26), channel_id=1, source_target_pairs={{0,1},{1,2},{2,3},{3,0},{4,5},{5,6},{6,7},{7,4},{8,9},{9,10},{10,1... | collective-permute-start | bytes 1572872 | tf_op jit(solution)/shard_map/ppermute | solution.py:34
  889.6 19.2 %collective-permute-done.94 = bf16[128,2048]{1,0:T(8,128)(2,1)S(1)} collective-permute-done((bf16[128,2048]{1,0:T(8,128)(2,1)S(1)}, bf16[128,2048]{1,0:T(8,128)(2,1)S(1)}, u32[]{:S(2)}, u32[]{:S(2)}) %collective-permute-start.94) | collective-permute-done | bytes 524320 | tf_op jit(solution)/shard_map/ppermute | solution.py:34
  974.0 17.7 %collective-permute-done.179 = bf16[512,512]{0,1:T(8,128)(2,1)S(1)} collective-permute-done((bf16[512,512]{0,1:T(8,128)(2,1)S(1)}, bf16[512,512]{0,1:T(8,128)(2,1)S(1)}, u32[]{:S(2)}, u32[]{:S(2)}) %collective-permute-start.179) | collective-permute-done | bytes 524320 | tf_op jit(solution)/shard_map/ppermute | solution.py:34
  1009.7 12.0 collective-permute-done.144
  1046.1 11.6 collective-permute-done.98
  1138.8 11.2 convolution_convert_fusion.3
  1153.7 12.6 collective-permute-start.118
  1175.2 25.2 %collective-permute-done.124 = f32[2,256]{1,0:T(2,128)S(1)} collective-permute-done((f32[2,256]{1,0:T(2,128)S(1)}, f32[2,256]{1,0:T(2,128)S(1)}, u32[]{:S(2)}, u32[]{:S(2)}) %collective-permute-start.124) | collective-permute-done | bytes 2080 | tf_op jit(solution)/shard_map/ppermute | solution.py:34
  1200.5 12.5 collective-permute-start.122
  1227.6 31.7 %collective-permute-done.104 = bf16[128,2048]{1,0:T(8,128)(2,1)S(1)} collective-permute-done((bf16[128,2048]{1,0:T(8,128)(2,1)S(1)}, bf16[128,2048]{1,0:T(8,128)(2,1)S(1)}, u32[]{:S(2)}, u32[]{:S(2)}) %collective-permute-start.104) | collective-permute-done | bytes 524320 | tf_op jit(solution)/shard_map/ppermute | solution.py:34
  1265.7 17.5 %collective-permute-done.137 = bf16[256,1536]{0,1:T(8,128)(2,1)S(1)} collective-permute-done((bf16[256,1536]{0,1:T(8,128)(2,1)S(1)}, bf16[256,1536]{0,1:T(8,128)(2,1)S(1)}, u32[]{:S(2)}, u32[]{:S(2)}) %collective-permute-start.137) | collective-permute-done | bytes 786464 | tf_op jit(solution)/shard_map/ppermute | solution.py:29
  1288.1 16.4 %collective-permute-done.134 = bf16[256,1536]{0,1:T(8,128)(2,1)S(1)} collective-permute-done((bf16[256,1536]{0,1:T(8,128)(2,1)S(1)}, bf16[256,1536]{0,1:T(8,128)(2,1)S(1)}, u32[]{:S(2)}, u32[]{:S(2)}) %collective-permute-start.134) | collective-permute-done | bytes 786464 | tf_op jit(solution)/shard_map/ppermute | solution.py:29
  1304.5 14.5 %collective-permute-done.138 = bf16[256,1536]{0,1:T(8,128)(2,1)S(1)} collective-permute-done((bf16[256,1536]{0,1:T(8,128)(2,1)S(1)}, bf16[256,1536]{0,1:T(8,128)(2,1)S(1)}, u32[]{:S(2)}, u32[]{:S(2)}) %collective-permute-start.138) | collective-permute-done | bytes 786464 | tf_op jit(solution)/shard_map/ppermute | solution.py:29
  (1272 shorter events, 735.9 us)
Async XLA Ops:
  9.5 65.3 %collective-permute-start = (bf16[128,2048]{1,0:T(8,128)(2,1)}, bf16[128,2048]{1,0:T(8,128)(2,1)}, u32[]{:S(2)}, u32[]{:S(2)}) collective-permute-start(bf16[128,2048]{1,0:T(8,128)(2,1)} %get-tuple-element.232), channel_id=1, source_target_pairs={{0,3},{1,0},{2,1},{3,2},{4,7},{5,4},{6,5},{7,6},{8,11},{9,8},{10,9... | collective-permute-start | bytes 1572872 | tf_op jit(solution)/shard_map/ppermute | solution.py:34
  14.5 65.5 %collective-permute-start.1 = (bf16[128,2048]{1,0:T(8,128)(2,1)}, bf16[128,2048]{1,0:T(8,128)(2,1)}, u32[]{:S(2)}, u32[]{:S(2)}) collective-permute-start(bf16[128,2048]{1,0:T(8,128)(2,1)} %get-tuple-element.232), channel_id=1, source_target_pairs={{0,2},{1,3},{2,0},{3,1},{4,6},{5,7},{6,4},{7,5},{8,10},{9,11},{10,... | collective-permute-start | bytes 1572872 | tf_op jit(solution)/shard_map/ppermute | solution.py:34
  71.1 54.7 %collective-permute-start.45 = (bf16[128,2048]{1,0:T(8,128)(2,1)S(1)}, bf16[128,2048]{1,0:T(8,128)(2,1)S(1)}, u32[]{:S(2)}, u32[]{:S(2)}) collective-permute-start(bf16[128,2048]{1,0:T(8,128)(2,1)S(1)} %copy-done.138), channel_id=1, source_target_pairs={{0,2},{1,3},{2,0},{3,1},{4,6},{5,7},{6,4},{7,5},{8,10},{9,11},{10,... | collective-permute-start | bytes 1572872 | tf_op jit(solution)/shard_map/ppermute | solution.py:34
  74.8 52.6 %collective-permute-start.46 = (bf16[128,2048]{1,0:T(8,128)(2,1)S(1)}, bf16[128,2048]{1,0:T(8,128)(2,1)S(1)}, u32[]{:S(2)}, u32[]{:S(2)}) collective-permute-start(bf16[128,2048]{1,0:T(8,128)(2,1)S(1)} %copy-done.138), channel_id=1, source_target_pairs={{0,1},{1,2},{2,3},{3,0},{4,5},{5,6},{6,7},{7,4},{8,9},{9,10},{10,1... | collective-permute-start | bytes 1572872 | tf_op jit(solution)/shard_map/ppermute | solution.py:34
  79.9 55.8 %collective-permute-start.37 = (bf16[512,256]{1,0:T(8,128)(2,1)}, bf16[512,256]{1,0:T(8,128)(2,1)S(1)}, u32[]{:S(2)}, u32[]{:S(2)}) collective-permute-start(bf16[512,256]{1,0:T(8,128)(2,1)} %get-tuple-element.241), channel_id=1, source_target_pairs={{0,4},{4,0},{8,12},{12,8},{16,20},{20,16},{24,28},{28,24},{1,5},{5... | collective-permute-start | bytes 786440 | tf_op jit(solution)/shard_map/ppermute | solution.py:29
  80.0 64.7 %collective-permute-start.30 = (bf16[512,256]{1,0:T(8,128)(2,1)S(1)}, bf16[512,256]{1,0:T(8,128)(2,1)S(1)}, u32[]{:S(2)}, u32[]{:S(2)}) collective-permute-start(bf16[512,256]{1,0:T(8,128)(2,1)S(1)} %copy-done.148), channel_id=1, source_target_pairs={{0,4},{4,0},{8,12},{12,8},{16,20},{20,16},{24,28},{28,24},{1,5},{5... | collective-permute-start | bytes 786440 | tf_op jit(solution)/shard_map/ppermute | solution.py:29
  95.1 170.8 %collective-permute-start.6 = (bf16[256,1536]{1,0:T(8,128)(2,1)S(1)}, bf16[256,1536]{1,0:T(8,128)(2,1)S(1)}, u32[]{:S(2)}, u32[]{:S(2)}) collective-permute-start(bf16[256,1536]{1,0:T(8,128)(2,1)S(1)} %copy-done.115), channel_id=1, source_target_pairs={{0,8},{4,12},{8,0},{12,4},{16,24},{20,28},{24,16},{28,20},{1,9},{5... | collective-permute-start | bytes 2359304 | tf_op jit(solution)/shard_map/ppermute | solution.py:29
  144.8 50.8 %collective-permute-start.82 = (bf16[512,512]{1,0:T(8,128)(2,1)S(1)}, bf16[512,512]{1,0:T(8,128)(2,1)S(1)}, u32[]{:S(2)}, u32[]{:S(2)}) collective-permute-start(bf16[512,512]{1,0:T(8,128)(2,1)S(1)} %pad_maximum_fusion.27), channel_id=1, source_target_pairs={{0,2},{1,3},{2,0},{3,1},{4,6},{5,7},{6,4},{7,5},{8,10},{9,11},{10,... | collective-permute-start | bytes 1572872 | tf_op jit(solution)/shard_map/ppermute | solution.py:34
  150.5 117.0 %collective-permute-start.7 = (bf16[256,1536]{1,0:T(8,128)(2,1)S(1)}, bf16[256,1536]{1,0:T(8,128)(2,1)S(1)}, u32[]{:S(2)}, u32[]{:S(2)}) collective-permute-start(bf16[256,1536]{1,0:T(8,128)(2,1)S(1)} %copy-done.115), channel_id=1, source_target_pairs={{0,16},{4,20},{8,24},{12,28},{16,0},{20,4},{24,8},{28,12},{1,17},{... | collective-permute-start | bytes 2359304 | tf_op jit(solution)/shard_map/ppermute | solution.py:29
  157.8 50.0 %collective-permute-start.70 = (bf16[512,512]{1,0:T(8,128)(2,1)S(1)}, bf16[512,512]{1,0:T(8,128)(2,1)S(1)}, u32[]{:S(2)}, u32[]{:S(2)}) collective-permute-start(bf16[512,512]{1,0:T(8,128)(2,1)S(1)} %pad_maximum_fusion.26), channel_id=1, source_target_pairs={{0,3},{1,0},{2,1},{3,2},{4,7},{5,4},{6,5},{7,6},{8,11},{9,8},{10,9... | collective-permute-start | bytes 1572872 | tf_op jit(solution)/shard_map/ppermute | solution.py:34
  262.2 108.7 %collective-permute-start.9 = (bf16[256,1536]{1,0:T(8,128)(2,1)S(1)}, bf16[256,1536]{1,0:T(8,128)(2,1)S(1)}, u32[]{:S(2)}, u32[]{:S(2)}) collective-permute-start(bf16[256,1536]{1,0:T(8,128)(2,1)S(1)} %copy-done.115), channel_id=1, source_target_pairs={{0,4},{4,0},{8,12},{12,8},{16,20},{20,16},{24,28},{28,24},{1,5},{5... | collective-permute-start | bytes 2359304 | tf_op jit(solution)/shard_map/ppermute | solution.py:29
  390.9 117.4 %collective-permute-start.65 = (bf16[512,512]{1,0:T(8,128)(2,1)S(1)}, bf16[512,512]{1,0:T(8,128)(2,1)S(1)}, u32[]{:S(2)}, u32[]{:S(2)}) collective-permute-start(bf16[512,512]{1,0:T(8,128)(2,1)S(1)} %collective-permute-done.63), channel_id=1, source_target_pairs={{0,16},{4,20},{8,24},{12,28},{16,0},{20,4},{24,8},{28,12},{1,17},{... | collective-permute-start | bytes 1572872 | tf_op jit(solution)/shard_map/ppermute | solution.py:29
  508.2 77.4 %collective-permute-start.55 = (bf16[128,2048]{1,0:T(8,128)(2,1)S(1)}, bf16[128,2048]{1,0:T(8,128)(2,1)S(1)}, u32[]{:S(2)}, u32[]{:S(2)}) collective-permute-start(bf16[128,2048]{1,0:T(8,128)(2,1)S(1)} %get-tuple-element.201), channel_id=1, source_target_pairs={{0,2},{1,3},{2,0},{3,1},{4,6},{5,7},{6,4},{7,5},{8,10},{9,11},{10,... | collective-permute-start | bytes 1572872 | tf_op jit(solution)/shard_map/ppermute | solution.py:34
  511.2 74.4 %collective-permute-start.54 = (bf16[128,2048]{1,0:T(8,128)(2,1)S(1)}, bf16[128,2048]{1,0:T(8,128)(2,1)S(1)}, u32[]{:S(2)}, u32[]{:S(2)}) collective-permute-start(bf16[128,2048]{1,0:T(8,128)(2,1)S(1)} %get-tuple-element.199), channel_id=1, source_target_pairs={{0,1},{1,2},{2,3},{3,0},{4,5},{5,6},{6,7},{7,4},{8,9},{9,10},{10,1... | collective-permute-start | bytes 1572872 | tf_op jit(solution)/shard_map/ppermute | solution.py:34
  541.2 69.2 %collective-permute-start.91 = (bf16[2,128,2048]{2,1,0:T(8,128)(2,1)}, bf16[2,128,2048]{2,1,0:T(8,128)(2,1)}, u32[]{:S(2)}, u32[]{:S(2)}) collective-permute-start(bf16[2,128,2048]{2,1,0:T(8,128)(2,1)} %constant_dynamic-update-slice_fusion.134), channel_id=1, source_target_pairs={{0,4},{4,0},{8,12},{12,8},{16,20},{20,16},{24,28},{28,24},{1,5},{5... | collective-permute-start | bytes 3145736 | tf_op jit(solution)/shard_map/ppermute | solution.py:29
  659.7 81.1 %collective-permute-start.90 = (bf16[256,2048]{1,0:T(8,128)(2,1)S(1)}, bf16[256,2048]{1,0:T(8,128)(2,1)S(1)}, u32[]{:S(2)}, u32[]{:S(2)}) collective-permute-start(bf16[256,2048]{1,0:T(8,128)(2,1)S(1)} %pad_maximum_fusion.15), channel_id=1, source_target_pairs={{0,4},{4,0},{8,12},{12,8},{16,20},{20,16},{24,28},{28,24},{1,5},{5... | collective-permute-start | bytes 3145736 | tf_op jit(solution)/shard_map/ppermute | solution.py:29
  661.4 74.4 %collective-permute-start.92 = (bf16[256,2048]{1,0:T(8,128)(2,1)S(1)}, bf16[256,2048]{1,0:T(8,128)(2,1)S(1)}, u32[]{:S(2)}, u32[]{:S(2)}) collective-permute-start(bf16[256,2048]{1,0:T(8,128)(2,1)S(1)} %pad_maximum_fusion.16), channel_id=1, source_target_pairs={{0,4},{4,0},{8,12},{12,8},{16,20},{20,16},{24,28},{28,24},{1,5},{5... | collective-permute-start | bytes 3145736 | tf_op jit(solution)/shard_map/ppermute | solution.py:29
  742.5 210.6 %collective-permute-start.153 = (bf16[512,512]{1,0:T(8,128)(2,1)}, bf16[512,512]{1,0:T(8,128)(2,1)}, u32[]{:S(2)}, u32[]{:S(2)}) collective-permute-start(bf16[512,512]{1,0:T(8,128)(2,1)} %pad_maximum_fusion.30), channel_id=1, source_target_pairs={{0,16},{4,20},{8,24},{12,28},{16,0},{20,4},{24,8},{28,12},{1,17},{... | collective-permute-start | bytes 1572872 | tf_op jit(solution)/shard_map/ppermute | solution.py:29
  795.6 158.2 %collective-permute-start.155 = (bf16[512,512]{1,0:T(8,128)(2,1)}, bf16[512,512]{1,0:T(8,128)(2,1)}, u32[]{:S(2)}, u32[]{:S(2)}) collective-permute-start(bf16[512,512]{1,0:T(8,128)(2,1)} %add_convert_fusion.36), channel_id=1, source_target_pairs={{0,8},{4,12},{8,0},{12,4},{16,24},{20,28},{24,16},{28,20},{1,9},{5... | collective-permute-start | bytes 1572872 | tf_op jit(solution)/shard_map/ppermute | solution.py:29
  806.8 53.6 %collective-permute-start.107 = (bf16[128,2048]{1,0:T(8,128)(2,1)S(1)}, bf16[128,2048]{1,0:T(8,128)(2,1)S(1)}, u32[]{:S(2)}, u32[]{:S(2)}) collective-permute-start(bf16[128,2048]{1,0:T(8,128)(2,1)S(1)} %get-tuple-element.75), channel_id=1, source_target_pairs={{0,2},{1,3},{2,0},{3,1},{4,6},{5,7},{6,4},{7,5},{8,10},{9,11},{10,... | collective-permute-start | bytes 1572872 | tf_op jit(solution)/shard_map/ppermute | solution.py:34
  810.3 50.1 %collective-permute-start.108 = (bf16[128,2048]{1,0:T(8,128)(2,1)S(1)}, bf16[128,2048]{1,0:T(8,128)(2,1)S(1)}, u32[]{:S(2)}, u32[]{:S(2)}) collective-permute-start(bf16[128,2048]{1,0:T(8,128)(2,1)S(1)} %get-tuple-element.75), channel_id=1, source_target_pairs={{0,1},{1,2},{2,3},{3,0},{4,5},{5,6},{6,7},{7,4},{8,9},{9,10},{10,1... | collective-permute-start | bytes 1572872 | tf_op jit(solution)/shard_map/ppermute | solution.py:34
  811.5 59.7 %collective-permute-start.93 = (bf16[128,2048]{1,0:T(8,128)(2,1)S(1)}, bf16[128,2048]{1,0:T(8,128)(2,1)S(1)}, u32[]{:S(2)}, u32[]{:S(2)}) collective-permute-start(bf16[128,2048]{1,0:T(8,128)(2,1)S(1)} %get-tuple-element.202), channel_id=1, source_target_pairs={{0,3},{1,0},{2,1},{3,2},{4,7},{5,4},{6,5},{7,6},{8,11},{9,8},{10,9... | collective-permute-start | bytes 1572872 | tf_op jit(solution)/shard_map/ppermute | solution.py:34
  860.4 49.7 %collective-permute-start.95 = (bf16[128,2048]{1,0:T(8,128)(2,1)S(1)}, bf16[128,2048]{1,0:T(8,128)(2,1)S(1)}, u32[]{:S(2)}, u32[]{:S(2)}) collective-permute-start(bf16[128,2048]{1,0:T(8,128)(2,1)S(1)} %get-tuple-element.202), channel_id=1, source_target_pairs={{0,1},{1,2},{2,3},{3,0},{4,5},{5,6},{6,7},{7,4},{8,9},{9,10},{10,1... | collective-permute-start | bytes 1572872 | tf_op jit(solution)/shard_map/ppermute | solution.py:34
  871.2 84.0 %collective-permute-start.167 = (bf16[512,512]{1,0:T(8,128)(2,1)}, bf16[512,512]{1,0:T(8,128)(2,1)}, u32[]{:S(2)}, u32[]{:S(2)}) collective-permute-start(bf16[512,512]{1,0:T(8,128)(2,1)} %add_convert_fusion.26), channel_id=1, source_target_pairs={{0,1},{1,2},{2,3},{3,0},{4,5},{5,6},{6,7},{7,4},{8,9},{9,10},{10,1... | collective-permute-start | bytes 1572872 | tf_op jit(solution)/shard_map/ppermute | solution.py:34
  908.8 48.5 %collective-permute-start.163 = (bf16[512,512]{1,0:T(8,128)(2,1)}, bf16[512,512]{1,0:T(8,128)(2,1)}, u32[]{:S(2)}, u32[]{:S(2)}) collective-permute-start(bf16[512,512]{1,0:T(8,128)(2,1)} %add_convert_fusion.29), channel_id=1, source_target_pairs={{0,2},{1,3},{2,0},{3,1},{4,6},{5,7},{6,4},{7,5},{8,10},{9,11},{10,... | collective-permute-start | bytes 1572872 | tf_op jit(solution)/shard_map/ppermute | solution.py:34
  910.1 50.1 %collective-permute-start.159 = (bf16[512,512]{1,0:T(8,128)(2,1)}, bf16[512,512]{1,0:T(8,128)(2,1)}, u32[]{:S(2)}, u32[]{:S(2)}) collective-permute-start(bf16[512,512]{1,0:T(8,128)(2,1)} %add_convert_fusion.32), channel_id=1, source_target_pairs={{0,3},{1,0},{2,1},{3,2},{4,7},{5,4},{6,5},{7,6},{8,11},{9,8},{10,9... | collective-permute-start | bytes 1572872 | tf_op jit(solution)/shard_map/ppermute | solution.py:34
  972.5 50.8 %collective-permute-start.96 = (bf16[1,2,256,512]{3,2,1,0:T(8,128)(2,1)}, bf16[1,2,256,512]{3,2,1,0:T(8,128)(2,1)}, u32[]{:S(2)}, u32[]{:S(2)}) collective-permute-start(bf16[1,2,256,512]{3,2,1,0:T(8,128)(2,1)} %fusion.158), channel_id=1, source_target_pairs={{0,8},{4,12},{8,0},{12,4},{16,24},{20,28},{24,16},{28,20},{1,9},{5... | collective-permute-start | bytes 1572872 | tf_op jit(solution)/shard_map/ppermute | solution.py:29
  1153.7 62.9 %collective-permute-start.118 = (bf16[128,2048]{1,0:T(8,128)(2,1)S(1)}, bf16[128,2048]{1,0:T(8,128)(2,1)S(1)}, u32[]{:S(2)}, u32[]{:S(2)}) collective-permute-start(bf16[128,2048]{1,0:T(8,128)(2,1)S(1)} %get-tuple-element.190), channel_id=1, source_target_pairs={{0,3},{1,0},{2,1},{3,2},{4,7},{5,4},{6,5},{7,6},{8,11},{9,8},{10,9... | collective-permute-start | bytes 1572872 | tf_op jit(solution)/shard_map/ppermute | solution.py:34
  1166.3 51.1 %collective-permute-start.117 = (bf16[128,2048]{1,0:T(8,128)(2,1)S(1)}, bf16[128,2048]{1,0:T(8,128)(2,1)S(1)}, u32[]{:S(2)}, u32[]{:S(2)}) collective-permute-start(bf16[128,2048]{1,0:T(8,128)(2,1)S(1)} %get-tuple-element.191), channel_id=1, source_target_pairs={{0,2},{1,3},{2,0},{3,1},{4,6},{5,7},{6,4},{7,5},{8,10},{9,11},{10,... | collective-permute-start | bytes 1572872 | tf_op jit(solution)/shard_map/ppermute | solution.py:34
  1166.5 50.8 %collective-permute-start.116 = (bf16[128,2048]{1,0:T(8,128)(2,1)S(1)}, bf16[128,2048]{1,0:T(8,128)(2,1)S(1)}, u32[]{:S(2)}, u32[]{:S(2)}) collective-permute-start(bf16[128,2048]{1,0:T(8,128)(2,1)S(1)} %get-tuple-element.189), channel_id=1, source_target_pairs={{0,1},{1,2},{2,3},{3,0},{4,5},{5,6},{6,7},{7,4},{8,9},{9,10},{10,1... | collective-permute-start | bytes 1572872 | tf_op jit(solution)/shard_map/ppermute | solution.py:34
  1227.6 56.4 %collective-permute-start.128 = (bf16[256,1536]{0,1:T(8,128)(2,1)S(1)}, bf16[256,1536]{0,1:T(8,128)(2,1)S(1)}, u32[]{:S(2)}, u32[]{:S(2)}) collective-permute-start(bf16[256,1536]{0,1:T(8,128)(2,1)S(1)} %get-tuple-element.161), channel_id=1, source_target_pairs={{0,4},{4,0},{8,12},{12,8},{16,20},{20,16},{24,28},{28,24},{1,5},{5... | collective-permute-start | bytes 2359304 | tf_op jit(solution)/shard_map/ppermute | solution.py:29
  1262.0 57.3 %collective-permute-start.125 = (bf16[256,1536]{0,1:T(8,128)(2,1)S(1)}, bf16[256,1536]{0,1:T(8,128)(2,1)S(1)}, u32[]{:S(2)}, u32[]{:S(2)}) collective-permute-start(bf16[256,1536]{0,1:T(8,128)(2,1)S(1)} %get-tuple-element.159), channel_id=1, source_target_pairs={{0,4},{4,0},{8,12},{12,8},{16,20},{20,16},{24,28},{28,24},{1,5},{5... | collective-permute-start | bytes 2359304 | tf_op jit(solution)/shard_map/ppermute | solution.py:29
  (375 other events, 10371.1 us)

commit v2 on v1

v2 whole, which is shorter than its diff:
```python
import functools

import jax
import jax.numpy as jnp
from jax import lax
from jax.experimental import pallas as pl
from jax.experimental.pallas import tpu as pltpu
from jax.sharding import Mesh
from jax.sharding import PartitionSpec as P

EPSILON = 1e-05
BF = jnp.bfloat16
F32 = jnp.float32
AXES = ("chip", "core", "uly")
BLK = ("chip", "core")
MESH = pl.DeviceIdType.MESH
VMEM_LIMIT = 60 * 1024 * 1024


def dot_nn(left, right, kind=F32):
    return jnp.dot(left, right, preferred_element_type=F32).astype(kind)


def dot_tn(left, right, kind=F32):
    return lax.dot_general(
        left, right, (((0,), (0,)), ((), ())), preferred_element_type=F32
    ).astype(kind)


def dot_nt(left, right, kind=F32):
    return lax.dot_general(
        left, right, (((1,), (1,)), ((), ())), preferred_element_type=F32
    ).astype(kind)


def block_index():
    return lax.axis_index("chip") * 2 + lax.axis_index("core")


def block_count():
    return lax.axis_size("chip") * 2


def swap(array, mask):
    if mask == 1:
        return lax.ppermute(array, "core", [(0, 1), (1, 0)])
    count = lax.axis_size("chip")
    return lax.ppermute(array, "chip", [(b, b ^ (mask // 2)) for b in range(count)])


def shift(array, step):
    count = lax.axis_size("uly")
    return lax.ppermute(array, "uly", [(z, (z + step) % count) for z in range(count)])


def is_cube():
    return lax.axis_size("chip") == 4 and lax.axis_size("uly") == 4


def masks():
    return [2 * k + j for j in range(2) for k in range(4)]


def plane_gather(first, second):
    first_x = swap(first, 2)
    second_y = swap(second, 4)
    first_y, first_xy = swap(first, 4), swap(first_x, 4)
    second_x, second_xy = swap(second, 2), swap(second_y, 2)
    return [first, first_x, first_y, first_xy], [second, second_x, second_y, second_xy]


def exchange(pieces):
    if not is_cube():
        return [lax.all_gather(p, BLK) for p in pieces]
    half = len(pieces) // 2
    a, b = plane_gather(jnp.stack(pieces[:half]), jnp.stack(pieces[half:]))
    got = []
    for four in (a, b):
        full = jnp.stack(four + [swap(p, 1) for p in four])
        got += [full[:, i] for i in range(full.shape[1])]
    return got


def spread(rows):
    return lax.all_gather(rows, "uly", axis=1, tiled=True)


def collect(partial):
    return lax.psum_scatter(partial.astype(BF), "uly", scatter_dimension=1, tiled=True).astype(F32)


def core_cut(array, dim):
    core = lax.axis_index("core")
    half = array.shape[dim] // 2
    own = lax.dynamic_slice_in_dim(array, core * half, half, dim)
    other = lax.dynamic_slice_in_dim(array, (1 - core) * half, half, dim)
    return own, other


def core_join(own, other, dim):
    first = lax.axis_index("core") == 0
    return jnp.concatenate([jnp.where(first, own, other), jnp.where(first, other, own)], axis=dim)


def feed_weights(up_shard, down_shard):
    own, other = core_cut(up_shard, 1)
    up = core_join(own, swap(other, 1), 0)
    own, other = core_cut(down_shard, 0)
    down = core_join(own, swap(other, 1), 1)
    pair = lax.all_gather(jnp.stack([up, down.T]), ("chip", "uly"), axis=0, tiled=False)
    chips, count = lax.axis_size("chip"), lax.axis_size("uly")
    rows, hidden = up.shape
    pair = pair.reshape(chips, count, 2, rows, hidden)
    return pair


def feed_reduce(up_grad, down_grad):
    pair = jnp.stack([up_grad, down_grad], axis=2)
    chips, count = pair.shape[:2]
    pair = pair.reshape(chips * count * 2, *pair.shape[3:])
    total = lax.psum_scatter(pair, ("chip", "uly"), scatter_dimension=0, tiled=True)
    half = total.shape[1] // 2
    own, other = core_cut(total, 1)
    both_halves = core_join(own, swap(other, 1), 2).astype(F32)
    return both_halves[0], both_halves[1].T


def normed(values):
    center = values - jnp.mean(values, axis=-1, keepdims=True)
    scale = lax.rsqrt(jnp.mean(center * center, axis=-1, keepdims=True) + EPSILON)
    return center * scale, scale


def norm_back(grad, hat, scale):
    return scale * (
        grad
        - jnp.mean(grad, axis=-1, keepdims=True)
        - hat * jnp.mean(grad * hat, axis=-1, keepdims=True)
    )


GELU_A = 0.7978845608028654
GELU_B = 0.044715


def gelu_pair(u):
    square = u * u
    tanh = jnp.tanh(GELU_A * u * (1.0 + GELU_B * square))
    slope = 0.5 * (1.0 + tanh) + 0.5 * u * (1.0 - tanh * tanh) * GELU_A * (
        1.0 + 3.0 * GELU_B * square
    )
    return 0.5 * u * (1.0 + tanh), slope


def segment_ids(positions, lengths_row):
    count = lengths_row.shape[0]
    before = jnp.arange(count)[None, :] < jnp.arange(count)[:, None]
    bounds = jnp.sum(jnp.where(before, lengths_row[None, :], 0), axis=1)
    return jnp.sum((bounds[None, :] <= positions[:, None]).astype(jnp.int32), axis=1)


def decay_parts(rates, lengths_row, length):
    me = block_index()
    count = block_count()
    places = jnp.arange(length, dtype=jnp.int32)
    seg = segment_ids(me * length + places, lengths_row)
    ends = segment_ids((jnp.arange(count, dtype=jnp.int32) + 1) * length - 1, lengths_row)
    seg_prev = segment_ids(jnp.reshape(me * length - 1, (1,)), lengths_row)[0]
    offset = places[:, None] - places[None, :]
    causal = (offset >= 0) & (seg[:, None] == seg[None, :])
    far = jnp.maximum(offset, 0).astype(F32)
    inner = jnp.where(causal[None], jnp.exp(-rates[:, None, None] * far[None]), 0.0)
    at = places.astype(F32)
    entry = jnp.where(seg == seg_prev, jnp.exp(-rates[:, None] * (at + 1.0)), 0.0)
    leave = jnp.where(seg == seg[length - 1], jnp.exp(-rates[:, None] * (length - 1.0 - at)), 0.0)
    if is_cube():
        source = me ^ jnp.asarray(masks(), jnp.int32)
    else:
        source = jnp.arange(count, dtype=jnp.int32)
    end_of = ends[source]
    end_before = jnp.where(source > 0, ends[jnp.maximum(source - 1, 0)], 0)
    past = jnp.maximum(me - 1 - source, 0).astype(F32)
    ahead = jnp.maximum(source - 1 - me, 0).astype(F32)
    from_past = jnp.where(
        (source < me) & (end_of == seg_prev), jnp.exp(-rates[:, None] * (length * past)), 0.0
    )
    from_ahead = jnp.where(
        (source > me) & (end_before == ends[me]), jnp.exp(-rates[:, None] * (length * ahead)), 0.0
    )
    return inner, entry[:, :, None], leave[:, :, None], from_past, from_ahead


def state_sum(weights, states):
    return jnp.einsum("hb,bhde->hde", weights, states.astype(F32))


def retention_state(heads, leave):
    return jnp.stack(
        [
            dot_tn((k.astype(F32) * leave[h]).astype(BF), v, BF)
            for h, (q, k, v) in enumerate(heads)
        ]
    )


def retention(heads, parts, state):
    inner, entry = parts[0], parts[1]
    out = []
    for h, (q, k, v) in enumerate(heads):
        scores = (dot_nt(q, k) * inner[h]).astype(BF)
        out.append(dot_nn(scores, v) + entry[h] * dot_nn(q, state[h].astype(BF)))
    return out


def mix(gate, retained):
    out = []
    for h, r in enumerate(retained):
        g = gate[:, h * r.shape[1] : (h + 1) * r.shape[1]]
        out.append((g * jax.nn.sigmoid(g) * normed(r)[0]).astype(BF))
    return jnp.concatenate(out, axis=1)


def mix_back(gate, retained, grad_mixed):
    grad_gate, grad_retained = [], []
    for h, r in enumerate(retained):
        cols = slice(h * r.shape[1], (h + 1) * r.shape[1])
        g, gm = gate[:, cols], grad_mixed[:, cols]
        sigma = jax.nn.sigmoid(g)
        hat, scale = normed(r)
        grad_gate.append((gm * hat * (sigma + g * sigma * (1.0 - sigma))).astype(BF))
        grad_retained.append(norm_back(gm * g * sigma, hat, scale).astype(BF))
    return jnp.concatenate(grad_gate, axis=1), grad_retained


def retention_back(heads, parts, state, grad_retained, grad_state):
    inner, entry, leave = parts[0], parts[1], parts[2]
    grads = []
    for h, (q, k, v) in enumerate(heads):
        gr = grad_retained[h]
        scores = (dot_nt(q, k) * inner[h]).astype(BF)
        pulls = (dot_nt(gr, v) * inner[h]).astype(BF)
        gs, st = grad_state[h].astype(BF), state[h].astype(BF)
        gq = dot_nn(pulls, k) + entry[h] * dot_nt(gr, st)
        gk = dot_tn(pulls, q) + leave[h] * dot_nt(v, gs)
        gv = dot_tn(scores, gr) + leave[h] * dot_nn(k, gs)
        grads.append((gq.astype(BF), gk.astype(BF), gv.astype(BF)))
    return grads


def vmem():
    return pl.BlockSpec(memory_space=pltpu.VMEM)


def anywhere():
    return pl.BlockSpec(memory_space=pl.ANY)


def greet(plane=False, line=False, cores=False, pair=False):
    barrier = pltpu.get_barrier_semaphore()
    chip, core, z = (lax.axis_index(a) for a in AXES)
    others = []
    if plane:
        others += [{"chip": chip ^ 1}, {"chip": chip ^ 2}]
    if cores:
        others.append({"core": 1 - core})
    if pair:
        others.append({"uly": z ^ 1})
    for to in others:
        pl.semaphore_signal(barrier, inc=1, device_id=to, device_id_type=MESH)
    count = len(others)
    if line:
        last = lax.axis_size("uly") - 1

        @pl.when(z > 0)
        def _():
            pl.semaphore_signal(barrier, inc=1, device_id={"uly": z - 1}, device_id_type=MESH)

        @pl.when(z < last)
        def _():
            pl.semaphore_signal(barrier, inc=1, device_id={"uly": z + 1}, device_id_type=MESH)

        count = count + jnp.where(z > 0, 1, 0) + jnp.where(z < last, 1, 0)
    pl.semaphore_wait(barrier, count)


class PlaneGather:
    def __init__(self, own, at, x_first, send, recv, cores=True):
        chip, core = lax.axis_index("chip"), lax.axis_index("core")
        x, y, other = {"chip": chip ^ 1}, {"chip": chip ^ 2}, {"core": 1 - core}

        def copy(i, src, place, to):
            return pltpu.make_async_remote_copy(
                src_ref=src,
                dst_ref=at(place),
                send_sem=send.at[i],
                recv_sem=recv.at[i],
                device_id=to,
                device_id_type=MESH,
            )

        self.x_first = x_first
        self.copies = [
            copy(0, own, 1, x),
            copy(1, own, 2, y),
            copy(2, at(1), 3, y) if x_first else copy(2, at(2), 3, x),
        ]
        self.cores = cores
        if cores:
            self.copies += [
                copy(3, own, 4, other),
                copy(4, at(1), 5, other),
                copy(5, at(2), 6, other),
                copy(6, at(3), 7, other),
            ]

    def start(self):
        for i in (0, 1) if self.x_first else (1, 0):
            self.copies[i].start()
        if self.cores:
            self.copies[3].start()

    def near(self):
        first = 0 if self.x_first else 1
        self.copies[first].wait_recv()
        self.copies[2].start()
        if self.cores:
            self.copies[4 + first].start()

    def far(self):
        second = 1 if self.x_first else 0
        self.copies[second].wait_recv()
        if self.cores:
            self.copies[4 + second].start()

    def corner(self):
        self.copies[2].wait_recv()
        if self.cores:
            self.copies[6].start()

    def finish(self):
        for c in self.copies[3:]:
            c.wait_recv()
        for c in self.copies:
            c.wait_send()


class LineGather:
    def __init__(self, slots, send, recv):
        self.z = lax.axis_index("uly")
        self.last = lax.axis_size("uly") - 1
        self.slots, self.send, self.recv = slots, send, recv

    def copy(self, right, d):
        z, last = self.z, self.last
        at = jnp.maximum(z - d, 0) if right else jnp.minimum(z + d, last)
        to = jnp.minimum(z + 1, last) if right else jnp.maximum(z - 1, 0)
        way = 0 if right else 1
        return pltpu.make_async_remote_copy(
            src_ref=self.slots.at[at],
            dst_ref=self.slots.at[at],
            send_sem=self.send.at[way, d],
            recv_sem=self.recv.at[way, d],
            device_id={"uly": to},
            device_id_type=MESH,
        )

    def pass_on(self, d):
        z, last = self.z, self.last

        @pl.when((z - d >= 0) & (z < last))
        def _():
            self.copy(True, d).start()

        @pl.when((z + d <= last) & (z > 0))
        def _():
            self.copy(False, d).start()

    def take(self, d, then):
        z, last = self.z, self.last

        @pl.when(z - d >= 0)
        def _():
            self.copy(True, d - 1).wait_recv()

        @pl.when(z + d <= last)
        def _():
            self.copy(False, d - 1).wait_recv()

        if d < last:
            self.pass_on(d)

        @pl.when(z - d >= 0)
        def _():
            then(jnp.maximum(z - d, 0))

        @pl.when(z + d <= last)
        def _():
            then(jnp.minimum(z + d, last))

    def finish(self):
        z, last = self.z, self.last
        for d in range(last):

            @pl.when((z - d >= 0) & (z < last))
            def _():
                self.copy(True, d).wait_send()

            @pl.when((z + d <= last) & (z > 0))
            def _():
                self.copy(False, d).wait_send()


class LineReduce:
    def __init__(self, make, out, held, came, send, recv):
        self.z = lax.axis_index("uly")
        self.last = lax.axis_size("uly") - 1
        self.make, self.out, self.held, self.came = make, out, held, came
        self.send, self.recv = send, recv

    def copy(self, right, d):
        z, last = self.z, self.last
        way = 0 if right else 1
        to = jnp.minimum(z + 1, last) if right else jnp.maximum(z - 1, 0)
        return pltpu.make_async_remote_copy(
            src_ref=self.held.at[way, d - 1],
            dst_ref=self.came.at[way, d - 1],
            send_sem=self.send.at[way, d - 1],
            recv_sem=self.recv.at[way, d - 1],
            device_id={"uly": to},
            device_id_type=MESH,
        )

    def step(self, d):
        z, last = self.z, self.last
        for right in (True, False):
            way = 0 if right else 1
            valid = (z + d <= last) if right else (z - d >= 0)
            more = (z > 0) if right else (z < last)
            to = jnp.minimum(z + d, last) if right else jnp.maximum(z - d, 0)

            @pl.when(valid)
            def _():
                self.make(to, self.held.at[way, d - 1])

                if d < last:

                    @pl.when(more)
                    def _():
                        self.copy(right, d + 1).wait_recv()
                        self.held[way, d - 1] = (
                            self.held[way, d - 1].astype(F32) + self.came[way, d].astype(F32)
                        ).astype(BF)

                self.copy(right, d).start()

    def close(self):
        z, last = self.z, self.last
        self.make(z, self.out)

        @pl.when(z > 0)
        def _():
            self.copy(True, 1).wait_recv()
            self.out[...] += self.came[0, 0].astype(F32)

        @pl.when(z < last)
        def _():
            self.copy(False, 1).wait_recv()
            self.out[...] += self.came[1, 0].astype(F32)

        for d in range(1, last + 1):

            @pl.when(z + d <= last)
            def _():
                self.copy(True, d).wait_send()

            @pl.when(z - d >= 0)
            def _():
                self.copy(False, d).wait_send()


def chunk_of(place, width):
    chip, core = lax.axis_index("chip"), lax.axis_index("core")
    block = (chip ^ (place % 4)) * 2 + (core ^ (place // 4))
    return pl.ds(pl.multiple_of(block * width, width), width)


def chip_order(place, width):
    core = lax.axis_index("core")
    return pl.ds(pl.multiple_of((place % 4) * (2 * width) + (core ^ (place // 4)) * width, width), width)


def project_kernel(
    tok_ref,
    gain_ref,
    first_hbm,
    second_hbm,
    out_hbm,
    one_ref,
    first_ref,
    high_ref,
    gate_ref,
    w_first_hbm,
    w_second_hbm,
    w_out_hbm,
    gains_ref,
    slots,
    wa,
    wb,
    gains,
    psend,
    precv,
    zsend,
    zrecv,
    lsem,
):
    z = lax.axis_index("uly")
    rows = tok_ref.shape[0] // 2
    width = tok_ref.shape[1]
    piece = width // 8
    greet(plane=True, line=True, cores=True)
    items = [
        PlaneGather(gain_ref, lambda p: gains.at[p], True, psend.at[0], precv.at[0]),
        PlaneGather(
            first_hbm,
            lambda p: wa.at[pl.ds(p * piece, piece)],
            True,
            psend.at[1],
            precv.at[1],
        ),
        PlaneGather(
            second_hbm,
            lambda p: wb.at[pl.ds(p * piece, piece)],
            False,
            psend.at[2],
            precv.at[2],
        ),
    ]
    half = out_hbm.shape[0] // 2
    for i in range(2):
        part = pl.ds(i * half, half)
        items.append(
            PlaneGather(
                out_hbm.at[part],
                lambda p, part=part: w_out_hbm.at[part, pl.ds(p * piece, piece)],
                i == 0,
                psend.at[3 + i],
                precv.at[3 + i],
            )
        )
    line = LineGather(slots, zsend, zrecv)
    slots[z] = tok_ref[...]
    line.pass_on(0)
    for item in items[:3]:
        item.start()
    local = [
        pltpu.make_async_copy(first_hbm, wa.at[pl.ds(0, piece)], lsem.at[0]),
        pltpu.make_async_copy(second_hbm, wb.at[pl.ds(0, piece)], lsem.at[1]),
        pltpu.make_async_copy(out_hbm, w_out_hbm.at[:, pl.ds(0, piece)], lsem.at[2]),
    ]
    for c in local:
        c.start()
    gains[0] = gain_ref[...]
    items[0].near()
    items[0].far()
    items[0].corner()
    items[0].finish()
    gains_ref[...] = gains[...]

    def normalize(slot):
        step = 32
        for m in range(2):

            @pl.loop(0, rows // step)
            def _(i):
                at = pl.multiple_of(i * step, step)
                v = slots[slot, pl.ds(m * rows + at, step), :].astype(F32)
                mean = jnp.mean(v, axis=-1, keepdims=True)
                center = v - mean
                scale = lax.rsqrt(jnp.mean(center * center, axis=-1, keepdims=True) + EPSILON)
                to = pl.ds(pl.multiple_of(slot * rows + at, step), step)
                for p in range(8):
                    src = slots[slot, pl.ds(m * rows + at, step), chunk_of(p, piece)].astype(F32)
                    one_ref[m, to, pl.ds(p * piece, piece)] = (
                        (src - mean) * scale * gains[p, 0:1, :].astype(F32)
                    ).astype(BF)

    normalize(z)
    line.take(1, normalize)
    items[1].near()
    items[2].near()
    for item in items[3:]:
        item.start()
    items[1].far()
    items[2].far()
    line.take(2, normalize)
    items[1].corner()
    items[2].corner()
    for item in items[3:]:
        item.near()
    line.take(3, normalize)
    for item in items[1:3]:
        item.finish()
    local[0].wait()
    local[1].wait()
    outs = [
        pltpu.make_async_copy(wa, w_first_hbm, lsem.at[3]),
        pltpu.make_async_copy(wb, w_second_hbm, lsem.at[4]),
    ]
    for c in outs:
        c.start()
    tile = 512
    for m in range(2):

        @pl.loop(0, wa.shape[1] // tile)
        def _(n):
            cols = pl.ds(pl.multiple_of(n * tile, tile), tile)
            first_ref[m, :, cols] = jnp.dot(
                one_ref[m], wa[:, cols], preferred_element_type=F32
            ).astype(BF)

        high = high_ref.shape[2]

        @pl.loop(0, high // tile)
        def _(n):
            cols = pl.ds(pl.multiple_of(n * tile, tile), tile)
            high_ref[m, :, cols] = jnp.dot(
                one_ref[m], wb[:, cols], preferred_element_type=F32
            ).astype(BF)

        @pl.loop(0, gate_ref.shape[2] // tile)
        def _(n):
            cols = pl.ds(pl.multiple_of(n * tile, tile), tile)
            from_ = pl.ds(pl.multiple_of(high + n * tile, tile), tile)
            gate_ref[m, :, cols] = jnp.dot(
                one_ref[m], wb[:, from_], preferred_element_type=F32
            )

    for item in items[3:]:
        item.far()
        item.corner()
        item.finish()
    line.finish()
    local[2].wait()
    for c in outs:
        c.wait()


def add_rows_kernel(
    x_ref,
    w_ref,
    up_hbm,
    down_hbm,
    out_ref,
    ups_hbm,
    downs_hbm,
    held,
    came,
    send,
    recv,
    psend,
    precv,
    lsem,
):
    rows = out_ref.shape[0] // 2
    width = out_ref.shape[1] // 8
    greet(plane=True, line=True)
    part = up_hbm.shape[0]

    def up_at(p):
        return ups_hbm.at[pl.ds(p * part, part)]

    def down_at(p):
        return downs_hbm.at[:, pl.ds(p * part, part)]

    items = [
        PlaneGather(up_hbm, up_at, True, psend.at[0], precv.at[0], False),
        PlaneGather(down_hbm, down_at, False, psend.at[1], precv.at[1], False),
    ]
    local = [
        pltpu.make_async_copy(up_hbm, up_at(0), lsem.at[0]),
        pltpu.make_async_copy(down_hbm, down_at(0), lsem.at[1]),
    ]

    def make(a, to):
        at = pl.ds(pl.multiple_of(a * rows, rows), rows)
        x = jnp.concatenate([x_ref[0, at, :], x_ref[1, at, :]], axis=0)

        @pl.loop(0, 8)
        def _(p):
            cols = w_ref[:, pl.ds(pl.multiple_of(p * width, width), width)]
            to[:, chip_order(p, width)] = jnp.dot(x, cols, preferred_element_type=F32).astype(
                to.dtype
            )

    line = LineReduce(make, out_ref, held, came, send, recv)
    for item in items:
        item.start()
    line.step(3)
    for c in local:
        c.start()
    for item in items:
        item.near()
    line.step(2)
    for item in items:
        item.far()
    line.step(1)
    line.close()
    for item in items:
        item.corner()
    for item in items:
        item.finish()
    for c in local:
        c.wait()


def fan_out_kernel(
    rows_ref,
    w_ref,
    up_hbm,
    down_hbm,
    wide_ref,
    grad_ref,
    up_ref,
    down_ref,
    slots,
    ordered,
    near_up,
    near_down,
    came_up,
    came_down,
    send,
    recv,
    psend,
    precv,
    lsem,
):
    z = lax.axis_index("uly")
    rows = rows_ref.shape[0] // 2
    width = rows_ref.shape[1] // 8
    greet(plane=True, line=True)
    line = LineGather(slots, send, recv)
    slots[z] = rows_ref[...]
    line.pass_on(0)
    local = [
        pltpu.make_async_copy(up_hbm, near_up, lsem.at[0]),
        pltpu.make_async_copy(down_hbm, near_down, lsem.at[1]),
    ]
    for c in local:
        c.start()
    groups = [
        PlaneReduce(None, near_up, came_up, True, psend.at[0], precv.at[0]),
        PlaneReduce(None, near_down, came_down, False, psend.at[1], precv.at[1]),
    ]
    for c in local:
        c.wait()
    for g in groups:
        g.start_first()

    def multiply(slot):
        at = pl.ds(pl.multiple_of(slot * rows, rows), rows)
        for m in range(2):
            wide_ref[m, at, :] = slots[slot, m * rows : (m + 1) * rows, :]
        for p in range(8):
            ordered[:, p * width : (p + 1) * width] = slots[slot, :, chip_order(p, width)]
        tile = 256

        @pl.loop(0, w_ref.shape[0] // tile)
        def _(n):
            part = pl.ds(pl.multiple_of(n * tile, tile), tile)
            product = dot_nt(ordered[...], w_ref[part, :])
            for m in range(2):
                grad_ref[m, at, part] = product[m * rows : (m + 1) * rows]

    multiply(z)
    line.take(1, multiply)
    for g in groups:
        g.first_sums(0)
    line.take(2, multiply)
    for g in groups:
        g.first_sums(1)
    line.take(3, multiply)
    groups[0].finish(up_ref)
    groups[1].finish(down_ref)
    line.finish()


def feed_kernel(
    hid_ref,
    douts_ref,
    gain_ref,
    ups_ref,
    downs_ref,
    out_ref,
    grad_ref,
    gain_grad_ref,
    up_grad_ref,
    down_grad_ref,
    two,
    act,
    gu,
    sums,
    held,
    came,
    send,
    recv,
):
    core, z = lax.axis_index("core"), lax.axis_index("uly")
    rows, width = hid_ref.shape
    hidden = ups_ref.shape[1]
    other, pair = {"core": 1 - core}, {"uly": z ^ 1}
    greet(cores=True, pair=True)

    def group(g):
        return pl.ds(g * rows, rows)

    def copy(i, src, dst, to):
        return pltpu.make_async_remote_copy(
            src_ref=src,
            dst_ref=dst,
            send_sem=send.at[i],
            recv_sem=recv.at[i],
            device_id=to,
            device_id_type=MESH,
        )

    step = 32

    @pl.loop(0, rows // step)
    def _(i):
        at = pl.ds(pl.multiple_of(i * step, step), step)
        hat, _scale = normed(hid_ref[at, :])
        two[at, :] = (hat * gain_ref[...]).astype(BF)

    to_pair = copy(0, two.at[group(0)], two.at[group(2)], pair)
    to_other = copy(1, two.at[group(0)], two.at[group(1)], other)
    through = copy(2, two.at[group(2)], two.at[group(3)], other)
    to_pair.start()
    to_other.start()

    def work(g):
        tile = 256

        @pl.loop(0, hidden // tile)
        def _(n):
            cols = pl.ds(pl.multiple_of(n * tile, tile), tile)
            upward = jnp.dot(two[group(g), :], ups_ref[:, cols], preferred_element_type=F32)
            value, slope = gelu_pair(upward)
            act[group(g), cols] = value.astype(BF)
            pulled = dot_nt(douts_ref[group(g), :], downs_ref[cols, :])
            gu[group(g), cols] = (pulled * slope).astype(BF)

        tile = 512

        @pl.loop(0, width // tile)
        def _(n):
            cols = pl.ds(pl.multiple_of(n * tile, tile), tile)
            back = dot_nt(gu[group(g), :], ups_ref[cols, :])
            down = jnp.dot(act[group(g), :], downs_ref[:, cols], preferred_element_type=F32)
            if g == 0:
                sums[0, :, cols] = back
                sums[1, :, cols] = down
            else:
                held[g - 1, 0, :, cols] = back.astype(BF)
                held[g - 1, 1, :, cols] = down.astype(BF)

    returns = [copy(3 + i, held.at[0, i], came.at[0, i], other) for i in range(2)]
    returns += [copy(5 + i, held.at[2, i], came.at[1, i], other) for i in range(2)]
    last = [copy(7 + i, held.at[1, i], came.at[2, i], pair) for i in range(2)]

    work(0)
    to_other.wait_recv()
    work(1)
    for c in returns[:2]:
        c.start()
    to_pair.wait_recv()
    through.start()
    work(2)
    through.wait_recv()
    work(3)
    for c in returns[2:]:
        c.start()
    for i in range(2):
        returns[2 + i].wait_recv()

        @pl.loop(0, rows // step)
        def _(r):
            at = pl.ds(pl.multiple_of(r * step, step), step)
            held[1, i, at, :] = (
                held[1, i, at, :].astype(F32) + came[1, i, at, :].astype(F32)
            ).astype(BF)

        last[i].start()
    tile = 512

    @pl.loop(0, width // tile)
    def _(n):
        cols = pl.ds(pl.multiple_of(n * tile, tile), tile)
        up_grad_ref[n] = dot_tn(two[:, cols], gu[...], BF)
        down_grad_ref[n] = dot_tn(act[...], douts_ref[:, cols], BF)

    for i in range(2):
        returns[i].wait_recv()
    last[0].wait_recv()
    gain_grad_ref[...] = jnp.zeros_like(gain_grad_ref)

    @pl.loop(0, rows // step)
    def _(r):
        at = pl.ds(pl.multiple_of(r * step, step), step)
        back = sums[0, at, :] + came[0, 0, at, :].astype(F32) + came[2, 0, at, :].astype(F32)
        hat, scale = normed(hid_ref[at, :])
        gain_grad_ref[...] += jnp.sum(back * hat, axis=0, keepdims=True)
        grad_ref[at, :] = douts_ref[at, :].astype(F32) + norm_back(
            back * gain_ref[...], hat, scale
        )

    last[1].wait_recv()

    @pl.loop(0, rows // step)
    def _(r):
        at = pl.ds(pl.multiple_of(r * step, step), step)
        out_ref[at, :] = (
            hid_ref[at, :]
            + sums[1, at, :]
            + came[0, 1, at, :].astype(F32)
            + came[2, 1, at, :].astype(F32)
        ).astype(BF)

    for c in [to_pair, to_other, through] + returns + last:
        c.wait_send()


class PlaneReduce:
    def __init__(self, far, near, came, x_first, send, recv):
        chip, core = lax.axis_index("chip"), lax.axis_index("core")
        x, y, other = {"chip": chip ^ 1}, {"chip": chip ^ 2}, {"core": 1 - core}
        self.near, self.came, self.x_first = near, came, x_first

        def copy(i, src, to):
            return pltpu.make_async_remote_copy(
                src_ref=src,
                dst_ref=came.at[i],
                send_sem=send.at[i],
                recv_sem=recv.at[i],
                device_id=to,
                device_id_type=MESH,
            )

        self.away = (1, 3) if x_first else (2, 3)
        self.stay = (0, 2) if x_first else (0, 1)
        one, two = (x, y) if x_first else (y, x)
        self.cores = 4 if far else 0
        self.copies = [copy(i, far(4 + i), other) for i in range(self.cores)]
        self.copies += [copy(self.cores + i, near.at[self.away[i]], one) for i in range(2)]
        self.copies.append(copy(self.cores + 2, near.at[self.stay[1]], two))

    def start(self):
        for i in (3, self.away[0], self.stay[1], 0):
            self.copies[i].start()

    def add(self, place, i):
        step = 64

        @pl.loop(0, self.near.shape[1] // step)
        def _(r):
            at = pl.ds(pl.multiple_of(r * step, step), step)
            self.near[place, at, :] = (
                self.near[place, at, :].astype(F32) + self.came[i, at, :].astype(F32)
            ).astype(BF)

    def core_sums(self):
        for i in (1, 0):
            p = self.away[i]
            self.copies[p].wait_recv()
            self.add(p, p)
            self.copies[4 + i].start()
        for p in (self.stay[1], self.stay[0]):
            self.copies[p].wait_recv()
            self.add(p, p)

    def start_first(self):
        for i in (1, 0):
            self.copies[self.cores + i].start()

    def first_sums(self, step):
        i = 1 - step
        self.copies[self.cores + i].wait_recv()
        self.add(self.stay[i], self.cores + i)
        if i == 1:
            self.copies[self.cores + 2].start()

    def finish(self, out_ref):
        self.copies[self.cores + 2].wait_recv()
        self.add(self.stay[0], self.cores + 2)
        out_ref[...] = self.near[0]
        for c in self.copies:
            c.wait_send()


def close_rows_kernel(
    xa_ref,
    xb_ref,
    wa_ref,
    wb_ref,
    ga_hbm,
    gb_hbm,
    go_hbm,
    out_ref,
    sum_a_ref,
    sum_b_ref,
    sum_o_ref,
    held,
    came,
    near_a,
    near_b,
    near_o,
    came_a,
    came_b,
    came_o,
    send,
    recv,
    psend,
    precv,
    lsem,
):
    rows = out_ref.shape[0] // 2
    width = out_ref.shape[1] // 8
    greet(plane=True, line=True, cores=True)
    groups = []
    local = []
    for i, (hbm, near, got, x_first) in enumerate(
        ((ga_hbm, near_a, came_a, True), (gb_hbm, near_b, came_b, False), (go_hbm, near_o, came_o, True))
    ):
        groups.append(
            PlaneReduce(
                lambda p, hbm=hbm: hbm.at[p], near, got, x_first, psend.at[i], precv.at[i]
            )
        )
        local.append(pltpu.make_async_copy(hbm.at[pl.ds(0, 4)], near, lsem.at[i]))
    for g in groups:
        g.start()
    for c in local:
        c.start()

    def make(a, to):
        at = pl.ds(pl.multiple_of(a * rows, rows), rows)
        xa = jnp.concatenate([xa_ref[0, at, :], xa_ref[1, at, :]], axis=0)
        xb = jnp.concatenate([xb_ref[0, at, :], xb_ref[1, at, :]], axis=0)

        @pl.loop(0, 8)
        def _(p):
            part = pl.ds(pl.multiple_of(p * width, width), width)
            to[:, chunk_of(p, width)] = (
                dot_nt(xa, wa_ref[part, :]) + dot_nt(xb, wb_ref[part, :])
            ).astype(to.dtype)

    line = LineReduce(make, out_ref, held, came, send, recv)
    line.step(3)
    for c in local:
        c.wait()
    for g in groups:
        g.core_sums()
    line.step(2)
    line.step(1)
    for g in groups:
        g.first_sums(0)
    for g in groups:
        g.first_sums(1)
    line.close()
    for g, out in zip(groups, (sum_a_ref, sum_b_ref, sum_o_ref)):
        g.finish(out)


def sems(*shape):
    return pltpu.SemaphoreType.DMA(shape)


def like(shape, kind):
    return jax.ShapeDtypeStruct(shape, kind)


def call(kernel, number, ins, outs, scratch, flops, *args):
    moved = sum(a.size * a.dtype.itemsize for a in args)
    return pl.pallas_call(
        kernel,
        out_shape=[like(s, t) for s, t, _ in outs],
        in_specs=ins,
        out_specs=[spec for _, _, spec in outs],
        scratch_shapes=scratch,
        compiler_params=pltpu.CompilerParams(
            collective_id=number, has_side_effects=True, vmem_limit_bytes=VMEM_LIMIT
        ),
        cost_estimate=pl.CostEstimate(flops=flops, bytes_accessed=moved, transcendentals=0),
    )(*args)


def project(tokens, gains, first, second, out_weight):
    micro, rows, width = tokens.shape
    count = lax.axis_size("uly")
    high = second.shape[1] - out_weight.shape[0]
    if not is_cube():
        full = lax.all_gather(gains, BLK, axis=1, tiled=True)
        w_first = lax.all_gather(first, BLK, axis=0, tiled=True)
        w_second = lax.all_gather(second, BLK, axis=0, tiled=True)
        w_out = lax.all_gather(out_weight, BLK, axis=1, tiled=True)
        one = (normed(spread(tokens).astype(F32))[0] * full[0].astype(F32)).astype(BF)
        return (
            one,
            dot_nn(one, w_first, BF),
            dot_nn(one, w_second[:, :high], BF),
            dot_nn(one, w_second[:, high:]),
            w_first,
            w_second,
            w_out,
            full,
        )
    wide = count * rows
    piece = width // 8
    padded = jnp.concatenate([gains, jnp.zeros((14, piece), BF)], axis=0)
    na, nb, no = first.shape[1], second.shape[1], out_weight.shape[0]
    out = call(
        project_kernel,
        0,
        [vmem(), vmem(), anywhere(), anywhere(), anywhere()],
        [
            ((micro, wide, width), BF, vmem()),
            ((micro, wide, na), BF, vmem()),
            ((micro, wide, high), BF, vmem()),
            ((micro, wide, nb - high), F32, vmem()),
            ((width, na), BF, anywhere()),
            ((width, nb), BF, anywhere()),
            ((no, width), BF, anywhere()),
            ((8, 16, piece), BF, vmem()),
        ],
        [
            pltpu.VMEM((count, micro * rows, width), BF),
            pltpu.VMEM((width, na), BF),
            pltpu.VMEM((width, nb), BF),
            pltpu.VMEM((8, 16, piece), BF),
            sems(5, 7),
            sems(5, 7),
            sems(2, count - 1),
            sems(2, count - 1),
            sems(5),
        ],
        2 * micro * wide * width * (na + nb),
        tokens.reshape(micro * rows, width),
        padded,
        first,
        second,
        out_weight,
    )
    got = out[7][:, :2]
    me = block_index()
    full = jnp.concatenate(
        [
            lax.dynamic_index_in_dim(got, ((me ^ b) & 1) * 4 + ((me ^ b) >> 1), 0, False)
            for b in range(8)
        ],
        axis=1,
    )
    return (*out[:7], full)


def line_scratch(count, rows, width):
    return [
        pltpu.VMEM((2, count - 1, rows, width), BF),
        pltpu.VMEM((2, count - 1, rows, width), BF),
    ]


def add_rows(mixed, w_out, up, down):
    micro, wide, hidden = mixed.shape
    count = lax.axis_size("uly")
    rows = wide // count
    width = w_out.shape[1]
    units = up.shape[1]
    out = call(
        add_rows_kernel,
        1,
        [vmem(), vmem(), anywhere(), anywhere()],
        [
            ((micro * rows, width), F32, vmem()),
            ((width, units), BF, anywhere()),
            ((units, width), BF, anywhere()),
        ],
        line_scratch(count, micro * rows, width)
        + [sems(2, count - 1)] * 2
        + [sems(2, 3), sems(2, 3), sems(2)],
        2 * micro * wide * hidden * width,
        mixed,
        w_out,
        up,
        down,
    )
    return out


def fan_out(rows_bf, w_out, up_grad, down_grad):
    own, width = rows_bf.shape
    micro, rows = 2, own // 2
    count = lax.axis_size("uly")
    hidden = w_out.shape[0]
    up_shape, down_shape = up_grad.shape[1:], down_grad.shape[1:]
    return call(
        fan_out_kernel,
        2,
        [vmem(), vmem(), anywhere(), anywhere()],
        [
            ((micro, count * rows, width), BF, vmem()),
            ((micro, count * rows, hidden), F32, vmem()),
            (up_shape, BF, vmem()),
            (down_shape, BF, vmem()),
        ],
        [
            pltpu.VMEM((count, own, width), BF),
            pltpu.VMEM((own, width), BF),
            pltpu.VMEM((4, *up_shape), BF),
            pltpu.VMEM((4, *down_shape), BF),
            pltpu.VMEM((3, *up_shape), BF),
            pltpu.VMEM((3, *down_shape), BF),
            sems(2, count - 1),
            sems(2, count - 1),
            sems(2, 3),
            sems(2, 3),
            sems(2),
        ],
        2 * micro * count * rows * hidden * width,
        rows_bf,
        w_out,
        up_grad,
        down_grad,
    )


def feed_all(hidden, douts, gain, ups, downs):
    own, width = hidden.shape
    units = ups.shape[1]
    return call(
        feed_kernel,
        4,
        [vmem()] * 5,
        [
            ((own, width), BF, vmem()),
            ((own, width), F32, vmem()),
            ((1, width), F32, vmem()),
            ((4, width // 4, units), BF, vmem()),
            ((4, units, width // 4), BF, vmem()),
        ],
        [
            pltpu.VMEM((4 * own, width), BF),
            pltpu.VMEM((4 * own, units), BF),
            pltpu.VMEM((4 * own, units), BF),
            pltpu.VMEM((2, own, width), F32),
            pltpu.VMEM((3, 2, own, width), BF),
            pltpu.VMEM((3, 2, own, width), BF),
            sems(9),
            sems(9),
        ],
        2 * 6 * 4 * own * units * width,
        hidden,
        douts,
        gain,
        ups,
        downs,
    )


def to_chips(array):
    if not is_cube():
        return array
    chip = lax.axis_index("chip")
    width = array.shape[-1] // 4
    return jnp.concatenate(
        [
            lax.dynamic_slice_in_dim(array, (chip ^ k) * width, width, array.ndim - 1)
            for k in range(4)
        ],
        axis=-1,
    )


def core_half(array, dim):
    own, other = core_cut(array, dim)
    return core_join(own, swap(other, 1), 1 - dim)


def feed_shards(up_shard, down_shard):
    up, down = core_half(up_shard, 1), core_half(down_shard, 0)
    return (
        jnp.concatenate([up, shift(up, 2)], axis=1),
        jnp.concatenate([down, shift(down, 2)], axis=0),
    )


def feed_gather(rows):
    count = lax.axis_size("uly")
    pair = lax.ppermute(rows, "uly", [(z, z ^ 1) for z in range(count)])
    return jnp.concatenate([rows, swap(rows, 1), pair, swap(pair, 1)], axis=0)


def feed_scatter(up_sum, down_sum):
    def settle(array, dim):
        half = array.shape[dim] // 2
        keep = lax.slice_in_dim(array, 0, half, axis=dim)
        away = lax.slice_in_dim(array, half, 2 * half, axis=dim)
        total = (keep.astype(F32) + shift(away, 2).astype(F32)).astype(BF)
        own, other = core_cut(total, 1 - dim)
        return core_join(own, swap(other, 1), dim).astype(F32)

    return settle(up_sum, 1), settle(down_sum, 0)


def middle(tokens, out_grad, gain_two, mixed, w_out, up_weight, down_weight):
    micro, rows, width = tokens.shape
    own = micro * rows
    if not is_cube():
        hidden = tokens.astype(F32) + collect(
            jnp.stack([dot_nn(mixed[m], w_out) for m in range(micro)])
        )
        pair = feed_weights(up_weight, down_weight)
        hat, scale = normed(hidden)
        two = (hat * gain_two).astype(BF)
        flat_two, flat_out = two.reshape(own, width), out_grad.reshape(own, width)
        two_both = jnp.concatenate([flat_two, swap(flat_two, 1)], axis=0)
        out_both = jnp.concatenate([flat_out, swap(flat_out, 1)], axis=0)
        down_rows, grad_two, up_part, down_part = feed(two_both, out_both, pair)
        grad_two = grad_two[:own] + swap(grad_two[own:].astype(BF), 1).astype(F32)
        down_rows = down_rows[:own] + swap(down_rows[own:].astype(BF), 1).astype(F32)
        up_grad, down_grad = feed_reduce(up_part, down_part)
        block_out = (hidden + down_rows.reshape(micro, rows, width)).astype(BF)
        grad_two = grad_two.reshape(micro, rows, width)
        gain_part = jnp.sum(grad_two * hat, axis=(0, 1))
        grad_hidden = out_grad.astype(F32) + norm_back(grad_two * gain_two, hat, scale)
        wide_att = spread(grad_hidden.astype(BF))
        grad_mixed = jnp.stack([dot_nt(wide_att[m], w_out) for m in range(micro)])
        return block_out, up_grad, down_grad, gain_part, grad_hidden, wide_att, grad_mixed
    up, down = feed_shards(up_weight, down_weight)
    douts = feed_gather(to_chips(out_grad).reshape(own, width))
    rows_sum, ups, downs = add_rows(mixed, w_out, up, down)
    hidden = to_chips(tokens).reshape(own, width).astype(F32) + rows_sum
    block_out, grad_hidden, gain_part, up_part, down_part = feed_all(
        hidden, douts, to_chips(gain_two[None]), ups, downs
    )
    wide_att, grad_mixed, up_sum, down_sum = fan_out(
        grad_hidden.astype(BF), w_out, up_part, down_part
    )
    up_grad, down_grad = feed_scatter(up_sum, down_sum)
    return (
        to_chips(block_out).reshape(micro, rows, width),
        up_grad,
        down_grad,
        to_chips(gain_part)[0],
        to_chips(grad_hidden).reshape(micro, rows, width),
        wide_att,
        grad_mixed,
    )


def close_rows(xa, xb, w_first, w_second, ga, gb, out_grad):
    micro, wide, na = xa.shape
    nb = xb.shape[2]
    width = w_first.shape[0]
    if not is_cube():
        partial = jnp.stack(
            [dot_nt(xa[m], w_first) + dot_nt(xb[m], w_second) for m in range(micro)]
        )
        return (
            collect(partial),
            lax.psum_scatter(ga, BLK, scatter_dimension=0, tiled=True),
            lax.psum_scatter(gb, BLK, scatter_dimension=0, tiled=True),
            lax.psum_scatter(out_grad, BLK, scatter_dimension=1, tiled=True),
        )
    count = lax.axis_size("uly")
    rows = wide // count
    piece = width // 8
    no = out_grad.shape[0]
    core = lax.axis_index("core")
    pieces_o = jnp.stack(
        [
            lax.dynamic_slice_in_dim(out_grad, (2 * k + (core ^ j)) * piece, piece, 1)
            for j in range(2)
            for k in range(4)
        ]
    )
    out = call(
        close_rows_kernel,
        3,
        [vmem()] * 4 + [anywhere()] * 3,
        [
            ((micro * rows, width), F32, vmem()),
            ((piece, na), BF, vmem()),
            ((piece, nb), BF, vmem()),
            ((no, piece), BF, vmem()),
        ],
        line_scratch(count, micro * rows, width)
        + [
            pltpu.VMEM((4, piece, na), BF),
            pltpu.VMEM((4, piece, nb), BF),
            pltpu.VMEM((4, no, piece), BF),
            pltpu.VMEM((7, piece, na), BF),
            pltpu.VMEM((7, piece, nb), BF),
            pltpu.VMEM((7, no, piece), BF),
            sems(2, count - 1),
            sems(2, count - 1),
            sems(3, 7),
            sems(3, 7),
            sems(3),
        ],
        2 * micro * wide * width * (na + nb),
        xa,
        xb,
        w_first,
        w_second,
        ga.reshape(8, piece, na),
        gb.reshape(8, piece, nb),
        pieces_o,
    )
    return out[0].reshape(micro, rows, width), out[1], out[2], out[3]


def feed(norm_two, out_rows, pair):
    chips, count, _, rows, hidden = pair.shape
    up = pair[:, :, 0].transpose(0, 2, 1, 3).reshape(chips * rows, count * hidden)
    down_t = pair[:, :, 1].transpose(0, 2, 1, 3).reshape(chips * rows, count * hidden)
    upward = dot_nn(norm_two, up)
    act, slope = gelu_pair(upward)
    act = act.astype(BF)
    grad_act = dot_nn(out_rows, down_t)
    grad_up = (grad_act * slope).astype(BF)

    def by_owner(grad):
        return grad.reshape(chips, rows, count, hidden).transpose(0, 2, 1, 3)

    return (
        dot_nt(act, down_t),
        dot_nt(grad_up, up),
        by_owner(dot_tn(norm_two, grad_up, BF)),
        by_owner(dot_tn(out_rows, act, BF)),
    )


def body(
    tokens,
    retain_gain,
    query_weight,
    key_weight,
    value_weight,
    gate_matrix,
    output_weight,
    feed_gain,
    up_weight,
    down_weight,
    decay_rate,
    lengths,
    out_grad,
):
    micro, rows, width = tokens.shape
    heads_here = decay_rate.shape[0] // lax.axis_size("uly")
    rates = lax.dynamic_slice_in_dim(decay_rate, lax.axis_index("uly") * heads_here, heads_here)
    qk = query_weight.shape[1]
    hd = qk // heads_here
    vd = value_weight.shape[1] // heads_here
    cut_v = value_weight.shape[1] // 2

    first = jnp.concatenate([query_weight, key_weight, value_weight[:, :cut_v]], axis=1)
    second = jnp.concatenate([value_weight[:, cut_v:], gate_matrix], axis=1)
    one, a, v_high, gate, w_first, w_second, w_out, gains = project(
        tokens, jnp.stack([retain_gain, feed_gain]), first, second, output_weight
    )
    gain_one, gain_two = gains[0].astype(F32), gains[1].astype(F32)
    length = one.shape[1]

    sets, parts, states = [], [], []
    for m in range(micro):
        values = jnp.concatenate([a[m, :, 2 * qk :], v_high[m]], axis=1)
        heads = [
            (
                a[m, :, h * hd : (h + 1) * hd],
                a[m, :, qk + h * hd : qk + (h + 1) * hd],
                values[:, h * vd : (h + 1) * vd],
            )
            for h in range(heads_here)
        ]
        part = decay_parts(rates, lengths[m], length)
        states.append(retention_state(heads, part[2]))
        sets.append(heads)
        parts.append(part)

    all_states = exchange(states)
    state_in, retained, mixed = [], [], []
    for m in range(micro):
        state = state_sum(parts[m][3], all_states[m])
        kept = retention(sets[m], parts[m], state)
        state_in.append(state)
        retained.append(kept)
        mixed.append(mix(gate[m], kept))
    mixed = jnp.stack(mixed)

    block_out, up_grad, down_grad, gain_two_part, grad_hidden, wide_att, grad_mixed = middle(
        tokens, out_grad, gain_two, mixed, w_out, up_weight, down_weight
    )

    grad_gates, grad_rets, grad_states = [], [], []
    for m in range(micro):
        gg, gr = mix_back(gate[m], retained[m], grad_mixed[m])
        grad_gates.append(gg)
        grad_rets.append(gr)
        grad_states.append(
            jnp.stack(
                [
                    dot_tn((q.astype(F32) * parts[m][1][h]).astype(BF), gr[h], BF)
                    for h, (q, k, v) in enumerate(sets[m])
                ]
            )
        )
    all_back = exchange(grad_states)

    def flat(array):
        return array.reshape(micro * length, array.shape[-1])

    out_part = dot_tn(flat(mixed), flat(wide_att), BF)

    xa, xb = [], []
    for m in range(micro):
        back = state_sum(parts[m][4], all_back[m])
        grads = retention_back(sets[m], parts[m], state_in[m], grad_rets[m], back)
        gq = jnp.concatenate([g[0] for g in grads], axis=1)
        gk = jnp.concatenate([g[1] for g in grads], axis=1)
        gv = jnp.concatenate([g[2] for g in grads], axis=1)
        xa.append(jnp.concatenate([gq, gk, gv[:, :cut_v]], axis=1))
        xb.append(jnp.concatenate([gv[:, cut_v:], grad_gates[m]], axis=1))
    xa, xb = jnp.stack(xa), jnp.stack(xb)
    grad_one, first_sum, second_sum, out_sum = close_rows(
        xa,
        xb,
        w_first,
        w_second,
        dot_tn(flat(one), flat(xa), BF),
        dot_tn(flat(one), flat(xb), BF),
        out_part,
    )
    hat, scale = normed(tokens.astype(F32))
    input_grad = grad_hidden + norm_back(grad_one * gain_one, hat, scale)
    gain_one_part = jnp.sum(grad_one * hat, axis=(0, 1))

    total = lax.psum_scatter(
        jnp.stack([gain_one_part, gain_two_part]), BLK, scatter_dimension=1, tiled=True
    )
    total = lax.psum(total, "uly")
    first_sum, second_sum = first_sum.astype(F32), second_sum.astype(F32)
    return (
        block_out,
        input_grad,
        total[0],
        first_sum[:, :qk],
        first_sum[:, qk : 2 * qk],
        jnp.concatenate([first_sum[:, 2 * qk :], second_sum[:, :cut_v]], axis=1),
        second_sum[:, cut_v:],
        out_sum.astype(F32),
        total[1],
        up_grad,
        down_grad,
    )


def solution(mesh):
    blocks, count = mesh.devices.shape
    split = Mesh(mesh.devices.reshape(blocks // 2, 2, count), AXES)
    rows = P(None, AXES, None)
    gain, wide, tall = P(BLK), P(BLK, "uly"), P("uly", BLK)
    return jax.shard_map(
        body,
        mesh=split,
        in_specs=(rows, gain, wide, wide, wide, wide, tall, gain, wide, tall, P(), P(), rows),
        out_specs=(rows, rows, gain, wide, wide, wide, wide, tall, gain, wide, tall),
        check_vma=False,
    )
```

time: 1330 us -> 877 us (0.66)
  waiting for transfers between devices: 717 us -> 155 us
  Pallas kernels: 0 us -> 497 us
  starting transfers between devices: 215 us -> 19.2 us
  matrix products: 199 us -> 64.8 us
  local copies, waits for them, and re-layouts: 118 us -> 44.9 us
    pallas_call x0 -> x5, Pallas kernels: none -> 497 us  [call(): pl.pallas_call(kernel, out_shape=[like(s, t) for s, t, _ in outs], in_spe...]
    ppermute x146 -> x35, waiting for transfers between devices: 377 us -> 55.6 us  [the longest x12 48.3 us: swap(): lax.ppermute(array, 'chip', [(b, b ^ mask // 2) for b in range(count)])]
    ppermute x39 -> x4, waiting for transfers between devices: 340 us -> 66.9 us  [shift(): lax.ppermute(array, 'uly', [(z, (z + step) % count) for z in range(count)])]
    ppermute x39 -> x4, starting transfers between devices: 101 us -> 2.93 us  [shift(): lax.ppermute(array, 'uly', [(z, (z + step) % count) for z in range(count)])]
    ppermute x146 -> x35, starting transfers between devices: 114 us -> 16.2 us  [the longest x12 11.2 us: swap(): lax.ppermute(array, 'chip', [(b, b ^ mask // 2) for b in range(count)])]
    dot_general x24 -> x16, matrix products: 75.2 us -> 6.64 us  [dot_nt(): lax.dot_general(left, right, (((1,), (1,)), ((), ())), preferred_element_...]
    unnamed x605 -> x164, local copies, waits for them, and re-layouts: 75 us -> 17.8 us
    dot_general x26 -> x16, matrix products: 53.8 us -> 6.24 us  [dot_nn(): return jnp.dot(left, right, preferred_element_type=F32).astype(kind)]
  transfers between devices with their start and end apart: 185 -> 40, of which waited for: 77 -> 13; matrix products, arithmetic and copies ran while one was open for 19% -> 11% of each run, Pallas kernels for 0% -> 12%
where the time goes in v2:
time: 877 us; the launch traced here: 871 us
  Pallas kernels  497 us (57%)
  waiting for transfers between devices  155 us (18%)
  matrix products  64.8 us (7%)
  other arithmetic  61.9 us (7%)
  local copies, waits for them, and re-layouts  44.9 us (5%)
  starting transfers between devices  19.2 us (2%)
  between operations  16.1 us (2%)
  blocking collectives  11.7 us (1%)
    pallas_call x5, Pallas kernels, call(): pl.pallas_call(kernel, out_shape=[like(s, t) for s, t, _ in outs], in_spe...  497 us
    ppermute x4, waiting for transfers between devices, shift(): lax.ppermute(array, 'uly', [(z, (z + step) % count) for z in range(count)])  66.9 us
    ppermute x12, waiting for transfers between devices, swap(): lax.ppermute(array, 'chip', [(b, b ^ mask // 2) for b in range(count)])  48.3 us
    dot_general x19, matrix products, dot_tn(): lax.dot_general(left, right, (((0,), (0,)), ((), ())), preferred_element_...  40.9 us
    unnamed x2, waiting for transfers between devices  32.6 us
    unnamed x164, local copies, waits for them, and re-layouts  17.8 us
  transfers between devices with their start and end apart: 40, of which 13 were waited for; matrix products, arithmetic and copies ran while one was open for 11% of the time, Pallas kernels for 12%

profile of v2, /device:TPU:0, one launch (start us, length us, event | category | flops | bytes accessed | tf_op | source)
XLA Modules:
  0.0 870.9 jit_solution(3175399651926093772)
XLA Ops:
  19.8 119.9 %shard_map.230 = (bf16[2,512,2048]{2,1,0:T(8,128)(2,1)}, bf16[2,512,1536]{2,1,0:T(8,128)(2,1)}, bf16[2,512,512]{2,1,0:T(8,128)(2,1)}, f32[2,512,1024]{2,1,0:T(8,...) custom-call(bf16[256,2048]{1,0:T(8,128)(2,1)} %bitcast.448, ...), custom_call_target="tpu_custom_call" | custom-call | flops 12884901888 | bytes 3153920 | tf_op jit(solution)/shard_map/pallas_call | solution.py:1083
  158.7 4.9 slice_bitcast_fusion.3
  173.2 2.5 compare_and_fusion.1
  186.8 6.1 collective-permute-done.7
  196.0 25.4 %collective-permute-done.15 = bf16[512,512]{1,0:T(8,128)(2,1)S(1)} collective-permute-done((bf16[512,512]{1,0:T(8,128)(2,1)S(1)}, bf16[512,512]{1,0:T(8,128)(2,1)S(1)}, u32[]{:S(2)}, u32[]{:S(2)}) %collective-permute-start.15) | collective-permute-done | bytes 524320 | tf_op jit(solution)/shard_map/ppermute | solution.py:53
  222.4 10.2 %collective-permute-done.17 = bf16[512,512]{1,0:T(8,128)(2,1)S(1)} collective-permute-done((bf16[512,512]{1,0:T(8,128)(2,1)S(1)}, bf16[512,512]{1,0:T(8,128)(2,1)S(1)}, u32[]{:S(2)}, u32[]{:S(2)}) %collective-permute-start.17) | collective-permute-done | bytes 524320 | tf_op jit(solution)/shard_map/ppermute | solution.py:53
  237.3 10.8 %collective-permute-done.9 = bf16[1,2,256,512]{3,2,1,0:T(8,128)(2,1)S(1)} collective-permute-done((bf16[1,2,256,512]{3,2,1,0:T(8,128)(2,1)S(1)}, bf16[1,2,256,512]{3,2,1,0:T(8,128)(2,1)S(1)}, u32[]{:S(2)}, u32[]{:S(2)}) %collective-permute-start.9) | collective-permute-done | bytes 524320 | tf_op jit(solution)/shard_map/ppermute | solution.py:48
  248.9 6.2 collective-permute-done.19
  255.3 2.8 fusion.6
  261.1 2.8 fusion.4
  270.8 105.6 %shard_map.231 = (f32[256,2048]{1,0:T(8,128)}, bf16[2048,1024]{1,0:T(8,128)(2,1)}, bf16[1024,2048]{1,0:T(8,128)(2,1)}) custom-call(bf16[2,512,1024]{2,1,0:T(8,128)(2,1)} %pad_maximum_fusion.3.x_ref, bf16[1024,2048]{1,0:T(8,128)(2,1)} %get-tuple-element.38.w_ref, bf16[512,1024]{1,0:T(8,128)(2,1)} %pad_maximum_fusion.6.up_hbm, ...), custom_call_target="tpu_custom_call" | custom-call | flops 4294967296 | bytes 8388608 | tf_op jit(solution)/shard_map/pallas_call | solution.py:1083
  376.4 3.5 convert_add_fusion.hid_ref
  379.9 3.9 pad_maximum_fusion.douts_ref
  383.9 98.5 %shard_map.232 = (bf16[256,2048]{1,0:T(8,128)(2,1)}, f32[256,2048]{1,0:T(8,128)}, f32[1,2048]{1,0:T(1,128)}, bf16[4,512,1024]{2,1,0:T(8,128)(2,1)}, bf16[4,1024,512]{2,1,0:T(8,128)(2,1)}) custom-call(f32[256,2048]{1,0:T(8,128)} %convert_add_fusion.hid_ref, bf16[1024,2048]{1,0:T(8,128)(2,1)} %pad_maximum_fusion.douts_ref, ...), custom_call_target="tpu_custom_call" | custom-call | flops 25769803776 | bytes 14688256 | tf_op jit(solution)/shard_map/pallas_call | solution.py:1083
  482.4 2.7 convert_element_type.415.rows_ref
  485.1 81.8 %shard_map.233 = (bf16[2,512,2048]{2,1,0:T(8,128)(2,1)}, f32[2,512,1024]{2,1,0:T(8,128)}, bf16[512,1024]{1,0:T(8,128)(2,1)}, bf16[1024,512]{1,0:T(8,128)(2,1)}) custom-call(bf16[256,2048]{1,0:T(8,128)(2,1)} %convert_element_type.415.rows_ref, bf16[1024,2048]{1,0:T(8,128)(2,1)} %get-tuple-element.38.w_ref, bf16[4,512,1024]{2,1,0:T(8,128)(2,1)} %get-tuple-element.45.up_hbm, ...), custom_call_target="tpu_custom_call" | custom-call | flops 4294967296 | bytes 13631488 | tf_op jit(solution)/shard_map/pallas_call | solution.py:1083
  567.0 2.7 slice_bitcast_fusion.1
  589.4 2.9 collective-permute-start.35
  592.3 7.5 bitcast_convert_fusion.2
  605.5 20.9 %collective-permute-done.37 = bf16[512,512]{1,0:T(8,128)(2,1)S(1)} collective-permute-done((bf16[512,512]{1,0:T(8,128)(2,1)}, bf16[512,512]{1,0:T(8,128)(2,1)S(1)}, u32[]{:S(2)}, u32[]{:S(2)}) %collective-permute-start.37) | collective-permute-done | bytes 524320 | tf_op jit(solution)/shard_map/ppermute | solution.py:53
  627.1 10.5 %collective-permute-done.35 = bf16[512,512]{1,0:T(8,128)(2,1)S(1)} collective-permute-done((bf16[512,512]{1,0:T(8,128)(2,1)}, bf16[512,512]{1,0:T(8,128)(2,1)S(1)}, u32[]{:S(2)}, u32[]{:S(2)}) %collective-permute-start.35) | collective-permute-done | bytes 524320 | tf_op jit(solution)/shard_map/ppermute | solution.py:53
  641.1 10.3 %collective-permute-done.29 = bf16[1,2,256,512]{3,2,1,0:T(8,128)(2,1)S(1)} collective-permute-done((bf16[1,2,256,512]{3,2,1,0:T(8,128)(2,1)S(1)}, bf16[1,2,256,512]{3,2,1,0:T(8,128)(2,1)S(1)}, u32[]{:S(2)}, u32[]{:S(2)}) %collective-permute-start.29) | collective-permute-done | bytes 524320 | tf_op jit(solution)/shard_map/ppermute | solution.py:48
  655.0 9.8 %collective-permute-done.23 = bf16[1,2,256,512]{3,2,1,0:T(8,128)(2,1)S(1)} collective-permute-done((bf16[1,2,256,512]{3,2,1,0:T(8,128)(2,1)}, bf16[1,2,256,512]{3,2,1,0:T(8,128)(2,1)S(1)}, u32[]{:S(2)}, u32[]{:S(2)}) %collective-permute-start.23) | collective-permute-done | bytes 524320 | tf_op jit(solution)/shard_map/ppermute | solution.py:48
  667.1 9.8 %collective-permute-done.30 = bf16[1,2,256,512]{3,2,1,0:T(8,128)(2,1)S(1)} collective-permute-done((bf16[1,2,256,512]{3,2,1,0:T(8,128)(2,1)S(1)}, bf16[1,2,256,512]{3,2,1,0:T(8,128)(2,1)S(1)}, u32[]{:S(2)}, u32[]{:S(2)}) %collective-permute-start.30) | collective-permute-done | bytes 524320 | tf_op jit(solution)/shard_map/ppermute | solution.py:48
  678.8 2.8 fusion.2
  682.4 2.8 fusion
  690.9 9.1 %bitcast_convert_fusion = bf16[2048,1536]{1,0:T(8,128)(2,1)} fusion(bf16[2,512,2048]{2,1,0:T(8,128)(2,1)S(1)} %copy-done.61, bf16[1,512,1536]{2,1,0:T(8,128)(2,1)S(1)} %maximum_bitcast_fusion.1, bf16[1,512,1536]{2,1,0:T(8,128)(2,1)S(1)} %maximum_bitcast_fusion), kind=kOutput, calls=%fused_computation.4 | convolution fusion | flops 6447169536 | bytes 13631488 | tf_op jit(solution)/shard_map/dot_general | solution.py:25
  702.6 9.2 %bitcast_convert_fusion.1 = bf16[2048,1536]{1,0:T(8,128)(2,1)} fusion(bf16[2,512,2048]{2,1,0:T(8,128)(2,1)S(1)} %copy-done.61, bf16[1,512,1536]{2,1,0:T(8,128)(2,1)S(1)} %bitcast.463, bf16[1,512,1536]{2,1,0:T(8,128)(2,1)S(1)} %bitcast.465), kind=kOutput, calls=%fused_computation.5 | convolution fusion | flops 6447169536 | bytes 13631488 | tf_op jit(solution)/shard_map/dot_general | solution.py:25
  713.8 91.4 %shard_map.234 = (f32[256,2048]{1,0:T(8,128)}, bf16[256,1536]{1,0:T(8,128)(2,1)}, bf16[256,1536]{1,0:T(8,128)(2,1)}, bf16[1024,256]{1,0:T(8,128)(2,1)}) custom-call(bf16[2,512,1536]{2,1,0:T(8,128)(2,1)} %pad_maximum_fusion.1.xa_ref, bf16[2,512,1536]{2,1,0:T(8,128)(2,1)} %pad_maximum_fusion.2.xb_ref, bf16[2048,1536]{1,0:T(8,128)(2,1)} %get-tuple-element.48.wa_ref, ...), custom_call_target="tpu_custom_call" | custom-call | flops 12884901888 | bytes 35651584 | tf_op jit(solution)/shard_map/pallas_call | solution.py:1083
  811.0 3.8 fusion.16
  818.0 32.6 %reduce-scatter.4.cloned.1.call-done = f32[256,2]{1,0:T(8,128)} async-done(((f32[2048,2]{1,0:T(8,128)}), f32[256,2]{1,0:T(8,128)}) %reduce-scatter.4.cloned.1.call-update) | async-done | bytes 2064
  851.5 11.7 %psum.7 = f32[2,256]{1,0:T(2,128)S(1)} all-reduce(f32[2,256]{1,0:T(2,128)S(1)} %copy.214), channel_id=1, replica_groups=mesh['chip'=4,'core'=2,'uly'=4] {'uly'}, use_global_device_ids=true, to_apply=%region_30.31 | all-reduce | flops 512 | bytes 4096 | tf_op jit(solution)/shard_map/psum | solution.py:1549
  (419 shorter events, 129.6 us)
Async XLA Ops:
  7.2 843.4 %reduce-scatter.4.cloned.1.call-start = ((), (), s32[]{:S(2)}) async-start(), calls=%async_computation.1 | async-start | bytes 1179648
  143.8 39.2 %collective-permute-start = (bf16[1,2,256,512]{3,2,1,0:T(8,128)(2,1)}, bf16[1,2,256,512]{3,2,1,0:T(8,128)(2,1)}, u32[]{:S(2)}, u32[]{:S(2)}) collective-permute-start(bf16[1,2,256,512]{3,2,1,0:T(8,128)(2,1)} %fusion.89), channel_id=1, source_target_pairs={{0,8},{8,0},{16,24},{24,16},{1,9},{9,1},{17,25},{25,17},{2,10},{10... | collective-permute-start | bytes 1572872 | tf_op jit(solution)/shard_map/ppermute | solution.py:48
  145.2 39.7 %collective-permute-start.1 = (bf16[1,2,256,512]{3,2,1,0:T(8,128)(2,1)}, bf16[1,2,256,512]{3,2,1,0:T(8,128)(2,1)}, u32[]{:S(2)}, u32[]{:S(2)}) collective-permute-start(bf16[1,2,256,512]{3,2,1,0:T(8,128)(2,1)} %fusion.89), channel_id=1, source_target_pairs={{0,16},{8,24},{16,0},{24,8},{1,17},{9,25},{17,1},{25,9},{2,18},{10... | collective-permute-start | bytes 1572872 | tf_op jit(solution)/shard_map/ppermute | solution.py:48
  145.8 88.5 %collective-permute-start.3 = (bf16[1,2,256,512]{3,2,1,0:T(8,128)(2,1)}, bf16[1,2,256,512]{3,2,1,0:T(8,128)(2,1)}, u32[]{:S(2)}, u32[]{:S(2)}) collective-permute-start(bf16[1,2,256,512]{3,2,1,0:T(8,128)(2,1)} %fusion.89), channel_id=1, source_target_pairs={{0,4},{4,0},{1,5},{5,1},{2,6},{6,2},{3,7},{7,3},{8,12},{12,8},{9,1... | collective-permute-start | bytes 1572872 | tf_op jit(solution)/shard_map/ppermute | solution.py:46
  146.5 31.8 %collective-permute-start.14 = (bf16[256,512]{1,0:T(8,128)(2,1)}, bf16[256,512]{1,0:T(8,128)(2,1)}, u32[]{:S(2)}, u32[]{:S(2)}) collective-permute-start(bf16[256,512]{1,0:T(8,128)(2,1)} %constant_dynamic-slice_fusion.31), channel_id=1, source_target_pairs={{0,4},{4,0},{1,5},{5,1},{2,6},{6,2},{3,7},{7,3},{8,12},{12,8},{9,1... | collective-permute-start | bytes 786440 | tf_op jit(solution)/shard_map/ppermute | solution.py:46
  147.7 32.5 %collective-permute-start.16 = (bf16[512,256]{1,0:T(8,128)(2,1)}, bf16[512,256]{1,0:T(8,128)(2,1)}, u32[]{:S(2)}, u32[]{:S(2)}) collective-permute-start(bf16[512,256]{1,0:T(8,128)(2,1)} %constant_dynamic-slice_fusion.30), channel_id=1, source_target_pairs={{0,4},{4,0},{1,5},{5,1},{2,6},{6,2},{3,7},{7,3},{8,12},{12,8},{9,1... | collective-permute-start | bytes 786440 | tf_op jit(solution)/shard_map/ppermute | solution.py:46
  178.3 14.6 %collective-permute-start.7 = (bf16[1,2,256,512]{3,2,1,0:T(8,128)(2,1)}, bf16[1,2,256,512]{3,2,1,0:T(8,128)(2,1)S(1)}, u32[]{:S(2)}, u32[]{:S(2)}) collective-permute-start(bf16[1,2,256,512]{3,2,1,0:T(8,128)(2,1)} %fusion.88), channel_id=1, source_target_pairs={{0,8},{8,0},{16,24},{24,16},{1,9},{9,1},{17,25},{25,17},{2,10},{10... | collective-permute-start | bytes 1572872 | tf_op jit(solution)/shard_map/ppermute | solution.py:48
  180.2 14.2 %collective-permute-start.8 = (bf16[1,2,256,512]{3,2,1,0:T(8,128)(2,1)}, bf16[1,2,256,512]{3,2,1,0:T(8,128)(2,1)S(1)}, u32[]{:S(2)}, u32[]{:S(2)}) collective-permute-start(bf16[1,2,256,512]{3,2,1,0:T(8,128)(2,1)} %fusion.88), channel_id=1, source_target_pairs={{0,16},{8,24},{16,0},{24,8},{1,17},{9,25},{17,1},{25,9},{2,18},{10... | collective-permute-start | bytes 1572872 | tf_op jit(solution)/shard_map/ppermute | solution.py:48
  182.9 65.2 %collective-permute-start.10 = (bf16[1,2,256,512]{3,2,1,0:T(8,128)(2,1)}, bf16[1,2,256,512]{3,2,1,0:T(8,128)(2,1)S(1)}, u32[]{:S(2)}, u32[]{:S(2)}) collective-permute-start(bf16[1,2,256,512]{3,2,1,0:T(8,128)(2,1)} %fusion.88), channel_id=1, source_target_pairs={{0,4},{4,0},{1,5},{5,1},{2,6},{6,2},{3,7},{7,3},{8,12},{12,8},{9,1... | collective-permute-start | bytes 1572872 | tf_op jit(solution)/shard_map/ppermute | solution.py:46
  184.9 36.4 %collective-permute-start.15 = (bf16[512,512]{1,0:T(8,128)(2,1)S(1)}, bf16[512,512]{1,0:T(8,128)(2,1)S(1)}, u32[]{:S(2)}, u32[]{:S(2)}) collective-permute-start(bf16[512,512]{1,0:T(8,128)(2,1)S(1)} %pad_maximum_fusion.15), channel_id=1, source_target_pairs={{0,2},{1,3},{2,0},{3,1},{4,6},{5,7},{6,4},{7,5},{8,10},{9,11},{10,... | collective-permute-start | bytes 1572872 | tf_op jit(solution)/shard_map/ppermute | solution.py:53
  192.9 39.8 %collective-permute-start.17 = (bf16[512,512]{1,0:T(8,128)(2,1)S(1)}, bf16[512,512]{1,0:T(8,128)(2,1)S(1)}, u32[]{:S(2)}, u32[]{:S(2)}) collective-permute-start(bf16[512,512]{1,0:T(8,128)(2,1)S(1)} %pad_maximum_fusion.16), channel_id=1, source_target_pairs={{0,2},{1,3},{2,0},{3,1},{4,6},{5,7},{6,4},{7,5},{8,10},{9,11},{10,... | collective-permute-start | bytes 1572872 | tf_op jit(solution)/shard_map/ppermute | solution.py:53
  194.4 39.3 %collective-permute-start.2 = (bf16[1,2,256,512]{3,2,1,0:T(8,128)(2,1)}, bf16[1,2,256,512]{3,2,1,0:T(8,128)(2,1)S(1)}, u32[]{:S(2)}, u32[]{:S(2)}) collective-permute-start(bf16[1,2,256,512]{3,2,1,0:T(8,128)(2,1)} %collective-permute-done), channel_id=1, source_target_pairs={{0,16},{8,24},{16,0},{24,8},{1,17},{9,25},{17,1},{25,9},{2,18},{10... | collective-permute-start | bytes 1572872 | tf_op jit(solution)/shard_map/ppermute | solution.py:48
  221.3 33.8 %collective-permute-start.19 = (bf16[256,2048]{1,0:T(8,128)(2,1)}, bf16[256,2048]{1,0:T(8,128)(2,1)}, u32[]{:S(2)}, u32[]{:S(2)}) collective-permute-start(bf16[256,2048]{1,0:T(8,128)(2,1)} %bitcast.72), channel_id=1, source_target_pairs={{0,1},{1,0},{2,3},{3,2},{4,5},{5,4},{6,7},{7,6},{8,9},{9,8},{10,11... | collective-permute-start | bytes 3145736 | tf_op jit(solution)/shard_map/ppermute | solution.py:1297
  234.2 13.9 %collective-permute-start.9 = (bf16[1,2,256,512]{3,2,1,0:T(8,128)(2,1)S(1)}, bf16[1,2,256,512]{3,2,1,0:T(8,128)(2,1)S(1)}, u32[]{:S(2)}, u32[]{:S(2)}) collective-permute-start(bf16[1,2,256,512]{3,2,1,0:T(8,128)(2,1)S(1)} %collective-permute-done.8), channel_id=1, source_target_pairs={{0,8},{8,0},{16,24},{24,16},{1,9},{9,1},{17,25},{25,17},{2,10},{10... | collective-permute-start | bytes 1572872 | tf_op jit(solution)/shard_map/ppermute | solution.py:48
  236.6 143.3 %collective-permute-start.18 = (bf16[256,2048]{1,0:T(8,128)(2,1)}, bf16[256,2048]{1,0:T(8,128)(2,1)}, u32[]{:S(2)}, u32[]{:S(2)}) collective-permute-start(bf16[256,2048]{1,0:T(8,128)(2,1)} %bitcast.72), channel_id=1, source_target_pairs={{0,4},{4,0},{1,5},{5,1},{2,6},{6,2},{3,7},{7,3},{8,12},{12,8},{9,1... | collective-permute-start | bytes 3145736 | tf_op jit(solution)/shard_map/ppermute | solution.py:46
  236.7 12.1 %collective-permute-start.11 = (bf16[1,2,256,512]{3,2,1,0:T(8,128)(2,1)S(1)}, bf16[1,2,256,512]{3,2,1,0:T(8,128)(2,1)S(1)}, u32[]{:S(2)}, u32[]{:S(2)}) collective-permute-start(bf16[1,2,256,512]{3,2,1,0:T(8,128)(2,1)S(1)} %collective-permute-done.7), channel_id=1, source_target_pairs={{0,4},{4,0},{1,5},{5,1},{2,6},{6,2},{3,7},{7,3},{8,12},{12,8},{9,1... | collective-permute-start | bytes 1572872 | tf_op jit(solution)/shard_map/ppermute | solution.py:46
  248.8 12.2 %collective-permute-start.13 = (bf16[1,2,256,512]{3,2,1,0:T(8,128)(2,1)S(1)}, bf16[1,2,256,512]{3,2,1,0:T(8,128)(2,1)S(1)}, u32[]{:S(2)}, u32[]{:S(2)}) collective-permute-start(bf16[1,2,256,512]{3,2,1,0:T(8,128)(2,1)S(1)} %collective-permute-done.9), channel_id=1, source_target_pairs={{0,4},{4,0},{1,5},{5,1},{2,6},{6,2},{3,7},{7,3},{8,12},{12,8},{9,1... | collective-permute-start | bytes 1572872 | tf_op jit(solution)/shard_map/ppermute | solution.py:46
  255.1 124.8 %collective-permute-start.20 = (bf16[256,2048]{1,0:T(8,128)(2,1)}, bf16[256,2048]{1,0:T(8,128)(2,1)}, u32[]{:S(2)}, u32[]{:S(2)}) collective-permute-start(bf16[256,2048]{1,0:T(8,128)(2,1)} %collective-permute-done.19), channel_id=1, source_target_pairs={{0,4},{4,0},{1,5},{5,1},{2,6},{6,2},{3,7},{7,3},{8,12},{12,8},{9,1... | collective-permute-start | bytes 3145736 | tf_op jit(solution)/shard_map/ppermute | solution.py:46
  574.4 63.7 %collective-permute-start.21 = (bf16[1,2,256,512]{3,2,1,0:T(8,128)(2,1)}, bf16[1,2,256,512]{3,2,1,0:T(8,128)(2,1)}, u32[]{:S(2)}, u32[]{:S(2)}) collective-permute-start(bf16[1,2,256,512]{3,2,1,0:T(8,128)(2,1)} %fusion.87), channel_id=1, source_target_pairs={{0,8},{8,0},{16,24},{24,16},{1,9},{9,1},{17,25},{25,17},{2,10},{10... | collective-permute-start | bytes 1572872 | tf_op jit(solution)/shard_map/ppermute | solution.py:48
  575.9 63.5 %collective-permute-start.22 = (bf16[1,2,256,512]{3,2,1,0:T(8,128)(2,1)}, bf16[1,2,256,512]{3,2,1,0:T(8,128)(2,1)}, u32[]{:S(2)}, u32[]{:S(2)}) collective-permute-start(bf16[1,2,256,512]{3,2,1,0:T(8,128)(2,1)} %fusion.87), channel_id=1, source_target_pairs={{0,16},{8,24},{16,0},{24,8},{1,17},{9,25},{17,1},{25,9},{2,18},{10... | collective-permute-start | bytes 1572872 | tf_op jit(solution)/shard_map/ppermute | solution.py:48
  576.9 88.4 %collective-permute-start.24 = (bf16[1,2,256,512]{3,2,1,0:T(8,128)(2,1)}, bf16[1,2,256,512]{3,2,1,0:T(8,128)(2,1)}, u32[]{:S(2)}, u32[]{:S(2)}) collective-permute-start(bf16[1,2,256,512]{3,2,1,0:T(8,128)(2,1)} %fusion.87), channel_id=1, source_target_pairs={{0,4},{4,0},{1,5},{5,1},{2,6},{6,2},{3,7},{7,3},{8,12},{12,8},{9,1... | collective-permute-start | bytes 1572872 | tf_op jit(solution)/shard_map/ppermute | solution.py:46
  588.6 37.8 %collective-permute-start.37 = (bf16[512,512]{1,0:T(8,128)(2,1)}, bf16[512,512]{1,0:T(8,128)(2,1)S(1)}, u32[]{:S(2)}, u32[]{:S(2)}) collective-permute-start(bf16[512,512]{1,0:T(8,128)(2,1)} %slice.313), channel_id=1, source_target_pairs={{0,2},{1,3},{2,0},{3,1},{4,6},{5,7},{6,4},{7,5},{8,10},{9,11},{10,... | collective-permute-start | bytes 1572872 | tf_op jit(solution)/shard_map/ppermute | solution.py:53
  589.4 48.2 %collective-permute-start.35 = (bf16[512,512]{1,0:T(8,128)(2,1)}, bf16[512,512]{1,0:T(8,128)(2,1)S(1)}, u32[]{:S(2)}, u32[]{:S(2)}) collective-permute-start(bf16[512,512]{1,0:T(8,128)(2,1)} %slice.311), channel_id=1, source_target_pairs={{0,2},{1,3},{2,0},{3,1},{4,6},{5,7},{6,4},{7,5},{8,10},{9,11},{10,... | collective-permute-start | bytes 1572872 | tf_op jit(solution)/shard_map/ppermute | solution.py:53
  626.4 14.6 %collective-permute-start.28 = (bf16[1,2,256,512]{3,2,1,0:T(8,128)(2,1)S(1)}, bf16[1,2,256,512]{3,2,1,0:T(8,128)(2,1)S(1)}, u32[]{:S(2)}, u32[]{:S(2)}) collective-permute-start(bf16[1,2,256,512]{3,2,1,0:T(8,128)(2,1)S(1)} %copy-done.53), channel_id=1, source_target_pairs={{0,8},{8,0},{16,24},{24,16},{1,9},{9,1},{17,25},{25,17},{2,10},{10... | collective-permute-start | bytes 1572872 | tf_op jit(solution)/shard_map/ppermute | solution.py:48
  637.6 13.9 %collective-permute-start.29 = (bf16[1,2,256,512]{3,2,1,0:T(8,128)(2,1)S(1)}, bf16[1,2,256,512]{3,2,1,0:T(8,128)(2,1)S(1)}, u32[]{:S(2)}, u32[]{:S(2)}) collective-permute-start(bf16[1,2,256,512]{3,2,1,0:T(8,128)(2,1)S(1)} %copy-done.53), channel_id=1, source_target_pairs={{0,16},{8,24},{16,0},{24,8},{1,17},{9,25},{17,1},{25,9},{2,18},{10... | collective-permute-start | bytes 1572872 | tf_op jit(solution)/shard_map/ppermute | solution.py:48
  638.1 39.4 %collective-permute-start.31 = (bf16[1,2,256,512]{3,2,1,0:T(8,128)(2,1)S(1)}, bf16[1,2,256,512]{3,2,1,0:T(8,128)(2,1)S(1)}, u32[]{:S(2)}, u32[]{:S(2)}) collective-permute-start(bf16[1,2,256,512]{3,2,1,0:T(8,128)(2,1)S(1)} %copy-done.53), channel_id=1, source_target_pairs={{0,4},{4,0},{1,5},{5,1},{2,6},{6,2},{3,7},{7,3},{8,12},{12,8},{9,1... | collective-permute-start | bytes 1572872 | tf_op jit(solution)/shard_map/ppermute | solution.py:46
  639.4 12.5 %collective-permute-start.38 = (bf16[512,256]{1,0:T(8,128)(2,1)S(1)}, bf16[512,256]{1,0:T(8,128)(2,1)S(1)}, u32[]{:S(2)}, u32[]{:S(2)}) collective-permute-start(bf16[512,256]{1,0:T(8,128)(2,1)S(1)} %constant_dynamic-slice_fusion), channel_id=1, source_target_pairs={{0,4},{4,0},{1,5},{5,1},{2,6},{6,2},{3,7},{7,3},{8,12},{12,8},{9,1... | collective-permute-start | bytes 786440 | tf_op jit(solution)/shard_map/ppermute | solution.py:46
  651.5 13.3 %collective-permute-start.23 = (bf16[1,2,256,512]{3,2,1,0:T(8,128)(2,1)}, bf16[1,2,256,512]{3,2,1,0:T(8,128)(2,1)S(1)}, u32[]{:S(2)}, u32[]{:S(2)}) collective-permute-start(bf16[1,2,256,512]{3,2,1,0:T(8,128)(2,1)} %collective-permute-done.21), channel_id=1, source_target_pairs={{0,16},{8,24},{16,0},{24,8},{1,17},{9,25},{17,1},{25,9},{2,18},{10... | collective-permute-start | bytes 1572872 | tf_op jit(solution)/shard_map/ppermute | solution.py:48
  651.9 14.6 %collective-permute-start.25 = (bf16[1,2,256,512]{3,2,1,0:T(8,128)(2,1)}, bf16[1,2,256,512]{3,2,1,0:T(8,128)(2,1)S(1)}, u32[]{:S(2)}, u32[]{:S(2)}) collective-permute-start(bf16[1,2,256,512]{3,2,1,0:T(8,128)(2,1)} %collective-permute-done.21), channel_id=1, source_target_pairs={{0,4},{4,0},{1,5},{5,1},{2,6},{6,2},{3,7},{7,3},{8,12},{12,8},{9,1... | collective-permute-start | bytes 1572872 | tf_op jit(solution)/shard_map/ppermute | solution.py:46
  652.1 24.8 %collective-permute-start.26 = (bf16[1,2,256,512]{3,2,1,0:T(8,128)(2,1)}, bf16[1,2,256,512]{3,2,1,0:T(8,128)(2,1)S(1)}, u32[]{:S(2)}, u32[]{:S(2)}) collective-permute-start(bf16[1,2,256,512]{3,2,1,0:T(8,128)(2,1)} %collective-permute-done.22), channel_id=1, source_target_pairs={{0,4},{4,0},{1,5},{5,1},{2,6},{6,2},{3,7},{7,3},{8,12},{12,8},{9,1... | collective-permute-start | bytes 1572872 | tf_op jit(solution)/shard_map/ppermute | solution.py:46
  664.7 12.1 %collective-permute-start.30 = (bf16[1,2,256,512]{3,2,1,0:T(8,128)(2,1)S(1)}, bf16[1,2,256,512]{3,2,1,0:T(8,128)(2,1)S(1)}, u32[]{:S(2)}, u32[]{:S(2)}) collective-permute-start(bf16[1,2,256,512]{3,2,1,0:T(8,128)(2,1)S(1)} %collective-permute-done.29), channel_id=1, source_target_pairs={{0,8},{8,0},{16,24},{24,16},{1,9},{9,1},{17,25},{25,17},{2,10},{10... | collective-permute-start | bytes 1572872 | tf_op jit(solution)/shard_map/ppermute | solution.py:48
  665.4 12.3 %collective-permute-start.32 = (bf16[1,2,256,512]{3,2,1,0:T(8,128)(2,1)S(1)}, bf16[1,2,256,512]{3,2,1,0:T(8,128)(2,1)S(1)}, u32[]{:S(2)}, u32[]{:S(2)}) collective-permute-start(bf16[1,2,256,512]{3,2,1,0:T(8,128)(2,1)S(1)} %collective-permute-done.28), channel_id=1, source_target_pairs={{0,4},{4,0},{1,5},{5,1},{2,6},{6,2},{3,7},{7,3},{8,12},{12,8},{9,1... | collective-permute-start | bytes 1572872 | tf_op jit(solution)/shard_map/ppermute | solution.py:46
  (70 other events, 594.5 us)
Sparse Core Ops, SparseCore 0:
  811.0 39.4 reduce-scatter.3

commit v3 on v2

--- a/solution.py
+++ b/solution.py
@@ -14,7 +14,7 @@
 AXES = ("chip", "core", "uly")
 BLK = ("chip", "core")
 MESH = pl.DeviceIdType.MESH
-VMEM_LIMIT = 60 * 1024 * 1024
+VMEM_LIMIT = 62 * 1024 * 1024
 
 
 def dot_nn(left, right, kind=F32):
@@ -255,7 +255,7 @@
     return pl.BlockSpec(memory_space=pl.ANY)
 
 
-def greet(plane=False, line=False, cores=False, pair=False):
+def greet(plane=False, line=False, cores=False, pair=False, across=False, whole=False):
     barrier = pltpu.get_barrier_semaphore()
     chip, core, z = (lax.axis_index(a) for a in AXES)
     others = []
@@ -265,6 +265,10 @@
         others.append({"core": 1 - core})
     if pair:
         others.append({"uly": z ^ 1})
+    if across:
+        others.append({"uly": z ^ 2})
+    if whole:
+        others += [{"uly": z ^ k} for k in range(1, 4)]
     for to in others:
         pl.semaphore_signal(barrier, inc=1, device_id=to, device_id_type=MESH)
     count = len(others)
@@ -388,6 +392,10 @@
 
         if d < last:
             self.pass_on(d)
+        self.each(d, then)
+
+    def each(self, d, then):
+        z, last = self.z, self.last
 
         @pl.when(z - d >= 0)
         def _():
@@ -422,7 +430,7 @@
         way = 0 if right else 1
         to = jnp.minimum(z + 1, last) if right else jnp.maximum(z - 1, 0)
         return pltpu.make_async_remote_copy(
-            src_ref=self.held.at[way, d - 1],
+            src_ref=self.held.at[self.place(right, d)],
             dst_ref=self.came.at[way, d - 1],
             send_sem=self.send.at[way, d - 1],
             recv_sem=self.recv.at[way, d - 1],
@@ -430,26 +438,30 @@
             device_id_type=MESH,
         )
 
+    def place(self, right, d):
+        return d - 1 if right else self.last - d
+
     def step(self, d):
         z, last = self.z, self.last
         for right in (True, False):
             way = 0 if right else 1
+            held = self.held.at[self.place(right, d)]
             valid = (z + d <= last) if right else (z - d >= 0)
             more = (z > 0) if right else (z < last)
             to = jnp.minimum(z + d, last) if right else jnp.maximum(z - d, 0)
 
             @pl.when(valid)
             def _():
-                self.make(to, self.held.at[way, d - 1])
+                self.make(to, held)
 
                 if d < last:
 
                     @pl.when(more)
                     def _():
                         self.copy(right, d + 1).wait_recv()
-                        self.held[way, d - 1] = (
-                            self.held[way, d - 1].astype(F32) + self.came[way, d].astype(F32)
-                        ).astype(BF)
+                        held[...] = (held[...].astype(F32) + self.came[way, d].astype(F32)).astype(
+                            BF
+                        )
 
                 self.copy(right, d).start()
 
@@ -484,6 +496,10 @@
     return pl.ds(pl.multiple_of(block * width, width), width)
 
 
+def chip_chunk(k, width):
+    return pl.ds(pl.multiple_of((lax.axis_index("chip") ^ k) * width, width), width)
+
+
 def chip_order(place, width):
     core = lax.axis_index("core")
     return pl.ds(pl.multiple_of((place % 4) * (2 * width) + (core ^ (place // 4)) * width, width), width)
@@ -491,10 +507,15 @@
 
 def project_kernel(
     tok_ref,
-    gain_ref,
-    first_hbm,
-    second_hbm,
+    gain_one_ref,
+    gain_two_ref,
+    q_hbm,
+    k_hbm,
+    v_hbm,
+    g_hbm,
     out_hbm,
+    up_hbm,
+    down_hbm,
     one_ref,
     first_ref,
     high_ref,
@@ -503,6 +524,8 @@
     w_second_hbm,
     w_out_hbm,
     gains_ref,
+    up_own_hbm,
+    down_own_hbm,
     slots,
     wa,
     wb,
@@ -511,30 +534,51 @@
     precv,
     zsend,
     zrecv,
+    fsend,
+    frecv,
     lsem,
 ):
-    z = lax.axis_index("uly")
+    core, z = lax.axis_index("core"), lax.axis_index("uly")
     rows = tok_ref.shape[0] // 2
     width = tok_ref.shape[1]
     piece = width // 8
+    qk, high = q_hbm.shape[1], high_ref.shape[2]
     greet(plane=True, line=True, cores=True)
+    line = LineGather(slots, zsend, zrecv)
+    slots[z] = tok_ref[...]
+    line.pass_on(0)
+    own = pl.ds(0, piece)
+    local = [
+        pltpu.make_async_copy(src, dst, lsem.at[i])
+        for i, (src, dst) in enumerate(
+            (
+                (q_hbm, wa.at[own, pl.ds(0, qk)]),
+                (k_hbm, wa.at[own, pl.ds(qk, qk)]),
+                (v_hbm.at[:, pl.ds(0, high)], wa.at[own, pl.ds(2 * qk, high)]),
+                (v_hbm.at[:, pl.ds(high, high)], wb.at[own, pl.ds(0, high)]),
+                (g_hbm, wb.at[own, pl.ds(high, g_hbm.shape[1])]),
+                (out_hbm, w_out_hbm.at[:, own]),
+            )
+        )
+    ]
+    for c in local:
+        c.start()
+    gains[0] = jnp.zeros_like(gains[0])
+    gains[0, 0:1, :] = gain_one_ref[...].astype(F32)
+    gains[0, 1:2, :] = gain_two_ref[...].astype(F32)
     items = [
-        PlaneGather(gain_ref, lambda p: gains.at[p], True, psend.at[0], precv.at[0]),
-        PlaneGather(
-            first_hbm,
-            lambda p: wa.at[pl.ds(p * piece, piece)],
-            True,
-            psend.at[1],
-            precv.at[1],
-        ),
-        PlaneGather(
-            second_hbm,
-            lambda p: wb.at[pl.ds(p * piece, piece)],
-            False,
-            psend.at[2],
-            precv.at[2],
-        ),
+        PlaneGather(gains.at[0], lambda p: gains.at[p], True, psend.at[0], precv.at[0])
     ]
+    for i, w in enumerate((wa, wb)):
+        items.append(
+            PlaneGather(
+                w.at[own],
+                lambda p, w=w: w.at[pl.ds(p * piece, piece)],
+                i == 0,
+                psend.at[1 + i],
+                precv.at[1 + i],
+            )
+        )
     half = out_hbm.shape[0] // 2
     for i in range(2):
         part = pl.ds(i * half, half)
@@ -547,24 +591,46 @@
                 precv.at[3 + i],
             )
         )
-    line = LineGather(slots, zsend, zrecv)
-    slots[z] = tok_ref[...]
-    line.pass_on(0)
-    for item in items[:3]:
+    items[0].start()
+    units, cols = up_hbm.shape[1] // 2, down_hbm.shape[1]
+    first_half = pl.ds(0, units)
+    mine, theirs = (pl.ds(pl.multiple_of(c * units, units), units) for c in (core, 1 - core))
+    here = pl.ds(pl.multiple_of(core * cols, cols), cols)
+
+    def remote(i, src, dst, to):
+        return pltpu.make_async_remote_copy(
+            src_ref=src,
+            dst_ref=dst,
+            send_sem=fsend.at[i],
+            recv_sem=frecv.at[i],
+            device_id=to,
+            device_id_type=MESH,
+        )
+
+    cut = [
+        pltpu.make_async_copy(up_hbm.at[:, mine], up_own_hbm.at[here, first_half], lsem.at[6]),
+        pltpu.make_async_copy(down_hbm.at[mine], down_own_hbm.at[first_half, here], lsem.at[7]),
+    ]
+    give = [
+        remote(0, up_hbm.at[:, theirs], up_own_hbm.at[here, first_half], {"core": 1 - core}),
+        remote(1, down_hbm.at[theirs], down_own_hbm.at[first_half, here], {"core": 1 - core}),
+    ]
+    for c in cut:
+        c.start()
+    for c in local[:5]:
+        c.wait()
+    for item in items[1:3]:
         item.start()
-    local = [
-        pltpu.make_async_copy(first_hbm, wa.at[pl.ds(0, piece)], lsem.at[0]),
-        pltpu.make_async_copy(second_hbm, wb.at[pl.ds(0, piece)], lsem.at[1]),
-        pltpu.make_async_copy(out_hbm, w_out_hbm.at[:, pl.ds(0, piece)], lsem.at[2]),
-    ]
-    for c in local:
+    for c in give:
         c.start()
-    gains[0] = gain_ref[...]
     items[0].near()
     items[0].far()
     items[0].corner()
     items[0].finish()
-    gains_ref[...] = gains[...]
+    gains_ref[...] = jnp.zeros_like(gains_ref)
+    for p in range(8):
+        gains_ref[0:1, chunk_of(p, piece)] = gains[p, 0:1, :]
+        gains_ref[1:2, chip_order(p, piece)] = gains[p, 1:2, :]
 
     def normalize(slot):
         step = 32
@@ -581,73 +647,76 @@
                 for p in range(8):
                     src = slots[slot, pl.ds(m * rows + at, step), chunk_of(p, piece)].astype(F32)
                     one_ref[m, to, pl.ds(p * piece, piece)] = (
-                        (src - mean) * scale * gains[p, 0:1, :].astype(F32)
+                        (src - mean) * scale * gains[p, 0:1, :]
                     ).astype(BF)
 
     normalize(z)
     line.take(1, normalize)
-    items[1].near()
-    items[2].near()
+    for item in items[1:3]:
+        item.near()
+    for item in items[1:3]:
+        item.far()
     for item in items[3:]:
         item.start()
-    items[1].far()
-    items[2].far()
     line.take(2, normalize)
-    items[1].corner()
-    items[2].corner()
-    for item in items[3:]:
-        item.near()
-    line.take(3, normalize)
+    for item in items[1:3]:
+        item.corner()
     for item in items[1:3]:
         item.finish()
-    local[0].wait()
-    local[1].wait()
     outs = [
-        pltpu.make_async_copy(wa, w_first_hbm, lsem.at[3]),
-        pltpu.make_async_copy(wb, w_second_hbm, lsem.at[4]),
+        pltpu.make_async_copy(wa, w_first_hbm, lsem.at[8]),
+        pltpu.make_async_copy(wb, w_second_hbm, lsem.at[9]),
     ]
     for c in outs:
         c.start()
     tile = 512
-    for m in range(2):
-
-        @pl.loop(0, wa.shape[1] // tile)
-        def _(n):
-            cols = pl.ds(pl.multiple_of(n * tile, tile), tile)
-            first_ref[m, :, cols] = jnp.dot(
-                one_ref[m], wa[:, cols], preferred_element_type=F32
-            ).astype(BF)
-
-        high = high_ref.shape[2]
-
-        @pl.loop(0, high // tile)
-        def _(n):
-            cols = pl.ds(pl.multiple_of(n * tile, tile), tile)
-            high_ref[m, :, cols] = jnp.dot(
-                one_ref[m], wb[:, cols], preferred_element_type=F32
-            ).astype(BF)
-
-        @pl.loop(0, gate_ref.shape[2] // tile)
-        def _(n):
-            cols = pl.ds(pl.multiple_of(n * tile, tile), tile)
-            from_ = pl.ds(pl.multiple_of(high + n * tile, tile), tile)
-            gate_ref[m, :, cols] = jnp.dot(
-                one_ref[m], wb[:, from_], preferred_element_type=F32
-            )
-
+
+    def multiply(slot):
+        at = pl.ds(pl.multiple_of(slot * rows, rows), rows)
+        x = jnp.concatenate([one_ref[0, at, :], one_ref[1, at, :]], axis=0)
+
+        def tiles(w, start, to_ref):
+            @pl.loop(0, to_ref.shape[2] // tile)
+            def _(n):
+                cols = pl.ds(pl.multiple_of(n * tile, tile), tile)
+                from_ = pl.ds(pl.multiple_of(start + n * tile, tile), tile)
+                r = jnp.dot(x, w[:, from_], preferred_element_type=F32).astype(to_ref.dtype)
+                for m in range(2):
+                    to_ref[m, at, cols] = r[m * rows : (m + 1) * rows]
+
+        tiles(wa, 0, first_ref)
+        tiles(wb, 0, high_ref)
+        tiles(wb, high, gate_ref)
+
+    multiply(z)
+    line.each(1, multiply)
+    for item in items[3:]:
+        item.near()
     for item in items[3:]:
         item.far()
+    line.each(2, multiply)
+
+    def both_steps(slot):
+        normalize(slot)
+        multiply(slot)
+
+    line.take(3, both_steps)
+    for item in items[3:]:
         item.corner()
+    for item in items[3:]:
         item.finish()
     line.finish()
-    local[2].wait()
-    for c in outs:
+    local[5].wait()
+    for c in outs + cut:
+        c.wait()
+    for c in give:
         c.wait()
 
 
 def add_rows_kernel(
     x_ref,
     w_ref,
+    tok_ref,
     up_hbm,
     down_hbm,
     out_ref,
@@ -698,13 +767,16 @@
     line.step(3)
     for c in local:
         c.start()
+    line.step(2)
     for item in items:
         item.near()
-    line.step(2)
     for item in items:
         item.far()
     line.step(1)
     line.close()
+    for k in range(4):
+        cols = pl.ds(k * 2 * width, 2 * width)
+        out_ref[:, cols] += tok_ref[:, chip_chunk(k, 2 * width)].astype(F32)
     for item in items:
         item.corner()
     for item in items:
@@ -716,14 +788,16 @@
 def fan_out_kernel(
     rows_ref,
     w_ref,
+    mixed_ref,
     up_hbm,
     down_hbm,
-    wide_ref,
     grad_ref,
+    part_ref,
     up_ref,
     down_ref,
     slots,
     ordered,
+    total,
     near_up,
     near_down,
     came_up,
@@ -758,8 +832,6 @@
 
     def multiply(slot):
         at = pl.ds(pl.multiple_of(slot * rows, rows), rows)
-        for m in range(2):
-            wide_ref[m, at, :] = slots[slot, m * rows : (m + 1) * rows, :]
         for p in range(8):
             ordered[:, p * width : (p + 1) * width] = slots[slot, :, chip_order(p, width)]
         tile = 256
@@ -771,6 +843,14 @@
             for m in range(2):
                 grad_ref[m, at, part] = product[m * rows : (m + 1) * rows]
 
+        mixed = jnp.concatenate([mixed_ref[0, at, :], mixed_ref[1, at, :]], axis=0)
+
+        @pl.loop(0, 8)
+        def _(p):
+            cols = pl.ds(pl.multiple_of(p * width, width), width)
+            total[p] += dot_tn(ordered[:, cols], mixed)
+
+    total[...] = jnp.zeros_like(total)
     multiply(z)
     line.take(1, multiply)
     for g in groups:
@@ -779,6 +859,7 @@
     for g in groups:
         g.first_sums(1)
     line.take(3, multiply)
+    part_ref[...] = total[...].astype(BF)
     groups[0].finish(up_ref)
     groups[1].finish(down_ref)
     line.finish()
@@ -790,8 +871,10 @@
     gain_ref,
     ups_ref,
     downs_ref,
-    out_ref,
+    keep_ref,
+    give_ref,
     grad_ref,
+    rows_ref,
     gain_grad_ref,
     up_grad_ref,
     down_grad_ref,
@@ -829,7 +912,7 @@
     def _(i):
         at = pl.ds(pl.multiple_of(i * step, step), step)
         hat, _scale = normed(hid_ref[at, :])
-        two[at, :] = (hat * gain_ref[...]).astype(BF)
+        two[at, :] = (hat * gain_ref[1:2, :]).astype(BF)
 
     to_pair = copy(0, two.at[group(0)], two.at[group(2)], pair)
     to_other = copy(1, two.at[group(0)], two.at[group(1)], other)
@@ -863,9 +946,9 @@
                 held[g - 1, 0, :, cols] = back.astype(BF)
                 held[g - 1, 1, :, cols] = down.astype(BF)
 
-    returns = [copy(3 + i, held.at[0, i], came.at[0, i], other) for i in range(2)]
-    returns += [copy(5 + i, held.at[2, i], came.at[1, i], other) for i in range(2)]
-    last = [copy(7 + i, held.at[1, i], came.at[2, i], pair) for i in range(2)]
+    returns = [copy(3 + i, held.at[0, i], came.at[3 * i], other) for i in range(2)]
+    returns += [copy(5 + i, held.at[2, i], came.at[1 + 3 * i], other) for i in range(2)]
+    last = copy(7, held.at[1, 0], came.at[2], pair)
 
     work(0)
     to_other.wait_recv()
@@ -886,10 +969,12 @@
         def _(r):
             at = pl.ds(pl.multiple_of(r * step, step), step)
             held[1, i, at, :] = (
-                held[1, i, at, :].astype(F32) + came[1, i, at, :].astype(F32)
+                held[1, i, at, :].astype(F32) + came[1 + 3 * i, at, :].astype(F32)
             ).astype(BF)
 
-        last[i].start()
+        if i == 0:
+            last.start()
+    give_ref[...] = held[1, 1]
     tile = 512
 
     @pl.loop(0, width // tile)
@@ -900,32 +985,21 @@
 
     for i in range(2):
         returns[i].wait_recv()
-    last[0].wait_recv()
+    last.wait_recv()
     gain_grad_ref[...] = jnp.zeros_like(gain_grad_ref)
 
     @pl.loop(0, rows // step)
     def _(r):
         at = pl.ds(pl.multiple_of(r * step, step), step)
-        back = sums[0, at, :] + came[0, 0, at, :].astype(F32) + came[2, 0, at, :].astype(F32)
+        back = sums[0, at, :] + came[0, at, :].astype(F32) + came[2, at, :].astype(F32)
         hat, scale = normed(hid_ref[at, :])
         gain_grad_ref[...] += jnp.sum(back * hat, axis=0, keepdims=True)
-        grad_ref[at, :] = douts_ref[at, :].astype(F32) + norm_back(
-            back * gain_ref[...], hat, scale
-        )
-
-    last[1].wait_recv()
-
-    @pl.loop(0, rows // step)
-    def _(r):
-        at = pl.ds(pl.multiple_of(r * step, step), step)
-        out_ref[at, :] = (
-            hid_ref[at, :]
-            + sums[1, at, :]
-            + came[0, 1, at, :].astype(F32)
-            + came[2, 1, at, :].astype(F32)
-        ).astype(BF)
-
-    for c in [to_pair, to_other, through] + returns + last:
+        grad = douts_ref[at, :].astype(F32) + norm_back(back * gain_ref[1:2, :], hat, scale)
+        grad_ref[at, :] = grad
+        rows_ref[at, :] = grad.astype(BF)
+        keep_ref[at, :] = hid_ref[at, :] + sums[1, at, :] + came[3, at, :].astype(F32)
+
+    for c in [to_pair, to_other, through, last] + returns:
         c.wait_send()
 
 
@@ -934,6 +1008,7 @@
         chip, core = lax.axis_index("chip"), lax.axis_index("core")
         x, y, other = {"chip": chip ^ 1}, {"chip": chip ^ 2}, {"core": 1 - core}
         self.near, self.came, self.x_first = near, came, x_first
+        self.waited = ()
 
         def copy(i, src, to):
             return pltpu.make_async_remote_copy(
@@ -992,8 +1067,13 @@
         self.copies[self.cores + 2].wait_recv()
         self.add(self.stay[0], self.cores + 2)
         out_ref[...] = self.near[0]
-        for c in self.copies:
-            c.wait_send()
+        for i, c in enumerate(self.copies):
+            if i not in self.waited:
+                c.wait_send()
+
+
+def far_slot(i, x_first):
+    return ((3, 1, 2, 0) if x_first else (3, 2, 1, 0)).index(i) % 2
 
 
 def close_rows_kernel(
@@ -1001,50 +1081,46 @@
     xb_ref,
     wa_ref,
     wb_ref,
-    ga_hbm,
-    gb_hbm,
-    go_hbm,
+    one_ref,
+    tok_ref,
+    hid_ref,
+    gain_ref,
+    gain_two_ref,
     out_ref,
     sum_a_ref,
     sum_b_ref,
-    sum_o_ref,
+    gains_ref,
     held,
     came,
     near_a,
     near_b,
-    near_o,
+    far_a,
+    far_b,
     came_a,
     came_b,
-    came_o,
+    gain_sum,
+    small,
+    small_came,
+    small_line,
     send,
     recv,
     psend,
     precv,
-    lsem,
+    ssend,
+    srecv,
 ):
+    chip, core, z = (lax.axis_index(a) for a in AXES)
     rows = out_ref.shape[0] // 2
+    length = one_ref.shape[0] // 2
     width = out_ref.shape[1] // 8
-    greet(plane=True, line=True, cores=True)
-    groups = []
-    local = []
-    for i, (hbm, near, got, x_first) in enumerate(
-        ((ga_hbm, near_a, came_a, True), (gb_hbm, near_b, came_b, False), (go_hbm, near_o, came_o, True))
-    ):
-        groups.append(
-            PlaneReduce(
-                lambda p, hbm=hbm: hbm.at[p], near, got, x_first, psend.at[i], precv.at[i]
-            )
-        )
-        local.append(pltpu.make_async_copy(hbm.at[pl.ds(0, 4)], near, lsem.at[i]))
-    for g in groups:
-        g.start()
-    for c in local:
-        c.start()
+    greet(plane=True, cores=True, whole=True)
 
     def make(a, to):
-        at = pl.ds(pl.multiple_of(a * rows, rows), rows)
-        xa = jnp.concatenate([xa_ref[0, at, :], xa_ref[1, at, :]], axis=0)
-        xb = jnp.concatenate([xb_ref[0, at, :], xb_ref[1, at, :]], axis=0)
+        at = [
+            pl.ds(pl.multiple_of(m * length + a * rows, rows), rows) for m in range(2)
+        ]
+        xa = jnp.concatenate([xa_ref[i, :] for i in at], axis=0)
+        xb = jnp.concatenate([xb_ref[i, :] for i in at], axis=0)
 
         @pl.loop(0, 8)
         def _(p):
@@ -1054,20 +1130,563 @@
             ).astype(to.dtype)
 
     line = LineReduce(make, out_ref, held, came, send, recv)
+    sets = []
+    for i, (x_ref, near, far, got, x_first) in enumerate(
+        (
+            (xa_ref, near_a, far_a, came_a, True),
+            (xb_ref, near_b, far_b, came_b, False),
+        )
+    ):
+        group = PlaneReduce(
+            lambda p, far=far, x=x_first: far.at[far_slot(p - 4, x)],
+            near,
+            got,
+            x_first,
+            psend.at[i],
+            precv.at[i],
+        )
+        group.waited = tuple((3, group.away[0]))
+        sets.append((group, x_ref, near, far, got))
+
+    tile = 512
+
+    def product(x_ref, place, to, more=None):
+        @pl.loop(0, x_ref.shape[1] // tile)
+        def _(n):
+            cols = pl.ds(pl.multiple_of(n * tile, tile), tile)
+            r = dot_tn(one_ref[:, place * width : (place + 1) * width], x_ref[:, cols])
+            if more is not None:
+                r = r + more[:, cols].astype(F32)
+            to[:, cols] = r.astype(BF)
+
     line.step(3)
-    for c in local:
+    for n in range(4):
+        for group, x_ref, near, far, got in sets:
+            order = (3, group.away[0], group.stay[1], 0)
+            if n >= 2:
+                group.copies[order[n - 2]].wait_send()
+            product(x_ref, 4 + order[n], far.at[n % 2])
+            group.copies[order[n]].start()
+
+    def add_near(n):
+        for group, x_ref, near, far, got in sets:
+            i = (3, group.away[0], group.stay[1], 0)[n]
+            group.copies[i].wait_recv()
+            product(x_ref, i, near.at[i], got.at[i])
+            if n < 2:
+                group.copies[4 + (1 - n)].start()
+
+    add_near(0)
+    add_near(1)
+    line.step(2)
+    add_near(2)
+    add_near(3)
+    line.step(1)
+    for group, *_ in sets:
+        group.first_sums(0)
+    line.close()
+    step = 32
+    gain_sum[...] = jnp.zeros_like(gain_sum)
+
+    @pl.loop(0, 2 * rows // step)
+    def _(r):
+        at = pl.ds(pl.multiple_of(r * step, step), step)
+        hat, scale = normed(tok_ref[at, :].astype(F32))
+        grad = out_ref[at, :]
+        gain_sum[...] += jnp.sum(grad * hat, axis=0, keepdims=True)
+        out_ref[at, :] = norm_back(grad * gain_ref[0:1, :], hat, scale)
+        for k in range(4):
+            out_ref[at, chip_chunk(k, 2 * width)] += hid_ref[
+                at, k * 2 * width : (k + 1) * 2 * width
+            ]
+
+    small[...] = jnp.zeros_like(small)
+    for p in range(8):
+        small[p, 0:1, :] = gain_sum[:, chunk_of(p, width)]
+        small[p, 1:2, :] = gain_two_ref[:, chip_order(p, width)]
+
+    def pass_small(i, src, dst, to):
+        return pltpu.make_async_remote_copy(
+            src_ref=src,
+            dst_ref=dst,
+            send_sem=ssend.at[i],
+            recv_sem=srecv.at[i],
+            device_id=to,
+            device_id_type=MESH,
+        )
+
+    sent = []
+    for i, (count, to) in enumerate(
+        ((4, {"core": 1 - core}), (2, {"chip": chip ^ 2}), (1, {"chip": chip ^ 1}))
+    ):
+        c = pass_small(
+            i, small.at[pl.ds(count, count)], small_came.at[pl.ds(count, count)], to
+        )
+        c.start()
+        if i == 0:
+            for group, *_ in sets:
+                group.first_sums(1)
+        c.wait_recv()
+        small[0:count] = small[0:count] + small_came[count : 2 * count]
+        sent.append(c)
+    last = [
+        pass_small(2 + k, small.at[0], small_line.at[k], {"uly": z ^ k}) for k in range(1, 4)
+    ]
+    for c in last:
+        c.start()
+    for (group, *_), out in zip(sets, (sum_a_ref, sum_b_ref)):
+        group.finish(out)
+    total = small[0]
+    for k in range(1, 4):
+        last[k - 1].wait_recv()
+        total = total + small_line[k]
+    gains_ref[...] = total
+    for c in sent + last:
+        c.wait_send()
+
+
+class StateExchange:
+    def __init__(self, coef_ref, own, sib, chips, mine, came, final, send, recv):
+        self.core = lax.axis_index("core")
+        self.coef, self.own, self.sib, self.chips = coef_ref, own, sib, chips
+        self.mine, self.came, self.final = mine, came, final
+
+        def copy(i, src, dst):
+            return pltpu.make_async_remote_copy(
+                src_ref=src,
+                dst_ref=dst,
+                send_sem=send.at[2, i],
+                recv_sem=recv.at[2, i],
+                device_id={"core": 1 - self.core},
+                device_id_type=MESH,
+            )
+
+        self.first = copy(0, own, sib)
+        self.second = copy(1, mine, came)
+        self.items = [
+            PlaneGather(
+                chips.at[0, h], lambda p, h=h: chips.at[p, h], h == 0, send.at[h], recv.at[h], False
+            )
+            for h in range(2)
+        ]
+
+    def start(self):
+        self.first.start()
+
+    def join(self):
+        self.first.wait_recv()
+        m = self.core
+        for h in range(2):
+            self.chips[0, h] = (
+                self.coef[m, h, 0] * self.own[m, h].astype(F32)
+                + self.coef[m, h, 1] * self.sib[m, h].astype(F32)
+            ).astype(BF)
+            self.items[h].start()
+
+    def near(self):
+        for item in self.items:
+            item.near()
+
+    def far(self):
+        for item in self.items:
+            item.far()
+
+    def settle(self):
+        for item in self.items:
+            item.corner()
+        m = self.core
+        for h in range(2):
+            total = self.coef[m, h, 5] * self.chips[1, h].astype(F32)
+            for k in (2, 3):
+                total = total + self.coef[m, h, 4 + k] * self.chips[k, h].astype(F32)
+            self.mine[h] = total.astype(BF)
+        self.second.start()
+        self.last(m, self.mine)
+        self.second.wait_recv()
+        self.last(1 - m, self.came)
+
+    def last(self, m, chip_state):
+        for h in range(2):
+            self.final[m, h] = (
+                self.coef[m, h, 2] * chip_state[h].astype(F32)
+                + self.coef[m, h, 3] * self.sib[m, h].astype(F32)
+            ).astype(BF)
+
+    def finish(self):
+        self.first.wait_send()
+        self.second.wait_send()
+        for item in self.items:
+            item.finish()
+
+
+def state_scratch(shape):
+    half = shape[1:]
+    return [
+        pltpu.VMEM(shape, BF),
+        pltpu.VMEM(shape, BF),
+        pltpu.VMEM((4, *half), BF),
+        pltpu.VMEM(half, BF),
+        pltpu.VMEM(half, BF),
+        sems(3, 3),
+        sems(3, 3),
+    ]
+
+
+class Places:
+    def __init__(self, lengths_ref, m, length):
+        self.length = length
+        self.base = (lax.axis_index("chip") * 2 + lax.axis_index("core")) * length
+        self.bounds = []
+        total = 0
+        for n in range(lengths_ref.shape[1]):
+            self.bounds.append(total)
+            total = total + lengths_ref[m, n]
+
+    def segment(self, at):
+        found = jnp.zeros_like(at)
+        for b in self.bounds:
+            found = found + jnp.where(self.base + at >= b, 1, 0)
+        return found
+
+    def table(self, rate, start, count, across):
+        shape = (count, self.length)
+        rows = start + lax.broadcasted_iota(jnp.int32, shape, 0)
+        cols = lax.broadcasted_iota(jnp.int32, shape, 1)
+        off = cols - rows if across else rows - cols
+        seg_rows = self.segment(start + lax.broadcasted_iota(jnp.int32, (count, 1), 0))
+        seg_cols = self.segment(lax.broadcasted_iota(jnp.int32, (1, self.length), 1))
+        far = jnp.maximum(off, 0).astype(F32)
+        return jnp.where((off >= 0) & (seg_rows == seg_cols), jnp.exp(-rate * far), 0.0)
+
+    def entry(self, rate, start, count):
+        at = start + lax.broadcasted_iota(jnp.int32, (count, 1), 0)
+        same = self.segment(at) == self.segment(jnp.full((1, 1), -1, jnp.int32))
+        return jnp.where(same, jnp.exp(-rate * (at + 1).astype(F32)), 0.0)
+
+    def leave(self, rate, start, count):
+        at = start + lax.broadcasted_iota(jnp.int32, (count, 1), 0)
+        end = jnp.full((1, 1), self.length - 1, jnp.int32)
+        same = self.segment(at) == self.segment(end)
+        return jnp.where(same, jnp.exp(-rate * (self.length - 1 - at).astype(F32)), 0.0)
+
+
+ROWS = 128
+
+
+def retain_kernel(
+    rates_ref,
+    lengths_ref,
+    coef_ref,
+    a_ref,
+    high_ref,
+    gate_ref,
+    dout_ref,
+    up_hbm,
+    down_hbm,
+    mixed_ref,
+    kept_ref,
+    state_ref,
+    douts_ref,
+    up_own_hbm,
+    down_own_hbm,
+    own,
+    sib,
+    chips,
+    mine,
+    came,
+    send,
+    recv,
+    ordered,
+    others,
+    dsend,
+    drecv,
+    fsend,
+    frecv,
+    lsem,
+):
+    _, length, vd = high_ref.shape
+    qk = (a_ref.shape[2] - vd) // 2
+    hd = qk // 2
+    greet(plane=True, cores=True, pair=True, across=True)
+    z = lax.axis_index("uly")
+    units = up_hbm.shape[1]
+    first_half, second_half = pl.ds(0, units), pl.ds(units, units)
+    keep, away = [], []
+    for i, (src, first, second) in enumerate(
+        (
+            (up_hbm, up_own_hbm.at[:, first_half], up_own_hbm.at[:, second_half]),
+            (down_hbm, down_own_hbm.at[first_half], down_own_hbm.at[second_half]),
+        )
+    ):
+        keep.append(pltpu.make_async_copy(src, first, lsem.at[i]))
+        away.append(
+            pltpu.make_async_remote_copy(
+                src_ref=src,
+                dst_ref=second,
+                send_sem=fsend.at[i],
+                recv_sem=frecv.at[i],
+                device_id={"uly": z ^ 2},
+                device_id_type=MESH,
+            )
+        )
+    for c in away + keep:
+        c.start()
+    quarter = ordered.shape[1] // 4
+    for k in range(4):
+        ordered[:, k * quarter : (k + 1) * quarter] = dout_ref[:, chip_chunk(k, quarter)]
+
+    def rows_to(i, src, to):
+        return pltpu.make_async_remote_copy(
+            src_ref=src,
+            dst_ref=others.at[i],
+            send_sem=dsend.at[i],
+            recv_sem=drecv.at[i],
+            device_id=to,
+            device_id_type=MESH,
+        )
+
+    other = {"core": 1 - lax.axis_index("core")}
+    to_pair = rows_to(1, ordered, {"uly": z ^ 1})
+    to_other = rows_to(0, ordered, other)
+    through = rows_to(2, others.at[1], other)
+    to_pair.start()
+    states = StateExchange(coef_ref, own, sib, chips, mine, came, state_ref, send, recv)
+
+    def values(m, h):
+        return high_ref[m] if h else a_ref[m, :, 2 * qk :]
+
+    def keys(m, h):
+        return a_ref[m, :, qk + h * hd : qk + (h + 1) * hd]
+
+    for h in range(2):
+
+        @pl.loop(0, 2)
+        def _(m):
+            leave = Places(lengths_ref, m, length).leave(rates_ref[h], 0, length)
+            k = (keys(m, h).astype(F32) * leave).astype(BF)
+            own[m, h] = dot_tn(k, values(m, h), BF)
+
+    states.start()
+    parts = length // ROWS
+
+    def local(h):
+        @pl.loop(0, 2 * parts)
+        def _(i):
+            m, r = i // parts, i % parts
+            at = pl.ds(pl.multiple_of(r * ROWS, ROWS), ROWS)
+            table = Places(lengths_ref, m, length).table(rates_ref[h], r * ROWS, ROWS, False)
+            q = a_ref[m, at, h * hd : (h + 1) * hd]
+            scores = (dot_nt(q, keys(m, h)) * table).astype(BF)
+            kept_ref[m, at, h * vd : (h + 1) * vd] = jnp.dot(
+                scores, values(m, h), preferred_element_type=F32
+            )
+
+    states.join()
+    to_other.start()
+    local(0)
+    states.near()
+    local(1)
+    states.far()
+    to_pair.wait_recv()
+    through.start()
+    states.settle()
+    for h in range(2):
+
+        @pl.loop(0, 2 * parts)
+        def _(i):
+            m, r = i // parts, i % parts
+            at = pl.ds(pl.multiple_of(r * ROWS, ROWS), ROWS)
+            cols = slice(h * vd, (h + 1) * vd)
+            entry = Places(lengths_ref, m, length).entry(rates_ref[h], r * ROWS, ROWS)
+            q = a_ref[m, at, h * hd : (h + 1) * hd]
+            kept = kept_ref[m, at, cols] + entry * jnp.dot(
+                q, state_ref[m, h], preferred_element_type=F32
+            )
+            kept_ref[m, at, cols] = kept
+            g = gate_ref[m, at, cols]
+            mixed_ref[m, at, cols] = (g * sigmoid(g) * normed(kept)[0]).astype(BF)
+
+    states.finish()
+    rows = ordered.shape[0]
+    douts_ref[0:rows, :] = ordered[...]
+    to_other.wait_recv()
+    through.wait_recv()
+    for i in range(3):
+        douts_ref[(1 + i) * rows : (2 + i) * rows, :] = others[i]
+    for c in (to_pair, to_other, through):
+        c.wait_send()
+    for c in keep + away:
         c.wait()
-    for g in groups:
-        g.core_sums()
-    line.step(2)
-    line.step(1)
-    for g in groups:
-        g.first_sums(0)
-    for g in groups:
-        g.first_sums(1)
-    line.close()
-    for g, out in zip(groups, (sum_a_ref, sum_b_ref, sum_o_ref)):
-        g.finish(out)
+
+
+def sigmoid(v):
+    return 0.5 * jnp.tanh(0.5 * v) + 0.5
+
+
+def retain_back_kernel(
+    rates_ref,
+    lengths_ref,
+    coef_ref,
+    a_ref,
+    high_ref,
+    gate_ref,
+    kept_ref,
+    grad_ref,
+    state_ref,
+    part_hbm,
+    keep_ref,
+    give_hbm,
+    xa_ref,
+    xb_ref,
+    sum_ref,
+    out_ref,
+    pulled,
+    grad_k,
+    grad_v,
+    final,
+    own,
+    sib,
+    chips,
+    mine,
+    came,
+    send,
+    recv,
+    near,
+    got,
+    psend,
+    precv,
+    lsem,
+    came_rows,
+    rsend,
+    rrecv,
+):
+    _, length, vd = high_ref.shape
+    qk = (a_ref.shape[2] - vd) // 2
+    hd = qk // 2
+    greet(plane=True, cores=True, pair=True)
+    give = pltpu.make_async_remote_copy(
+        src_ref=give_hbm,
+        dst_ref=came_rows,
+        send_sem=rsend,
+        recv_sem=rrecv,
+        device_id={"uly": lax.axis_index("uly") ^ 1},
+        device_id_type=MESH,
+    )
+    give.start()
+    group = PlaneReduce(lambda p: part_hbm.at[p], near, got, True, psend, precv)
+    local = pltpu.make_async_copy(part_hbm.at[pl.ds(0, 4)], near, lsem)
+    local.start()
+    group.start()
+    states = StateExchange(coef_ref, own, sib, chips, mine, came, final, send, recv)
+    parts = length // ROWS
+
+    def values(m, h, at=slice(None)):
+        return high_ref[m, at, :] if h else a_ref[m, at, 2 * qk :]
+
+    def keys(m, h, at=slice(None)):
+        return a_ref[m, at, qk + h * hd : qk + (h + 1) * hd]
+
+    def queries(m, h, at=slice(None)):
+        return a_ref[m, at, h * hd : (h + 1) * hd]
+
+    for h in range(2):
+        cols = slice(h * vd, (h + 1) * vd)
+
+        @pl.loop(0, 2 * parts)
+        def _(i):
+            m, r = i // parts, i % parts
+            at = pl.ds(pl.multiple_of(r * ROWS, ROWS), ROWS)
+            g, gm = gate_ref[m, at, cols], grad_ref[m, at, cols]
+            sigma = sigmoid(g)
+            hat, scale = normed(kept_ref[m, at, cols])
+            xb_ref[m, at, vd + h * vd : vd + (h + 1) * vd] = (
+                gm * hat * (sigma + g * sigma * (1.0 - sigma))
+            ).astype(BF)
+            pulled[m, at, cols] = norm_back(gm * g * sigma, hat, scale).astype(BF)
+
+        @pl.loop(0, 2)
+        def _(m):
+            entry = Places(lengths_ref, m, length).entry(rates_ref[h], 0, length)
+            q = (queries(m, h).astype(F32) * entry).astype(BF)
+            own[m, h] = dot_tn(q, pulled[m, :, cols], BF)
+
+    states.start()
+
+    def local_q(h):
+        cols = slice(h * vd, (h + 1) * vd)
+
+        @pl.loop(0, 2 * parts)
+        def _(i):
+            m, r = i // parts, i % parts
+            at = pl.ds(pl.multiple_of(r * ROWS, ROWS), ROWS)
+            places = Places(lengths_ref, m, length)
+            table = places.table(rates_ref[h], r * ROWS, ROWS, False)
+            gr = pulled[m, at, cols]
+            p = (dot_nt(gr, values(m, h)) * table).astype(BF)
+            entry = places.entry(rates_ref[h], r * ROWS, ROWS)
+            xa_ref[m, at, h * hd : (h + 1) * hd] = (
+                jnp.dot(p, keys(m, h), preferred_element_type=F32)
+                + entry * dot_nt(gr, state_ref[m, h])
+            ).astype(BF)
+
+    def local_kv(h):
+        cols = slice(h * vd, (h + 1) * vd)
+
+        @pl.loop(0, 2 * parts)
+        def _(i):
+            m, r = i // parts, i % parts
+            at = pl.ds(pl.multiple_of(r * ROWS, ROWS), ROWS)
+            table = Places(lengths_ref, m, length).table(rates_ref[h], r * ROWS, ROWS, True)
+            p = (dot_nt(values(m, h, at), pulled[m, :, cols]) * table).astype(BF)
+            scores = (dot_nt(keys(m, h, at), queries(m, h)) * table).astype(BF)
+            grad_k[m, at, h * hd : (h + 1) * hd] = jnp.dot(
+                p, queries(m, h), preferred_element_type=F32
+            )
+            grad_v[m, at, cols] = jnp.dot(
+                scores, pulled[m, :, cols], preferred_element_type=F32
+            )
+
+    states.join()
+    local_q(0)
+    states.near()
+    states.far()
+    local_q(1)
+    states.settle()
+    local.wait()
+    group.core_sums()
+    local_kv(0)
+    local_kv(1)
+    group.first_sums(0)
+    group.first_sums(1)
+    for h in range(2):
+
+        @pl.loop(0, 2 * parts)
+        def _(i):
+            m, r = i // parts, i % parts
+            at = pl.ds(pl.multiple_of(r * ROWS, ROWS), ROWS)
+            leave = Places(lengths_ref, m, length).leave(rates_ref[h], r * ROWS, ROWS)
+            xa_ref[m, at, qk + h * hd : qk + (h + 1) * hd] = (
+                grad_k[m, at, h * hd : (h + 1) * hd]
+                + leave * dot_nt(values(m, h, at), final[m, h])
+            ).astype(BF)
+            gv = (
+                grad_v[m, at, h * vd : (h + 1) * vd]
+                + leave * jnp.dot(keys(m, h, at), final[m, h], preferred_element_type=F32)
+            ).astype(BF)
+            if h:
+                xb_ref[m, at, :vd] = gv
+            else:
+                xa_ref[m, at, 2 * qk :] = gv
+
+    states.finish()
+    give.wait()
+    quarter = keep_ref.shape[1] // 4
+    for k in range(4):
+        cols = slice(k * quarter, (k + 1) * quarter)
+        out_ref[:, chip_chunk(k, quarter)] = (
+            keep_ref[:, cols] + came_rows[:, cols].astype(F32)
+        ).astype(BF)
+    group.finish(sum_ref)
 
 
 def sems(*shape):
@@ -1093,12 +1712,142 @@
     )(*args)
 
 
-def project(tokens, gains, first, second, out_weight):
+def smem():
+    return pl.BlockSpec(memory_space=pltpu.SMEM)
+
+
+def chip_weights(rates, lengths, block):
+    chip, core = lax.axis_index("chip"), lax.axis_index("core")
+    count = block_count()
+    places = jnp.arange(count, dtype=jnp.int32)
+    ahead, back = [], []
+    others = chip ^ jnp.arange(4, dtype=jnp.int32)
+    for m in range(lengths.shape[0]):
+        ends = segment_ids((places + 1) * block - 1, lengths[m])
+
+        def end(b):
+            return jnp.where(b < 0, 0, ends[jnp.maximum(b, 0)])
+
+        whole = jnp.exp(-rates * block)
+        even = jnp.where(end(2 * chip) == end(2 * chip - 1), whole, 0.0)
+        odd = jnp.where(end(2 * chip + 1) == end(2 * chip), whole, 0.0)
+        one, zero = jnp.ones_like(whole), jnp.zeros_like(whole)
+        first = core == 0
+
+        def pick(a, b):
+            return jnp.where(first, a, b)
+
+        past = jnp.where(
+            ((others < chip) & (end(2 * others + 1) == end(2 * chip - 1)))[None],
+            jnp.exp(-rates[:, None] * (2.0 * block) * jnp.maximum(chip - 1 - others, 0)[None]),
+            0.0,
+        )
+        later = jnp.where(
+            ((others > chip) & (end(2 * chip + 1) == end(2 * others - 1)))[None],
+            jnp.exp(-rates[:, None] * (2.0 * block) * jnp.maximum(others - 1 - chip, 0)[None]),
+            0.0,
+        )
+        four = [pick(odd, one), pick(one, odd), pick(one, even), pick(zero, one)]
+        ahead.append(jnp.concatenate([jnp.stack(four, axis=1), past], axis=1))
+        four = [pick(one, even), pick(even, one), pick(odd, one), pick(one, zero)]
+        back.append(jnp.concatenate([jnp.stack(four, axis=1), later], axis=1))
+    return jnp.stack(ahead), jnp.stack(back)
+
+
+def retain(rates, lengths, coef, a, high, gate, out_rows, up, down):
+    micro, length, vd = high.shape
+    hd = (a.shape[2] - vd) // 4
+    state = (micro, 2, hd, vd)
+    return call(
+        retain_kernel,
+        5,
+        [smem()] * 3 + [vmem()] * 4 + [anywhere()] * 2,
+        [
+            ((micro, length, 2 * vd), BF, vmem()),
+            ((micro, length, 2 * vd), F32, vmem()),
+            (state, BF, vmem()),
+            ((4 * out_rows.shape[0], out_rows.shape[1]), BF, vmem()),
+            ((up.shape[0], 2 * up.shape[1]), BF, anywhere()),
+            ((2 * down.shape[0], down.shape[1]), BF, anywhere()),
+        ],
+        state_scratch(state)
+        + [
+            pltpu.VMEM(out_rows.shape, BF),
+            pltpu.VMEM((3, *out_rows.shape), BF),
+            sems(3),
+            sems(3),
+            sems(2),
+            sems(2),
+            sems(2),
+        ],
+        4 * micro * length * length * (hd + vd),
+        rates,
+        lengths,
+        coef,
+        a,
+        high,
+        gate,
+        out_rows,
+        up,
+        down,
+    )
+
+
+def retain_back(rates, lengths, coef, a, high, gate, kept, grad_mixed, state, part, keep, give):
+    micro, length, vd = high.shape
+    hd = (a.shape[2] - vd) // 4
+    return call(
+        retain_back_kernel,
+        6,
+        [smem()] * 3 + [vmem()] * 6 + [anywhere(), vmem(), anywhere()],
+        [
+            ((micro, length, a.shape[2]), BF, vmem()),
+            ((micro, length, 3 * vd), BF, vmem()),
+            (part.shape[1:], BF, vmem()),
+            (give.shape, BF, vmem()),
+        ],
+        [
+            pltpu.VMEM((micro, length, 2 * vd), BF),
+            pltpu.VMEM((micro, length, 2 * hd), F32),
+            pltpu.VMEM((micro, length, 2 * vd), F32),
+            pltpu.VMEM(state.shape, BF),
+        ]
+        + state_scratch(state.shape)
+        + [
+            pltpu.VMEM((4, *part.shape[1:]), BF),
+            pltpu.VMEM((7, *part.shape[1:]), BF),
+            sems(7),
+            sems(7),
+            pltpu.SemaphoreType.DMA,
+            pltpu.VMEM(give.shape, BF),
+            pltpu.SemaphoreType.DMA,
+            pltpu.SemaphoreType.DMA,
+        ],
+        12 * micro * length * length * (hd + vd),
+        rates,
+        lengths,
+        coef,
+        a,
+        high,
+        gate,
+        kept,
+        grad_mixed,
+        state,
+        part,
+        keep,
+        give,
+    )
+
+
+def project(tokens, gains, weights, out_weight, up_weight, down_weight):
     micro, rows, width = tokens.shape
     count = lax.axis_size("uly")
-    high = second.shape[1] - out_weight.shape[0]
+    query, key, value, gate = weights
+    high = value.shape[1] // 2
     if not is_cube():
-        full = lax.all_gather(gains, BLK, axis=1, tiled=True)
+        first = jnp.concatenate([query, key, value[:, :high]], axis=1)
+        second = jnp.concatenate([value[:, high:], gate], axis=1)
+        full = lax.all_gather(jnp.stack(gains), BLK, axis=1, tiled=True)
         w_first = lax.all_gather(first, BLK, axis=0, tiled=True)
         w_second = lax.all_gather(second, BLK, axis=0, tiled=True)
         w_out = lax.all_gather(out_weight, BLK, axis=1, tiled=True)
@@ -1111,16 +1860,18 @@
             w_first,
             w_second,
             w_out,
-            full,
+            full.astype(F32),
+            up_weight,
+            down_weight,
         )
     wide = count * rows
     piece = width // 8
-    padded = jnp.concatenate([gains, jnp.zeros((14, piece), BF)], axis=0)
-    na, nb, no = first.shape[1], second.shape[1], out_weight.shape[0]
-    out = call(
+    na, nb, no = 2 * query.shape[1] + high, high + gate.shape[1], out_weight.shape[0]
+    units = up_weight.shape[1]
+    return call(
         project_kernel,
         0,
-        [vmem(), vmem(), anywhere(), anywhere(), anywhere()],
+        [vmem()] * 3 + [anywhere()] * 7,
         [
             ((micro, wide, width), BF, vmem()),
             ((micro, wide, na), BF, vmem()),
@@ -1129,46 +1880,45 @@
             ((width, na), BF, anywhere()),
             ((width, nb), BF, anywhere()),
             ((no, width), BF, anywhere()),
-            ((8, 16, piece), BF, vmem()),
+            ((8, width), F32, vmem()),
+            ((2 * piece, units // 2), BF, anywhere()),
+            ((units // 2, 2 * piece), BF, anywhere()),
         ],
         [
             pltpu.VMEM((count, micro * rows, width), BF),
             pltpu.VMEM((width, na), BF),
             pltpu.VMEM((width, nb), BF),
-            pltpu.VMEM((8, 16, piece), BF),
+            pltpu.VMEM((8, 8, piece), F32),
             sems(5, 7),
             sems(5, 7),
             sems(2, count - 1),
             sems(2, count - 1),
-            sems(5),
+            sems(2),
+            sems(2),
+            sems(10),
         ],
         2 * micro * wide * width * (na + nb),
         tokens.reshape(micro * rows, width),
-        padded,
-        first,
-        second,
+        gains[0][None],
+        gains[1][None],
+        query,
+        key,
+        value,
+        gate,
         out_weight,
+        up_weight,
+        down_weight,
     )
-    got = out[7][:, :2]
-    me = block_index()
-    full = jnp.concatenate(
-        [
-            lax.dynamic_index_in_dim(got, ((me ^ b) & 1) * 4 + ((me ^ b) >> 1), 0, False)
-            for b in range(8)
-        ],
-        axis=1,
-    )
-    return (*out[:7], full)
 
 
 def line_scratch(count, rows, width):
     return [
-        pltpu.VMEM((2, count - 1, rows, width), BF),
+        pltpu.VMEM((count - 1, rows, width), BF),
         pltpu.VMEM((2, count - 1, rows, width), BF),
     ]
 
 
-def add_rows(mixed, w_out, up, down):
+def add_rows(mixed, w_out, tokens, up, down):
     micro, wide, hidden = mixed.shape
     count = lax.axis_size("uly")
     rows = wide // count
@@ -1177,7 +1927,7 @@
     out = call(
         add_rows_kernel,
         1,
-        [vmem(), vmem(), anywhere(), anywhere()],
+        [vmem()] * 3 + [anywhere()] * 2,
         [
             ((micro * rows, width), F32, vmem()),
             ((width, units), BF, anywhere()),
@@ -1189,13 +1939,14 @@
         2 * micro * wide * hidden * width,
         mixed,
         w_out,
+        tokens,
         up,
         down,
     )
     return out
 
 
-def fan_out(rows_bf, w_out, up_grad, down_grad):
+def fan_out(rows_bf, w_out, mixed, up_grad, down_grad):
     own, width = rows_bf.shape
     micro, rows = 2, own // 2
     count = lax.axis_size("uly")
@@ -1204,16 +1955,17 @@
     return call(
         fan_out_kernel,
         2,
-        [vmem(), vmem(), anywhere(), anywhere()],
+        [vmem()] * 3 + [anywhere()] * 2,
         [
-            ((micro, count * rows, width), BF, vmem()),
             ((micro, count * rows, hidden), F32, vmem()),
+            ((8, width // 8, hidden), BF, vmem()),
             (up_shape, BF, vmem()),
             (down_shape, BF, vmem()),
         ],
         [
             pltpu.VMEM((count, own, width), BF),
             pltpu.VMEM((own, width), BF),
+            pltpu.VMEM((8, width // 8, hidden), F32),
             pltpu.VMEM((4, *up_shape), BF),
             pltpu.VMEM((4, *down_shape), BF),
             pltpu.VMEM((3, *up_shape), BF),
@@ -1224,9 +1976,10 @@
             sems(2, 3),
             sems(2),
         ],
-        2 * micro * count * rows * hidden * width,
+        4 * micro * count * rows * hidden * width,
         rows_bf,
         w_out,
+        mixed,
         up_grad,
         down_grad,
     )
@@ -1240,8 +1993,10 @@
         4,
         [vmem()] * 5,
         [
+            ((own, width), F32, vmem()),
             ((own, width), BF, vmem()),
             ((own, width), F32, vmem()),
+            ((own, width), BF, vmem()),
             ((1, width), F32, vmem()),
             ((4, width // 4, units), BF, vmem()),
             ((4, units, width // 4), BF, vmem()),
@@ -1252,9 +2007,9 @@
             pltpu.VMEM((4 * own, units), BF),
             pltpu.VMEM((2, own, width), F32),
             pltpu.VMEM((3, 2, own, width), BF),
-            pltpu.VMEM((3, 2, own, width), BF),
-            sems(9),
-            sems(9),
+            pltpu.VMEM((5, own, width), BF),
+            sems(8),
+            sems(8),
         ],
         2 * 6 * 4 * own * units * width,
         hidden,
@@ -1265,39 +2020,6 @@
     )
 
 
-def to_chips(array):
-    if not is_cube():
-        return array
-    chip = lax.axis_index("chip")
-    width = array.shape[-1] // 4
-    return jnp.concatenate(
-        [
-            lax.dynamic_slice_in_dim(array, (chip ^ k) * width, width, array.ndim - 1)
-            for k in range(4)
-        ],
-        axis=-1,
-    )
-
-
-def core_half(array, dim):
-    own, other = core_cut(array, dim)
-    return core_join(own, swap(other, 1), 1 - dim)
-
-
-def feed_shards(up_shard, down_shard):
-    up, down = core_half(up_shard, 1), core_half(down_shard, 0)
-    return (
-        jnp.concatenate([up, shift(up, 2)], axis=1),
-        jnp.concatenate([down, shift(down, 2)], axis=0),
-    )
-
-
-def feed_gather(rows):
-    count = lax.axis_size("uly")
-    pair = lax.ppermute(rows, "uly", [(z, z ^ 1) for z in range(count)])
-    return jnp.concatenate([rows, swap(rows, 1), pair, swap(pair, 1)], axis=0)
-
-
 def feed_scatter(up_sum, down_sum):
     def settle(array, dim):
         half = array.shape[dim] // 2
@@ -1310,10 +2032,11 @@
     return settle(up_sum, 1), settle(down_sum, 0)
 
 
-def middle(tokens, out_grad, gain_two, mixed, w_out, up_weight, down_weight):
+def middle(tokens, out_grad, douts, gains, mixed, w_out, up_weight, down_weight):
     micro, rows, width = tokens.shape
     own = micro * rows
     if not is_cube():
+        gain_two = gains[1]
         hidden = tokens.astype(F32) + collect(
             jnp.stack([dot_nn(mixed[m], w_out) for m in range(micro)])
         )
@@ -1333,89 +2056,91 @@
         grad_hidden = out_grad.astype(F32) + norm_back(grad_two * gain_two, hat, scale)
         wide_att = spread(grad_hidden.astype(BF))
         grad_mixed = jnp.stack([dot_nt(wide_att[m], w_out) for m in range(micro)])
-        return block_out, up_grad, down_grad, gain_part, grad_hidden, wide_att, grad_mixed
-    up, down = feed_shards(up_weight, down_weight)
-    douts = feed_gather(to_chips(out_grad).reshape(own, width))
-    rows_sum, ups, downs = add_rows(mixed, w_out, up, down)
-    hidden = to_chips(tokens).reshape(own, width).astype(F32) + rows_sum
-    block_out, grad_hidden, gain_part, up_part, down_part = feed_all(
-        hidden, douts, to_chips(gain_two[None]), ups, downs
+        part = dot_tn(
+            mixed.reshape(-1, mixed.shape[2]), wide_att.reshape(-1, wide_att.shape[2]), BF
+        )
+        return block_out, up_grad, down_grad, gain_part, grad_hidden, grad_mixed, part
+    hidden, ups, downs = add_rows(mixed, w_out, tokens.reshape(own, width), up_weight, down_weight)
+    keep, give, grad_hidden, rows_bf, gain_part, up_part, down_part = feed_all(
+        hidden, douts, gains, ups, downs
     )
-    wide_att, grad_mixed, up_sum, down_sum = fan_out(
-        grad_hidden.astype(BF), w_out, up_part, down_part
-    )
+    grad_mixed, part, up_sum, down_sum = fan_out(rows_bf, w_out, mixed, up_part, down_part)
     up_grad, down_grad = feed_scatter(up_sum, down_sum)
     return (
-        to_chips(block_out).reshape(micro, rows, width),
+        (keep, give),
         up_grad,
         down_grad,
-        to_chips(gain_part)[0],
-        to_chips(grad_hidden).reshape(micro, rows, width),
-        wide_att,
+        gain_part,
+        grad_hidden,
         grad_mixed,
+        part,
     )
 
 
-def close_rows(xa, xb, w_first, w_second, ga, gb, out_grad):
+def close_rows(xa, xb, w_first, w_second, one, tokens, grad_hidden, gains, gain_two):
     micro, wide, na = xa.shape
     nb = xb.shape[2]
     width = w_first.shape[0]
+    flat_a, flat_b = xa.reshape(micro * wide, na), xb.reshape(micro * wide, nb)
+    flat_one = one.reshape(micro * wide, width)
     if not is_cube():
         partial = jnp.stack(
             [dot_nt(xa[m], w_first) + dot_nt(xb[m], w_second) for m in range(micro)]
         )
+        grad_one = collect(partial)
+        hat, scale = normed(tokens.astype(F32))
+        both_gains = jnp.stack([jnp.sum(grad_one * hat, axis=(0, 1)), gain_two])
+        total = lax.psum_scatter(both_gains, BLK, scatter_dimension=1, tiled=True)
         return (
-            collect(partial),
-            lax.psum_scatter(ga, BLK, scatter_dimension=0, tiled=True),
-            lax.psum_scatter(gb, BLK, scatter_dimension=0, tiled=True),
-            lax.psum_scatter(out_grad, BLK, scatter_dimension=1, tiled=True),
+            grad_hidden + norm_back(grad_one * gains[0], hat, scale),
+            lax.psum_scatter(dot_tn(flat_one, flat_a, BF), BLK, scatter_dimension=0, tiled=True),
+            lax.psum_scatter(dot_tn(flat_one, flat_b, BF), BLK, scatter_dimension=0, tiled=True),
+            lax.psum(total, "uly"),
         )
     count = lax.axis_size("uly")
     rows = wide // count
     piece = width // 8
-    no = out_grad.shape[0]
-    core = lax.axis_index("core")
-    pieces_o = jnp.stack(
-        [
-            lax.dynamic_slice_in_dim(out_grad, (2 * k + (core ^ j)) * piece, piece, 1)
-            for j in range(2)
-            for k in range(4)
-        ]
-    )
     out = call(
         close_rows_kernel,
         3,
-        [vmem()] * 4 + [anywhere()] * 3,
+        [vmem()] * 9,
         [
             ((micro * rows, width), F32, vmem()),
             ((piece, na), BF, vmem()),
             ((piece, nb), BF, vmem()),
-            ((no, piece), BF, vmem()),
+            ((8, piece), F32, vmem()),
         ],
         line_scratch(count, micro * rows, width)
         + [
             pltpu.VMEM((4, piece, na), BF),
             pltpu.VMEM((4, piece, nb), BF),
-            pltpu.VMEM((4, no, piece), BF),
+            pltpu.VMEM((2, piece, na), BF),
+            pltpu.VMEM((2, piece, nb), BF),
             pltpu.VMEM((7, piece, na), BF),
             pltpu.VMEM((7, piece, nb), BF),
-            pltpu.VMEM((7, no, piece), BF),
+            pltpu.VMEM((1, width), F32),
+            pltpu.VMEM((8, 8, piece), F32),
+            pltpu.VMEM((8, 8, piece), F32),
+            pltpu.VMEM((4, 8, piece), F32),
             sems(2, count - 1),
             sems(2, count - 1),
-            sems(3, 7),
-            sems(3, 7),
-            sems(3),
+            sems(2, 7),
+            sems(2, 7),
+            sems(6),
+            sems(6),
         ],
-        2 * micro * wide * width * (na + nb),
-        xa,
-        xb,
+        4 * micro * wide * width * (na + nb),
+        flat_a,
+        flat_b,
         w_first,
         w_second,
-        ga.reshape(8, piece, na),
-        gb.reshape(8, piece, nb),
-        pieces_o,
+        flat_one,
+        tokens.reshape(micro * rows, width),
+        grad_hidden,
+        gains,
+        gain_two,
     )
-    return out[0].reshape(micro, rows, width), out[1], out[2], out[3]
+    return out[0].reshape(micro, rows, width), *out[1:]
 
 
 def feed(norm_two, out_rows, pair):
@@ -1437,6 +2162,70 @@
         by_owner(dot_tn(norm_two, grad_up, BF)),
         by_owner(dot_tn(out_rows, act, BF)),
     )
+
+
+def plain_forward(rates, lengths, a, v_high, gate):
+    micro, length = a.shape[:2]
+    heads_here = rates.shape[0]
+    cut_v = v_high.shape[2]
+    qk = (a.shape[2] - cut_v) // 2
+    hd, vd = qk // heads_here, 2 * cut_v // heads_here
+    sets, parts, states = [], [], []
+    for m in range(micro):
+        values = jnp.concatenate([a[m, :, 2 * qk :], v_high[m]], axis=1)
+        heads = [
+            (
+                a[m, :, h * hd : (h + 1) * hd],
+                a[m, :, qk + h * hd : qk + (h + 1) * hd],
+                values[:, h * vd : (h + 1) * vd],
+            )
+            for h in range(heads_here)
+        ]
+        part = decay_parts(rates, lengths[m], length)
+        states.append(retention_state(heads, part[2]))
+        sets.append(heads)
+        parts.append(part)
+
+    all_states = exchange(states)
+    state_in, retained, mixed = [], [], []
+    for m in range(micro):
+        state = state_sum(parts[m][3], all_states[m])
+        kept = retention(sets[m], parts[m], state)
+        state_in.append(state)
+        retained.append(kept)
+        mixed.append(mix(gate[m], kept))
+    mixed = jnp.stack(mixed)
+    return mixed, (sets, parts, state_in, retained)
+
+
+def plain_backward(gate, kept, grad_mixed):
+    sets, parts, state_in, retained = kept
+    micro, cut_v = len(sets), gate.shape[2] // 2
+    grad_gates, grad_rets, grad_states = [], [], []
+    for m in range(micro):
+        gg, gr = mix_back(gate[m], retained[m], grad_mixed[m])
+        grad_gates.append(gg)
+        grad_rets.append(gr)
+        grad_states.append(
+            jnp.stack(
+                [
+                    dot_tn((q.astype(F32) * parts[m][1][h]).astype(BF), gr[h], BF)
+                    for h, (q, k, v) in enumerate(sets[m])
+                ]
+            )
+        )
+    all_back = exchange(grad_states)
+    xa, xb = [], []
+    for m in range(micro):
+        back = state_sum(parts[m][4], all_back[m])
+        grads = retention_back(sets[m], parts[m], state_in[m], grad_rets[m], back)
+        gq = jnp.concatenate([g[0] for g in grads], axis=1)
+        gk = jnp.concatenate([g[1] for g in grads], axis=1)
+        gv = jnp.concatenate([g[2] for g in grads], axis=1)
+        xa.append(jnp.concatenate([gq, gk, gv[:, :cut_v]], axis=1))
+        xb.append(jnp.concatenate([gv[:, cut_v:], grad_gates[m]], axis=1))
+    xa, xb = jnp.stack(xa), jnp.stack(xb)
+    return xa, xb
 
 
 def body(
@@ -1458,106 +2247,53 @@
     heads_here = decay_rate.shape[0] // lax.axis_size("uly")
     rates = lax.dynamic_slice_in_dim(decay_rate, lax.axis_index("uly") * heads_here, heads_here)
     qk = query_weight.shape[1]
-    hd = qk // heads_here
-    vd = value_weight.shape[1] // heads_here
     cut_v = value_weight.shape[1] // 2
 
-    first = jnp.concatenate([query_weight, key_weight, value_weight[:, :cut_v]], axis=1)
-    second = jnp.concatenate([value_weight[:, cut_v:], gate_matrix], axis=1)
-    one, a, v_high, gate, w_first, w_second, w_out, gains = project(
-        tokens, jnp.stack([retain_gain, feed_gain]), first, second, output_weight
+    one, a, v_high, gate, w_first, w_second, w_out, gains, up, down = project(
+        tokens,
+        (retain_gain, feed_gain),
+        (query_weight, key_weight, value_weight, gate_matrix),
+        output_weight,
+        up_weight,
+        down_weight,
     )
-    gain_one, gain_two = gains[0].astype(F32), gains[1].astype(F32)
-    length = one.shape[1]
-
-    sets, parts, states = [], [], []
-    for m in range(micro):
-        values = jnp.concatenate([a[m, :, 2 * qk :], v_high[m]], axis=1)
-        heads = [
-            (
-                a[m, :, h * hd : (h + 1) * hd],
-                a[m, :, qk + h * hd : qk + (h + 1) * hd],
-                values[:, h * vd : (h + 1) * vd],
-            )
-            for h in range(heads_here)
-        ]
-        part = decay_parts(rates, lengths[m], length)
-        states.append(retention_state(heads, part[2]))
-        sets.append(heads)
-        parts.append(part)
-
-    all_states = exchange(states)
-    state_in, retained, mixed = [], [], []
-    for m in range(micro):
-        state = state_sum(parts[m][3], all_states[m])
-        kept = retention(sets[m], parts[m], state)
-        state_in.append(state)
-        retained.append(kept)
-        mixed.append(mix(gate[m], kept))
-    mixed = jnp.stack(mixed)
-
-    block_out, up_grad, down_grad, gain_two_part, grad_hidden, wide_att, grad_mixed = middle(
-        tokens, out_grad, gain_two, mixed, w_out, up_weight, down_weight
+    if is_cube():
+        coef, coef_back = chip_weights(rates, lengths, one.shape[1])
+        mixed, kept, state, douts, up, down = retain(
+            rates, lengths, coef, a, v_high, gate, out_grad.reshape(micro * rows, width), up, down
+        )
+    else:
+        mixed, kept = plain_forward(rates, lengths, a, v_high, gate)
+        douts = None
+
+    block_out, up_grad, down_grad, gain_two, grad_hidden, grad_mixed, part = middle(
+        tokens, out_grad, douts, gains, mixed, w_out, up, down
     )
 
-    grad_gates, grad_rets, grad_states = [], [], []
-    for m in range(micro):
-        gg, gr = mix_back(gate[m], retained[m], grad_mixed[m])
-        grad_gates.append(gg)
-        grad_rets.append(gr)
-        grad_states.append(
-            jnp.stack(
-                [
-                    dot_tn((q.astype(F32) * parts[m][1][h]).astype(BF), gr[h], BF)
-                    for h, (q, k, v) in enumerate(sets[m])
-                ]
-            )
+    if is_cube():
+        xa, xb, out_sum, block_out = retain_back(
+            rates, lengths, coef_back, a, v_high, gate, kept, grad_mixed, state, part, *block_out
         )
-    all_back = exchange(grad_states)
-
-    def flat(array):
-        return array.reshape(micro * length, array.shape[-1])
-
-    out_part = dot_tn(flat(mixed), flat(wide_att), BF)
-
-    xa, xb = [], []
-    for m in range(micro):
-        back = state_sum(parts[m][4], all_back[m])
-        grads = retention_back(sets[m], parts[m], state_in[m], grad_rets[m], back)
-        gq = jnp.concatenate([g[0] for g in grads], axis=1)
-        gk = jnp.concatenate([g[1] for g in grads], axis=1)
-        gv = jnp.concatenate([g[2] for g in grads], axis=1)
-        xa.append(jnp.concatenate([gq, gk, gv[:, :cut_v]], axis=1))
-        xb.append(jnp.concatenate([gv[:, cut_v:], grad_gates[m]], axis=1))
-    xa, xb = jnp.stack(xa), jnp.stack(xb)
-    grad_one, first_sum, second_sum, out_sum = close_rows(
-        xa,
-        xb,
-        w_first,
-        w_second,
-        dot_tn(flat(one), flat(xa), BF),
-        dot_tn(flat(one), flat(xb), BF),
-        out_part,
+        block_out = block_out.reshape(tokens.shape)
+        out_sum = out_sum.T
+    else:
+        xa, xb = plain_backward(gate, kept, grad_mixed)
+        out_sum = lax.psum_scatter(part, BLK, scatter_dimension=1, tiled=True)
+
+    input_grad, first_sum, second_sum, gain_sums = close_rows(
+        xa, xb, w_first, w_second, one, tokens, grad_hidden, gains, gain_two
     )
-    hat, scale = normed(tokens.astype(F32))
-    input_grad = grad_hidden + norm_back(grad_one * gain_one, hat, scale)
-    gain_one_part = jnp.sum(grad_one * hat, axis=(0, 1))
-
-    total = lax.psum_scatter(
-        jnp.stack([gain_one_part, gain_two_part]), BLK, scatter_dimension=1, tiled=True
-    )
-    total = lax.psum(total, "uly")
     first_sum, second_sum = first_sum.astype(F32), second_sum.astype(F32)
     return (
         block_out,
         input_grad,
-        total[0],
+        gain_sums[0],
         first_sum[:, :qk],
         first_sum[:, qk : 2 * qk],
         jnp.concatenate([first_sum[:, 2 * qk :], second_sum[:, :cut_v]], axis=1),
         second_sum[:, cut_v:],
         out_sum.astype(F32),
-        total[1],
+        gain_sums[1],
         up_grad,
         down_grad,
     )

time: 877 us -> 654 us (0.75)
  waiting for transfers between devices: 155 us -> 0.01 us
  Pallas kernels: 497 us -> 614 us
  matrix products: 64.8 us -> 0 us
  other arithmetic: 61.9 us -> 8.53 us
  local copies, waits for them, and re-layouts: 44.9 us -> 20.3 us
  starting transfers between devices: 19.2 us -> 3.47 us
  blocking collectives: 11.7 us -> 0 us
  between operations: 16.1 us -> 4.98 us
    pallas_call x5 -> x7, Pallas kernels: 497 us -> 614 us  [call(): pl.pallas_call(kernel, out_shape=[like(s, t) for s, t, _ in outs], in_spe...]
    ppermute x4 -> x2, waiting for transfers between devices: 66.9 us -> 0.01 us  [shift(): lax.ppermute(array, 'uly', [(z, (z + step) % count) for z in range(count)])]
    dot_general x55 -> x0, matrix products: 64.8 us -> none  [the longest x19 40.9 us: dot_tn(): lax.dot_general(left, right, (((0,), (0,)), ((), ())), preferred_element_...]
    ppermute x13 -> x0, waiting for transfers between devices: 54.5 us -> none  [the longest x12 48.3 us: swap(): lax.ppermute(array, 'chip', [(b, b ^ mask // 2) for b in range(count)])]
    unnamed x2 -> x0, waiting for transfers between devices: 32.6 us -> none
    concatenate x12 -> x0, other arithmetic: 14.6 us -> none  [the longest x5 5.36 us: to_chips(): jnp.concatenate([lax.dynamic_slice_in_dim(array, (chip ^ k) * width, widt...]
    unnamed x164 -> x15, local copies, waits for them, and re-layouts: 17.8 us -> 3.62 us
    psum x1 -> x0, blocking collectives: 11.7 us -> none  [body(): total = lax.psum(total, 'uly')]
  transfers between devices with their start and end apart: 40 -> 4, of which waited for: 13 -> 0; matrix products, arithmetic and copies ran while one was open for 11% -> 2% of each run, Pallas kernels for 12% -> 27%
where the time goes in v3:
time: 654 us; the launch traced here: 651 us
  Pallas kernels  614 us (94%)
  local copies, waits for them, and re-layouts  20.3 us (3%)
  other arithmetic  8.53 us (1%)
    pallas_call x7, Pallas kernels, call(): pl.pallas_call(kernel, out_shape=[like(s, t) for s, t, _ in outs], in_spe...  614 us
  transfers between devices with their start and end apart: 4, of which 0 were waited for; matrix products, arithmetic and copies ran while one was open for 2% of the time, Pallas kernels for 27%

profile of v3, /device:TPU:0, one launch (start us, length us, event | category | flops | bytes accessed | tf_op | source)
XLA Modules:
  0.0 651.3 jit_solution(17448809504245174774)
XLA Ops:
  0.7 0.8 slice_bitcast_fusion
  1.8 0.6 fusion.19
  2.4 0.6 fusion.20
  3.0 0.6 gather_fusion.3
  3.6 0.6 gather_fusion.2
  4.3 0.6 gather_fusion.1
  4.9 0.6 gather_fusion
  9.4 0.7 fusion.12
  10.6 1.2 broadcast_in_dim.103.gain_one_ref
  11.8 1.2 broadcast_in_dim.104.gain_two_ref
  13.5 0.6 pad_maximum_fusion.2.coef_ref
  14.1 120.6 %shard_map.212 = (bf16[2,512,2048]{2,1,0:T(8,128)(2,1)}, bf16[2,512,1536]{2,1,0:T(8,128)(2,1)}, bf16[2,512,512]{2,1,0:T(8,128)(2,1)}, f32[2,512,1024]{2,1,0:T(8,...) custom-call(bf16[256,2048]{1,0:T(8,128)(2,1)} %bitcast.56, ...), custom_call_target="tpu_custom_call" | custom-call | flops 12884901888 | bytes 4195328 | tf_op jit(solution)/shard_map/pallas_call | solution.py:1702
  134.7 57.3 %shard_map.213 = (bf16[2,512,1024]{2,1,0:T(8,128)(2,1)}, f32[2,512,1024]{2,1,0:T(8,128)}, bf16[2,2,256,512]{3,2,1,0:T(8,128)(2,1)}, bf16[1024,2048]{1,0:T(8,128)...) custom-call(f32[2]{0:T(128)} %copy-done.5, s32[2,2]{1,0:T(2,128)} %lengths_ref.3, ...), custom_call_target="tpu_custom_call" | custom-call | flops 1610612736 | bytes 10485912 | tf_op jit(solution)/shard_map/pallas_call | solution.py:1702
  192.0 92.3 %shard_map.214 = (f32[256,2048]{1,0:T(8,128)}, bf16[2048,1024]{1,0:T(8,128)(2,1)}, bf16[1024,2048]{1,0:T(8,128)(2,1)}) custom-call(bf16[2,512,1024]{2,1,0:T(8,128)(2,1)} %get-tuple-element.55.x_ref.mixed_ref, bf16[1024,2048]{1,0:T(8,128)(2,1)} %get-tuple-element.56.w_ref, bf16[256,2048]{1,0:T(8,128)(2,1)} %bitcast.57, ...), custom_call_target="tpu_custom_call" | custom-call | flops 4294967296 | bytes 9437184 | tf_op jit(solution)/shard_map/pallas_call | solution.py:1702
  284.3 78.1 %shard_map.215 = (f32[256,2048]{1,0:T(8,128)}, bf16[256,2048]{1,0:T(8,128)(2,1)}, f32[256,2048]{1,0:T(8,128)}, bf16[256,2048]{1,0:T(8,128)(2,1)}, f32[1,2048]{1,...) custom-call(f32[256,2048]{1,0:T(8,128)} %get-tuple-element.59.hid_ref, ...), custom_call_target="tpu_custom_call" | custom-call | flops 25769803776 | bytes 14745600 | tf_op jit(solution)/shard_map/pallas_call | solution.py:1702
  362.4 88.1 %shard_map.216 = (f32[2,512,1024]{2,1,0:T(8,128)}, bf16[8,256,1024]{2,1,0:T(8,128)(2,1)}, bf16[512,1024]{1,0:T(8,128)(2,1)}, bf16[1024,512]{1,0:T(8,128)(2,1)}) custom-call(bf16[256,2048]{1,0:T(8,128)(2,1)} %get-tuple-element.64.rows_ref, bf16[1024,2048]{1,0:T(8,128)(2,1)} %get-tuple-element.56.w_ref, ...), custom_call_target="tpu_custom_call" | custom-call | flops 8589934592 | bytes 15728640 | tf_op jit(solution)/shard_map/pallas_call | solution.py:1702
  450.5 1.9 slice.49
  452.4 1.9 slice.51
  454.3 2.9 collective-permute-start.2
  458.1 73.7 %shard_map.217 = (bf16[2,512,1536]{2,1,0:T(8,128)(2,1)}, bf16[2,512,1536]{2,1,0:T(8,128)(2,1)}, bf16[256,1024]{1,0:T(8,128)(2,1)}, bf16[256,2048]{1,0:T(8,128)(2,1)}) custom-call(f32[2]{0:T(128)} %copy-done.5, s32[2,2]{1,0:T(2,128)} %lengths_ref.3, f32[2,2,8]{2,1,0:T(2,128)} %pad_maximum_fusion.1.coef_ref, bf16[2,512,1536]{2,1,0:T(8,128)(2,1)} %get-tuple-element.49.a_ref, ...), custom_call_target="tpu_custom_call" | custom-call | flops 4831838208 | bytes 25165976 | tf_op jit(solution)/shard_map/pallas_call | solution.py:1702
  531.9 103.9 %shard_map.218 = (f32[256,2048]{1,0:T(8,128)}, bf16[256,1536]{1,0:T(8,128)(2,1)}, bf16[256,1536]{1,0:T(8,128)(2,1)}, f32[8,256]{1,0:T(8,128)}) custom-call(bf16[1024,1536]{1,0:T(8,128)(2,1)} %bitcast.54, bf16[1024,1536]{1,0:T(8,128)(2,1)} %bitcast.55, bf16[2048,1536]{1,0:T(8,128)(2,1)} %get-tuple-element.75.wa_ref, ...), custom_call_target="tpu_custom_call" | custom-call | flops 25769803776 | bytes 26288128 | tf_op jit(solution)/shard_map/pallas_call | solution.py:1702
  635.8 2.4 fusion.17
  638.3 1.3 fusion.18
  639.7 1.1 slice.64
  640.8 1.3 copy.62
  642.1 1.1 pad_maximum_fusion
  643.2 1.3 add_convert_fusion.1
  644.6 1.2 add_convert_fusion
  646.5 1.1 maximum_convert_fusion
  647.8 1.0 maximum_convert_fusion.1
  648.8 1.0 copy.65
  649.8 1.3 copy.66
  (53 shorter events, 3.2 us)
Async XLA Ops:
  10.2 124.5 %copy-start.5 = (f32[2]{0:T(128)}, f32[2]{0:T(128)S(1)}, u32[]{:S(2)}) copy-start(f32[2]{0:T(128)S(1)} %get-tuple-element.123.rates_ref) | copy-start | bytes 28
  452.4 190.8 %collective-permute-start = (bf16[512,512]{1,0:T(8,128)(2,1)}, bf16[512,512]{1,0:T(8,128)(2,1)}, u32[]{:S(2)}, u32[]{:S(2)}) collective-permute-start(bf16[512,512]{1,0:T(8,128)(2,1)} %slice.49), channel_id=1, source_target_pairs={{0,2},{1,3},{2,0},{3,1},{4,6},{5,7},{6,4},{7,5},{8,10},{9,11},{10,... | collective-permute-start | bytes 1572872 | tf_op jit(solution)/shard_map/ppermute | solution.py:53
  454.3 190.4 %collective-permute-start.2 = (bf16[512,512]{1,0:T(8,128)(2,1)}, bf16[512,512]{1,0:T(8,128)(2,1)}, u32[]{:S(2)}, u32[]{:S(2)}) collective-permute-start(bf16[512,512]{1,0:T(8,128)(2,1)} %slice.51), channel_id=1, source_target_pairs={{0,2},{1,3},{2,0},{3,1},{4,6},{5,7},{6,4},{7,5},{8,10},{9,11},{10,... | collective-permute-start | bytes 1572872 | tf_op jit(solution)/shard_map/ppermute | solution.py:53
  531.9 106.3 %copy-start.4 = (bf16[256,1024]{1,0:T(8,128)(2,1)S(1)}, bf16[256,1024]{1,0:T(8,128)(2,1)}, u32[]{:S(2)}) copy-start(bf16[256,1024]{1,0:T(8,128)(2,1)} %get-tuple-element.84) | copy-start | bytes 1572868
  635.8 3.8 copy-start
  639.7 4.9 copy-start.2
  644.5 4.3 copy-start.3
  644.5 1.9 collective-permute-start.1
  645.9 3.9 copy-start.1
  645.9 1.7 collective-permute-start.3

commit v4 on v3

--- a/solution.py
+++ b/solution.py
@@ -255,7 +255,7 @@
     return pl.BlockSpec(memory_space=pl.ANY)
 
 
-def greet(plane=False, line=False, cores=False, pair=False, across=False, whole=False):
+def greet(plane=False, line=False, cores=False, pair=False, across=False, whole=False, every=False):
     barrier = pltpu.get_barrier_semaphore()
     chip, core, z = (lax.axis_index(a) for a in AXES)
     others = []
@@ -269,6 +269,8 @@
         others.append({"uly": z ^ 2})
     if whole:
         others += [{"uly": z ^ k} for k in range(1, 4)]
+    if every:
+        others += [{"chip": chip ^ (p % 4), "core": core ^ (p // 4)} for p in range(1, 8)]
     for to in others:
         pl.semaphore_signal(barrier, inc=1, device_id=to, device_id_type=MESH)
     count = len(others)
@@ -505,10 +507,12 @@
     return pl.ds(pl.multiple_of((place % 4) * (2 * width) + (core ^ (place // 4)) * width, width), width)
 
 
-def project_kernel(
+def front_kernel(
+    rates_ref,
+    lengths_ref,
     tok_ref,
-    gain_one_ref,
-    gain_two_ref,
+    dout_ref,
+    gain_ref,
     q_hbm,
     k_hbm,
     v_hbm,
@@ -526,6 +530,10 @@
     gains_ref,
     up_own_hbm,
     down_own_hbm,
+    mixed_ref,
+    kept_ref,
+    state_ref,
+    douts_ref,
     slots,
     wa,
     wb,
@@ -536,14 +544,17 @@
     zrecv,
     fsend,
     frecv,
+    dsend,
+    drecv,
     lsem,
+    *state_refs,
 ):
     core, z = lax.axis_index("core"), lax.axis_index("uly")
     rows = tok_ref.shape[0] // 2
     width = tok_ref.shape[1]
     piece = width // 8
     qk, high = q_hbm.shape[1], high_ref.shape[2]
-    greet(plane=True, line=True, cores=True)
+    greet(plane=True, line=True, cores=True, across=True)
     line = LineGather(slots, zsend, zrecv)
     slots[z] = tok_ref[...]
     line.pass_on(0)
@@ -564,8 +575,7 @@
     for c in local:
         c.start()
     gains[0] = jnp.zeros_like(gains[0])
-    gains[0, 0:1, :] = gain_one_ref[...].astype(F32)
-    gains[0, 1:2, :] = gain_two_ref[...].astype(F32)
+    gains[0, 0:2, :] = gain_ref[...]
     items = [
         PlaneGather(gains.at[0], lambda p: gains.at[p], True, psend.at[0], precv.at[0])
     ]
@@ -615,6 +625,29 @@
         remote(0, up_hbm.at[:, theirs], up_own_hbm.at[here, first_half], {"core": 1 - core}),
         remote(1, down_hbm.at[theirs], down_own_hbm.at[first_half, here], {"core": 1 - core}),
     ]
+    first_wide, second_wide = up_own_hbm.at[:, first_half], up_own_hbm.at[:, pl.ds(units, units)]
+    first_tall, second_tall = down_own_hbm.at[first_half], down_own_hbm.at[pl.ds(units, units)]
+    away = [
+        remote(2, first_wide, second_wide, {"uly": z ^ 2}),
+        remote(3, first_tall, second_tall, {"uly": z ^ 2}),
+    ]
+    own_rows = 2 * rows
+
+    def rows_to(i, src, dst, to):
+        return pltpu.make_async_remote_copy(
+            src_ref=douts_ref.at[pl.ds(src * own_rows, own_rows)],
+            dst_ref=douts_ref.at[pl.ds(dst * own_rows, own_rows)],
+            send_sem=dsend.at[i],
+            recv_sem=drecv.at[i],
+            device_id=to,
+            device_id_type=MESH,
+        )
+
+    send_rows = [
+        rows_to(0, 0, 2, {"uly": z ^ 1}),
+        rows_to(1, 0, 1, {"core": 1 - core}),
+        rows_to(2, 2, 3, {"core": 1 - core}),
+    ]
     for c in cut:
         c.start()
     for c in local[:5]:
@@ -650,6 +683,10 @@
                         (src - mean) * scale * gains[p, 0:1, :]
                     ).astype(BF)
 
+    for k in range(4):
+        douts_ref[0:own_rows, k * 2 * piece : (k + 1) * 2 * piece] = dout_ref[
+            :, chip_chunk(k, 2 * piece)
+        ]
     normalize(z)
     line.take(1, normalize)
     for item in items[1:3]:
@@ -700,16 +737,35 @@
         normalize(slot)
         multiply(slot)
 
-    line.take(3, both_steps)
+    line.take(3, lambda slot: None)
+    for c in cut:
+        c.wait()
+    for c in give:
+        c.wait()
+    for c in away:
+        c.start()
+    send_rows[0].start()
+    line.each(3, both_steps)
     for item in items[3:]:
         item.corner()
     for item in items[3:]:
         item.finish()
     line.finish()
+    retain_part(
+        rates_ref,
+        lengths_ref,
+        first_ref,
+        high_ref,
+        gate_ref,
+        mixed_ref,
+        kept_ref,
+        state_ref,
+        douts_ref,
+        send_rows,
+        *state_refs,
+    )
     local[5].wait()
-    for c in outs + cut:
-        c.wait()
-    for c in give:
+    for c in outs + away:
         c.wait()
 
 
@@ -859,7 +915,9 @@
     for g in groups:
         g.first_sums(1)
     line.take(3, multiply)
-    part_ref[...] = total[...].astype(BF)
+    half = part_ref.shape[3]
+    for i in range(2):
+        part_ref[i] = total[:, :, i * half : (i + 1) * half].astype(BF)
     groups[0].finish(up_ref)
     groups[1].finish(down_ref)
     line.finish()
@@ -1113,7 +1171,7 @@
     rows = out_ref.shape[0] // 2
     length = one_ref.shape[0] // 2
     width = out_ref.shape[1] // 8
-    greet(plane=True, cores=True, whole=True)
+    greet(every=True, whole=True)
 
     def make(a, to):
         at = [
@@ -1215,28 +1273,31 @@
             device_id_type=MESH,
         )
 
-    sent = []
-    for i, (count, to) in enumerate(
-        ((4, {"core": 1 - core}), (2, {"chip": chip ^ 2}), (1, {"chip": chip ^ 1}))
-    ):
-        c = pass_small(
-            i, small.at[pl.ds(count, count)], small_came.at[pl.ds(count, count)], to
+    sent = [
+        pass_small(
+            p - 1,
+            small.at[p],
+            small_came.at[p],
+            {"chip": chip ^ (p % 4), "core": core ^ (p // 4)},
         )
+        for p in range(1, 8)
+    ]
+    for c in sent:
         c.start()
-        if i == 0:
-            for group, *_ in sets:
-                group.first_sums(1)
-        c.wait_recv()
-        small[0:count] = small[0:count] + small_came[count : 2 * count]
-        sent.append(c)
+    for group, *_ in sets:
+        group.first_sums(1)
+    total = small[0]
+    for p in range(1, 8):
+        sent[p - 1].wait_recv()
+        total = total + small_came[p]
+    small_line[0] = total
     last = [
-        pass_small(2 + k, small.at[0], small_line.at[k], {"uly": z ^ k}) for k in range(1, 4)
+        pass_small(6 + k, small_line.at[0], small_line.at[k], {"uly": z ^ k}) for k in range(1, 4)
     ]
     for c in last:
         c.start()
     for (group, *_), out in zip(sets, (sum_a_ref, sum_b_ref)):
         group.finish(out)
-    total = small[0]
     for k in range(1, 4):
         last[k - 1].wait_recv()
         total = total + small_line[k]
@@ -1246,9 +1307,9 @@
 
 
 class StateExchange:
-    def __init__(self, coef_ref, own, sib, chips, mine, came, final, send, recv):
+    def __init__(self, weights, own, sib, chips, mine, came, final, send, recv):
         self.core = lax.axis_index("core")
-        self.coef, self.own, self.sib, self.chips = coef_ref, own, sib, chips
+        self.weights, self.own, self.sib, self.chips = weights, own, sib, chips
         self.mine, self.came, self.final = mine, came, final
 
         def copy(i, src, dst):
@@ -1277,9 +1338,9 @@
         self.first.wait_recv()
         m = self.core
         for h in range(2):
+            mine, other = self.weights.joined(m, h)
             self.chips[0, h] = (
-                self.coef[m, h, 0] * self.own[m, h].astype(F32)
-                + self.coef[m, h, 1] * self.sib[m, h].astype(F32)
+                mine * self.own[m, h].astype(F32) + other * self.sib[m, h].astype(F32)
             ).astype(BF)
             self.items[h].start()
 
@@ -1296,9 +1357,9 @@
             item.corner()
         m = self.core
         for h in range(2):
-            total = self.coef[m, h, 5] * self.chips[1, h].astype(F32)
+            total = self.weights.chip(m, h, 1) * self.chips[1, h].astype(F32)
             for k in (2, 3):
-                total = total + self.coef[m, h, 4 + k] * self.chips[k, h].astype(F32)
+                total = total + self.weights.chip(m, h, k) * self.chips[k, h].astype(F32)
             self.mine[h] = total.astype(BF)
         self.second.start()
         self.last(m, self.mine)
@@ -1307,9 +1368,9 @@
 
     def last(self, m, chip_state):
         for h in range(2):
+            whole, other = self.weights.final(m, h)
             self.final[m, h] = (
-                self.coef[m, h, 2] * chip_state[h].astype(F32)
-                + self.coef[m, h, 3] * self.sib[m, h].astype(F32)
+                whole * chip_state[h].astype(F32) + other * self.sib[m, h].astype(F32)
             ).astype(BF)
 
     def finish(self):
@@ -1370,25 +1431,71 @@
         return jnp.where(same, jnp.exp(-rate * (self.length - 1 - at).astype(F32)), 0.0)
 
 
+def rate_of(rates_ref, h):
+    return rates_ref[lax.axis_index("uly") * 2 + h]
+
+
+class StateWeights:
+    def __init__(self, rates_ref, lengths_ref, length, back):
+        self.rates, self.lengths, self.length, self.back = rates_ref, lengths_ref, length, back
+        self.chip_at, self.core = lax.axis_index("chip"), lax.axis_index("core")
+
+    def end(self, m, block):
+        at = jnp.full((1, 1), (block + 1) * self.length - 1, jnp.int32)
+        found = jnp.zeros_like(at)
+        total = 0
+        for n in range(self.lengths.shape[1]):
+            found = found + jnp.where(at >= total, 1, 0)
+            total = total + self.lengths[m, n]
+        return found
+
+    def decay(self, h, count):
+        far = jnp.full((1, 1), count * self.length, jnp.int32).astype(F32)
+        return jnp.exp(-rate_of(self.rates, h) * far)
+
+    def through(self, m, h, block):
+        same = self.end(m, block) == self.end(m, block - 1)
+        return jnp.where(same, self.decay(h, 1), 0.0)
+
+    def pick(self, first, second):
+        return jnp.where(jnp.full((1, 1), self.core, jnp.int32) == 0, first, second)
+
+    def joined(self, m, h):
+        one = jnp.ones((1, 1), F32)
+        if self.back:
+            even = self.through(m, h, 2 * self.chip_at)
+            return self.pick(one, even), self.pick(even, one)
+        odd = self.through(m, h, 2 * self.chip_at + 1)
+        return self.pick(odd, one), self.pick(one, odd)
+
+    def final(self, m, h):
+        one, zero = jnp.ones((1, 1), F32), jnp.zeros((1, 1), F32)
+        if self.back:
+            return self.pick(self.through(m, h, 2 * self.chip_at + 1), one), self.pick(one, zero)
+        return self.pick(one, self.through(m, h, 2 * self.chip_at)), self.pick(zero, one)
+
+    def chip(self, m, h, k):
+        here, there = self.chip_at, self.chip_at ^ k
+        low, high = (here, there) if self.back else (there, here)
+        before = jnp.full((1, 1), low, jnp.int32) < jnp.full((1, 1), high, jnp.int32)
+        same = self.end(m, 2 * low + 1) == self.end(m, 2 * high - 1)
+        return jnp.where(before & same, self.decay(h, 2 * jnp.maximum(high - 1 - low, 0)), 0.0)
+
+
 ROWS = 128
 
 
-def retain_kernel(
+def retain_part(
     rates_ref,
     lengths_ref,
-    coef_ref,
     a_ref,
     high_ref,
     gate_ref,
-    dout_ref,
-    up_hbm,
-    down_hbm,
     mixed_ref,
     kept_ref,
     state_ref,
     douts_ref,
-    up_own_hbm,
-    down_own_hbm,
+    send_rows,
     own,
     sib,
     chips,
@@ -1396,61 +1503,13 @@
     came,
     send,
     recv,
-    ordered,
-    others,
-    dsend,
-    drecv,
-    fsend,
-    frecv,
-    lsem,
 ):
     _, length, vd = high_ref.shape
     qk = (a_ref.shape[2] - vd) // 2
     hd = qk // 2
-    greet(plane=True, cores=True, pair=True, across=True)
-    z = lax.axis_index("uly")
-    units = up_hbm.shape[1]
-    first_half, second_half = pl.ds(0, units), pl.ds(units, units)
-    keep, away = [], []
-    for i, (src, first, second) in enumerate(
-        (
-            (up_hbm, up_own_hbm.at[:, first_half], up_own_hbm.at[:, second_half]),
-            (down_hbm, down_own_hbm.at[first_half], down_own_hbm.at[second_half]),
-        )
-    ):
-        keep.append(pltpu.make_async_copy(src, first, lsem.at[i]))
-        away.append(
-            pltpu.make_async_remote_copy(
-                src_ref=src,
-                dst_ref=second,
-                send_sem=fsend.at[i],
-                recv_sem=frecv.at[i],
-                device_id={"uly": z ^ 2},
-                device_id_type=MESH,
-            )
-        )
-    for c in away + keep:
-        c.start()
-    quarter = ordered.shape[1] // 4
-    for k in range(4):
-        ordered[:, k * quarter : (k + 1) * quarter] = dout_ref[:, chip_chunk(k, quarter)]
-
-    def rows_to(i, src, to):
-        return pltpu.make_async_remote_copy(
-            src_ref=src,
-            dst_ref=others.at[i],
-            send_sem=dsend.at[i],
-            recv_sem=drecv.at[i],
-            device_id=to,
-            device_id_type=MESH,
-        )
-
-    other = {"core": 1 - lax.axis_index("core")}
-    to_pair = rows_to(1, ordered, {"uly": z ^ 1})
-    to_other = rows_to(0, ordered, other)
-    through = rows_to(2, others.at[1], other)
-    to_pair.start()
-    states = StateExchange(coef_ref, own, sib, chips, mine, came, state_ref, send, recv)
+    weights = StateWeights(rates_ref, lengths_ref, length, False)
+    states = StateExchange(weights, own, sib, chips, mine, came, state_ref, send, recv)
+    to_pair, to_other, through = send_rows
 
     def values(m, h):
         return high_ref[m] if h else a_ref[m, :, 2 * qk :]
@@ -1462,7 +1521,7 @@
 
         @pl.loop(0, 2)
         def _(m):
-            leave = Places(lengths_ref, m, length).leave(rates_ref[h], 0, length)
+            leave = Places(lengths_ref, m, length).leave(rate_of(rates_ref, h), 0, length)
             k = (keys(m, h).astype(F32) * leave).astype(BF)
             own[m, h] = dot_tn(k, values(m, h), BF)
 
@@ -1474,7 +1533,7 @@
         def _(i):
             m, r = i // parts, i % parts
             at = pl.ds(pl.multiple_of(r * ROWS, ROWS), ROWS)
-            table = Places(lengths_ref, m, length).table(rates_ref[h], r * ROWS, ROWS, False)
+            table = Places(lengths_ref, m, length).table(rate_of(rates_ref, h), r * ROWS, ROWS, False)
             q = a_ref[m, at, h * hd : (h + 1) * hd]
             scores = (dot_nt(q, keys(m, h)) * table).astype(BF)
             kept_ref[m, at, h * vd : (h + 1) * vd] = jnp.dot(
@@ -1497,7 +1556,7 @@
             m, r = i // parts, i % parts
             at = pl.ds(pl.multiple_of(r * ROWS, ROWS), ROWS)
             cols = slice(h * vd, (h + 1) * vd)
-            entry = Places(lengths_ref, m, length).entry(rates_ref[h], r * ROWS, ROWS)
+            entry = Places(lengths_ref, m, length).entry(rate_of(rates_ref, h), r * ROWS, ROWS)
             q = a_ref[m, at, h * hd : (h + 1) * hd]
             kept = kept_ref[m, at, cols] + entry * jnp.dot(
                 q, state_ref[m, h], preferred_element_type=F32
@@ -1507,16 +1566,10 @@
             mixed_ref[m, at, cols] = (g * sigmoid(g) * normed(kept)[0]).astype(BF)
 
     states.finish()
-    rows = ordered.shape[0]
-    douts_ref[0:rows, :] = ordered[...]
     to_other.wait_recv()
     through.wait_recv()
-    for i in range(3):
-        douts_ref[(1 + i) * rows : (2 + i) * rows, :] = others[i]
-    for c in (to_pair, to_other, through):
+    for c in send_rows:
         c.wait_send()
-    for c in keep + away:
-        c.wait()
 
 
 def sigmoid(v):
@@ -1526,7 +1579,6 @@
 def retain_back_kernel(
     rates_ref,
     lengths_ref,
-    coef_ref,
     a_ref,
     high_ref,
     gate_ref,
@@ -1536,10 +1588,14 @@
     part_hbm,
     keep_ref,
     give_hbm,
+    up_sum_ref,
+    down_sum_ref,
     xa_ref,
     xb_ref,
     sum_ref,
     out_ref,
+    up_ref,
+    down_ref,
     pulled,
     grad_k,
     grad_v,
@@ -1559,11 +1615,42 @@
     came_rows,
     rsend,
     rrecv,
+    came_up,
+    came_down,
+    swap_up,
+    swap_down,
+    came_swap_up,
+    came_swap_down,
+    fsend,
+    frecv,
 ):
     _, length, vd = high_ref.shape
     qk = (a_ref.shape[2] - vd) // 2
     hd = qk // 2
-    greet(plane=True, cores=True, pair=True)
+    greet(plane=True, cores=True, pair=True, across=True)
+    core, z = lax.axis_index("core"), lax.axis_index("uly")
+
+    def feed_copy(i, src, dst, to):
+        return pltpu.make_async_remote_copy(
+            src_ref=src,
+            dst_ref=dst,
+            send_sem=fsend.at[i],
+            recv_sem=frecv.at[i],
+            device_id=to,
+            device_id_type=MESH,
+        )
+
+    units = came_up.shape[1]
+    across = [
+        feed_copy(0, up_sum_ref.at[:, pl.ds(units, units)], came_up, {"uly": z ^ 2}),
+        feed_copy(1, down_sum_ref.at[pl.ds(units, units)], came_down, {"uly": z ^ 2}),
+    ]
+    swaps = [
+        feed_copy(2, swap_up, came_swap_up, {"core": 1 - core}),
+        feed_copy(3, swap_down, came_swap_down, {"core": 1 - core}),
+    ]
+    for c in across:
+        c.start()
     give = pltpu.make_async_remote_copy(
         src_ref=give_hbm,
         dst_ref=came_rows,
@@ -1573,11 +1660,26 @@
         device_id_type=MESH,
     )
     give.start()
-    group = PlaneReduce(lambda p: part_hbm.at[p], near, got, True, psend, precv)
-    local = pltpu.make_async_copy(part_hbm.at[pl.ds(0, 4)], near, lsem)
-    local.start()
-    group.start()
-    states = StateExchange(coef_ref, own, sib, chips, mine, came, final, send, recv)
+    groups = [
+        PlaneReduce(
+            lambda p, i=i: part_hbm.at[i, p],
+            near.at[i],
+            got.at[i],
+            i == 0,
+            psend.at[i],
+            precv.at[i],
+        )
+        for i in range(2)
+    ]
+    local = [
+        pltpu.make_async_copy(part_hbm.at[i, pl.ds(0, 4)], near.at[i], lsem.at[i]) for i in range(2)
+    ]
+    for c in local:
+        c.start()
+    for group in groups:
+        group.start()
+    weights = StateWeights(rates_ref, lengths_ref, length, True)
+    states = StateExchange(weights, own, sib, chips, mine, came, final, send, recv)
     parts = length // ROWS
 
     def values(m, h, at=slice(None)):
@@ -1606,7 +1708,7 @@
 
         @pl.loop(0, 2)
         def _(m):
-            entry = Places(lengths_ref, m, length).entry(rates_ref[h], 0, length)
+            entry = Places(lengths_ref, m, length).entry(rate_of(rates_ref, h), 0, length)
             q = (queries(m, h).astype(F32) * entry).astype(BF)
             own[m, h] = dot_tn(q, pulled[m, :, cols], BF)
 
@@ -1620,10 +1722,10 @@
             m, r = i // parts, i % parts
             at = pl.ds(pl.multiple_of(r * ROWS, ROWS), ROWS)
             places = Places(lengths_ref, m, length)
-            table = places.table(rates_ref[h], r * ROWS, ROWS, False)
+            table = places.table(rate_of(rates_ref, h), r * ROWS, ROWS, False)
             gr = pulled[m, at, cols]
             p = (dot_nt(gr, values(m, h)) * table).astype(BF)
-            entry = places.entry(rates_ref[h], r * ROWS, ROWS)
+            entry = places.entry(rate_of(rates_ref, h), r * ROWS, ROWS)
             xa_ref[m, at, h * hd : (h + 1) * hd] = (
                 jnp.dot(p, keys(m, h), preferred_element_type=F32)
                 + entry * dot_nt(gr, state_ref[m, h])
@@ -1636,7 +1738,7 @@
         def _(i):
             m, r = i // parts, i % parts
             at = pl.ds(pl.multiple_of(r * ROWS, ROWS), ROWS)
-            table = Places(lengths_ref, m, length).table(rates_ref[h], r * ROWS, ROWS, True)
+            table = Places(lengths_ref, m, length).table(rate_of(rates_ref, h), r * ROWS, ROWS, True)
             p = (dot_nt(values(m, h, at), pulled[m, :, cols]) * table).astype(BF)
             scores = (dot_nt(keys(m, h, at), queries(m, h)) * table).astype(BF)
             grad_k[m, at, h * hd : (h + 1) * hd] = jnp.dot(
@@ -1650,21 +1752,25 @@
     local_q(0)
     states.near()
     states.far()
+    for c in local:
+        c.wait()
+    for group in groups:
+        group.core_sums()
     local_q(1)
     states.settle()
-    local.wait()
-    group.core_sums()
     local_kv(0)
+    for group in groups:
+        group.first_sums(0)
+    for group in groups:
+        group.first_sums(1)
     local_kv(1)
-    group.first_sums(0)
-    group.first_sums(1)
     for h in range(2):
 
         @pl.loop(0, 2 * parts)
         def _(i):
             m, r = i // parts, i % parts
             at = pl.ds(pl.multiple_of(r * ROWS, ROWS), ROWS)
-            leave = Places(lengths_ref, m, length).leave(rates_ref[h], r * ROWS, ROWS)
+            leave = Places(lengths_ref, m, length).leave(rate_of(rates_ref, h), r * ROWS, ROWS)
             xa_ref[m, at, qk + h * hd : qk + (h + 1) * hd] = (
                 grad_k[m, at, h * hd : (h + 1) * hd]
                 + leave * dot_nt(values(m, h, at), final[m, h])
@@ -1686,7 +1792,35 @@
         out_ref[:, chip_chunk(k, quarter)] = (
             keep_ref[:, cols] + came_rows[:, cols].astype(F32)
         ).astype(BF)
-    group.finish(sum_ref)
+    for i, group in enumerate(groups):
+        group.finish(sum_ref.at[i])
+    rows, cols = up_ref.shape[0], down_ref.shape[1]
+
+    def mine(size, own):
+        return pl.ds(pl.multiple_of((core if own else 1 - core) * size, size), size)
+
+    for c in across:
+        c.wait()
+    kept_units = slice(0, units)
+
+    def up_total(own):
+        at = mine(rows, own)
+        return up_sum_ref[at, kept_units].astype(F32) + came_up[at, :].astype(F32)
+
+    def down_total(own):
+        at = mine(cols, own)
+        return down_sum_ref[kept_units, at].astype(F32) + came_down[:, at].astype(F32)
+
+    swap_up[...] = up_total(False).astype(BF)
+    swap_down[...] = down_total(False).astype(BF)
+    for c in swaps:
+        c.start()
+    up_ref[:, mine(units, True)] = up_total(True)
+    down_ref[mine(units, True), :] = down_total(True)
+    for c in swaps:
+        c.wait()
+    up_ref[:, mine(units, False)] = came_swap_up[...].astype(F32)
+    down_ref[mine(units, False), :] = came_swap_down[...].astype(F32)
 
 
 def sems(*shape):
@@ -1716,95 +1850,67 @@
     return pl.BlockSpec(memory_space=pltpu.SMEM)
 
 
-def chip_weights(rates, lengths, block):
-    chip, core = lax.axis_index("chip"), lax.axis_index("core")
-    count = block_count()
-    places = jnp.arange(count, dtype=jnp.int32)
-    ahead, back = [], []
-    others = chip ^ jnp.arange(4, dtype=jnp.int32)
-    for m in range(lengths.shape[0]):
-        ends = segment_ids((places + 1) * block - 1, lengths[m])
-
-        def end(b):
-            return jnp.where(b < 0, 0, ends[jnp.maximum(b, 0)])
-
-        whole = jnp.exp(-rates * block)
-        even = jnp.where(end(2 * chip) == end(2 * chip - 1), whole, 0.0)
-        odd = jnp.where(end(2 * chip + 1) == end(2 * chip), whole, 0.0)
-        one, zero = jnp.ones_like(whole), jnp.zeros_like(whole)
-        first = core == 0
-
-        def pick(a, b):
-            return jnp.where(first, a, b)
-
-        past = jnp.where(
-            ((others < chip) & (end(2 * others + 1) == end(2 * chip - 1)))[None],
-            jnp.exp(-rates[:, None] * (2.0 * block) * jnp.maximum(chip - 1 - others, 0)[None]),
-            0.0,
-        )
-        later = jnp.where(
-            ((others > chip) & (end(2 * chip + 1) == end(2 * others - 1)))[None],
-            jnp.exp(-rates[:, None] * (2.0 * block) * jnp.maximum(others - 1 - chip, 0)[None]),
-            0.0,
-        )
-        four = [pick(odd, one), pick(one, odd), pick(one, even), pick(zero, one)]
-        ahead.append(jnp.concatenate([jnp.stack(four, axis=1), past], axis=1))
-        four = [pick(one, even), pick(even, one), pick(odd, one), pick(one, zero)]
-        back.append(jnp.concatenate([jnp.stack(four, axis=1), later], axis=1))
-    return jnp.stack(ahead), jnp.stack(back)
-
-
-def retain(rates, lengths, coef, a, high, gate, out_rows, up, down):
-    micro, length, vd = high.shape
-    hd = (a.shape[2] - vd) // 4
-    state = (micro, 2, hd, vd)
-    return call(
-        retain_kernel,
-        5,
-        [smem()] * 3 + [vmem()] * 4 + [anywhere()] * 2,
-        [
-            ((micro, length, 2 * vd), BF, vmem()),
-            ((micro, length, 2 * vd), F32, vmem()),
-            (state, BF, vmem()),
-            ((4 * out_rows.shape[0], out_rows.shape[1]), BF, vmem()),
-            ((up.shape[0], 2 * up.shape[1]), BF, anywhere()),
-            ((2 * down.shape[0], down.shape[1]), BF, anywhere()),
-        ],
-        state_scratch(state)
-        + [
-            pltpu.VMEM(out_rows.shape, BF),
-            pltpu.VMEM((3, *out_rows.shape), BF),
-            sems(3),
-            sems(3),
-            sems(2),
-            sems(2),
-            sems(2),
-        ],
-        4 * micro * length * length * (hd + vd),
-        rates,
-        lengths,
-        coef,
-        a,
-        high,
-        gate,
-        out_rows,
-        up,
-        down,
-    )
-
-
-def retain_back(rates, lengths, coef, a, high, gate, kept, grad_mixed, state, part, keep, give):
+def settle_kernel(
+    block_in, input_in, first_in, second_in, out_in, up_in, down_in, *outs
+):
+    block, inputs, query, key, value, gate, output, up, down = outs
+    qk, half = query.shape[1], out_in.shape[2]
+    high = value.shape[1] // 2
+    block[...] = block_in[...]
+    inputs[...] = input_in[...]
+    query[...] = first_in[:, :qk].astype(F32)
+    key[...] = first_in[:, qk : 2 * qk].astype(F32)
+    value[:, :high] = first_in[:, 2 * qk :].astype(F32)
+    value[:, high:] = second_in[:, :high].astype(F32)
+    gate[...] = second_in[:, high:].astype(F32)
+    for i in range(2):
+        output[i * half : (i + 1) * half, :] = out_in[i].astype(F32).T
+    up[...] = up_in[...]
+    down[...] = down_in[...]
+
+
+def settle(block_out, input_grad, first_sum, second_sum, out_sum, up_grad, down_grad, qk):
+    piece = first_sum.shape[0]
+    high = first_sum.shape[1] - 2 * qk
+    args = (block_out, input_grad, first_sum, second_sum, out_sum, up_grad, down_grad)
+    shapes = [
+        (block_out.shape, BF),
+        (input_grad.shape, F32),
+        ((piece, qk), F32),
+        ((piece, qk), F32),
+        ((piece, 2 * high), F32),
+        ((piece, second_sum.shape[1] - high), F32),
+        ((2 * out_sum.shape[2], piece), F32),
+        (up_grad.shape, F32),
+        (down_grad.shape, F32),
+    ]
+    return pl.pallas_call(
+        settle_kernel,
+        out_shape=[like(s, t) for s, t in shapes],
+        in_specs=[vmem()] * len(args),
+        out_specs=[vmem()] * len(shapes),
+        compiler_params=pltpu.CompilerParams(vmem_limit_bytes=VMEM_LIMIT),
+    )(*args)
+
+
+def retain_back(
+    rates, lengths, a, high, gate, kept, grad_mixed, state, part, keep, give, up_sum, down_sum
+):
+    units = up_sum.shape[1] // 2
+    rows, cols = up_sum.shape[0] // 2, down_sum.shape[1] // 2
     micro, length, vd = high.shape
     hd = (a.shape[2] - vd) // 4
     return call(
         retain_back_kernel,
         6,
-        [smem()] * 3 + [vmem()] * 6 + [anywhere(), vmem(), anywhere()],
+        [smem()] * 2 + [vmem()] * 6 + [anywhere(), vmem(), anywhere(), vmem(), vmem()],
         [
             ((micro, length, a.shape[2]), BF, vmem()),
             ((micro, length, 3 * vd), BF, vmem()),
-            (part.shape[1:], BF, vmem()),
+            ((2, *part.shape[2:]), BF, vmem()),
             (give.shape, BF, vmem()),
+            ((rows, 2 * units), F32, vmem()),
+            ((2 * units, cols), F32, vmem()),
         ],
         [
             pltpu.VMEM((micro, length, 2 * vd), BF),
@@ -1814,19 +1920,26 @@
         ]
         + state_scratch(state.shape)
         + [
-            pltpu.VMEM((4, *part.shape[1:]), BF),
-            pltpu.VMEM((7, *part.shape[1:]), BF),
-            sems(7),
-            sems(7),
-            pltpu.SemaphoreType.DMA,
+            pltpu.VMEM((2, 4, *part.shape[2:]), BF),
+            pltpu.VMEM((2, 7, *part.shape[2:]), BF),
+            sems(2, 7),
+            sems(2, 7),
+            sems(2),
             pltpu.VMEM(give.shape, BF),
             pltpu.SemaphoreType.DMA,
             pltpu.SemaphoreType.DMA,
+            pltpu.VMEM((2 * rows, units), BF),
+            pltpu.VMEM((units, 2 * cols), BF),
+            pltpu.VMEM((rows, units), BF),
+            pltpu.VMEM((units, cols), BF),
+            pltpu.VMEM((rows, units), BF),
+            pltpu.VMEM((units, cols), BF),
+            sems(4),
+            sems(4),
         ],
         12 * micro * length * length * (hd + vd),
         rates,
         lengths,
-        coef,
         a,
         high,
         gate,
@@ -1836,10 +1949,12 @@
         part,
         keep,
         give,
+        up_sum,
+        down_sum,
     )
 
 
-def project(tokens, gains, weights, out_weight, up_weight, down_weight):
+def front(rates, lengths, tokens, out_grad, gains, weights, out_weight, up_weight, down_weight):
     micro, rows, width = tokens.shape
     count = lax.axis_size("uly")
     query, key, value, gate = weights
@@ -1852,26 +1967,39 @@
         w_second = lax.all_gather(second, BLK, axis=0, tiled=True)
         w_out = lax.all_gather(out_weight, BLK, axis=1, tiled=True)
         one = (normed(spread(tokens).astype(F32))[0] * full[0].astype(F32)).astype(BF)
+        a, v_high = dot_nn(one, w_first, BF), dot_nn(one, w_second[:, :high], BF)
+        gate_rows = dot_nn(one, w_second[:, high:])
+        heads_here = rates.shape[0] // count
+        own_rates = lax.dynamic_slice_in_dim(
+            rates, lax.axis_index("uly") * heads_here, heads_here
+        )
+        mixed, kept = plain_forward(own_rates, lengths, a, v_high, gate_rows)
         return (
             one,
-            dot_nn(one, w_first, BF),
-            dot_nn(one, w_second[:, :high], BF),
-            dot_nn(one, w_second[:, high:]),
+            a,
+            v_high,
+            gate_rows,
             w_first,
             w_second,
             w_out,
             full.astype(F32),
             up_weight,
             down_weight,
+            mixed,
+            kept,
+            None,
+            None,
         )
     wide = count * rows
+    own = micro * rows
     piece = width // 8
     na, nb, no = 2 * query.shape[1] + high, high + gate.shape[1], out_weight.shape[0]
     units = up_weight.shape[1]
+    state = (micro, 2, query.shape[1] // 2, high)
     return call(
-        project_kernel,
+        front_kernel,
         0,
-        [vmem()] * 3 + [anywhere()] * 7,
+        [smem()] * 2 + [vmem()] * 3 + [anywhere()] * 7,
         [
             ((micro, wide, width), BF, vmem()),
             ((micro, wide, na), BF, vmem()),
@@ -1881,11 +2009,15 @@
             ((width, nb), BF, anywhere()),
             ((no, width), BF, anywhere()),
             ((8, width), F32, vmem()),
-            ((2 * piece, units // 2), BF, anywhere()),
-            ((units // 2, 2 * piece), BF, anywhere()),
+            ((2 * piece, units), BF, anywhere()),
+            ((units, 2 * piece), BF, anywhere()),
+            ((micro, wide, 2 * high), BF, vmem()),
+            ((micro, wide, 2 * high), F32, vmem()),
+            (state, BF, vmem()),
+            ((4 * own, width), BF, vmem()),
         ],
         [
-            pltpu.VMEM((count, micro * rows, width), BF),
+            pltpu.VMEM((count, own, width), BF),
             pltpu.VMEM((width, na), BF),
             pltpu.VMEM((width, nb), BF),
             pltpu.VMEM((8, 8, piece), F32),
@@ -1893,14 +2025,19 @@
             sems(5, 7),
             sems(2, count - 1),
             sems(2, count - 1),
-            sems(2),
-            sems(2),
+            sems(4),
+            sems(4),
+            sems(3),
+            sems(3),
             sems(10),
-        ],
+        ]
+        + state_scratch(state),
         2 * micro * wide * width * (na + nb),
-        tokens.reshape(micro * rows, width),
-        gains[0][None],
-        gains[1][None],
+        rates,
+        lengths,
+        tokens.reshape(own, width),
+        out_grad.reshape(own, width),
+        jnp.stack(gains).astype(F32),
         query,
         key,
         value,
@@ -1958,7 +2095,7 @@
         [vmem()] * 3 + [anywhere()] * 2,
         [
             ((micro, count * rows, hidden), F32, vmem()),
-            ((8, width // 8, hidden), BF, vmem()),
+            ((2, 8, width // 8, hidden // 2), BF, vmem()),
             (up_shape, BF, vmem()),
             (down_shape, BF, vmem()),
         ],
@@ -2020,18 +2157,6 @@
     )
 
 
-def feed_scatter(up_sum, down_sum):
-    def settle(array, dim):
-        half = array.shape[dim] // 2
-        keep = lax.slice_in_dim(array, 0, half, axis=dim)
-        away = lax.slice_in_dim(array, half, 2 * half, axis=dim)
-        total = (keep.astype(F32) + shift(away, 2).astype(F32)).astype(BF)
-        own, other = core_cut(total, 1 - dim)
-        return core_join(own, swap(other, 1), dim).astype(F32)
-
-    return settle(up_sum, 1), settle(down_sum, 0)
-
-
 def middle(tokens, out_grad, douts, gains, mixed, w_out, up_weight, down_weight):
     micro, rows, width = tokens.shape
     own = micro * rows
@@ -2065,11 +2190,10 @@
         hidden, douts, gains, ups, downs
     )
     grad_mixed, part, up_sum, down_sum = fan_out(rows_bf, w_out, mixed, up_part, down_part)
-    up_grad, down_grad = feed_scatter(up_sum, down_sum)
     return (
         (keep, give),
-        up_grad,
-        down_grad,
+        up_sum,
+        down_sum,
         gain_part,
         grad_hidden,
         grad_mixed,
@@ -2126,8 +2250,8 @@
             sems(2, count - 1),
             sems(2, 7),
             sems(2, 7),
-            sems(6),
-            sems(6),
+            sems(10),
+            sems(10),
         ],
         4 * micro * wide * width * (na + nb),
         flat_a,
@@ -2140,7 +2264,7 @@
         gains,
         gain_two,
     )
-    return out[0].reshape(micro, rows, width), *out[1:]
+    return out
 
 
 def feed(norm_two, out_rows, pair):
@@ -2244,38 +2368,54 @@
     out_grad,
 ):
     micro, rows, width = tokens.shape
-    heads_here = decay_rate.shape[0] // lax.axis_size("uly")
-    rates = lax.dynamic_slice_in_dim(decay_rate, lax.axis_index("uly") * heads_here, heads_here)
     qk = query_weight.shape[1]
     cut_v = value_weight.shape[1] // 2
 
-    one, a, v_high, gate, w_first, w_second, w_out, gains, up, down = project(
+    (
+        one,
+        a,
+        v_high,
+        gate,
+        w_first,
+        w_second,
+        w_out,
+        gains,
+        up,
+        down,
+        mixed,
+        kept,
+        state,
+        douts,
+    ) = front(
+        decay_rate,
+        lengths,
         tokens,
+        out_grad,
         (retain_gain, feed_gain),
         (query_weight, key_weight, value_weight, gate_matrix),
         output_weight,
         up_weight,
         down_weight,
     )
-    if is_cube():
-        coef, coef_back = chip_weights(rates, lengths, one.shape[1])
-        mixed, kept, state, douts, up, down = retain(
-            rates, lengths, coef, a, v_high, gate, out_grad.reshape(micro * rows, width), up, down
-        )
-    else:
-        mixed, kept = plain_forward(rates, lengths, a, v_high, gate)
-        douts = None
-
     block_out, up_grad, down_grad, gain_two, grad_hidden, grad_mixed, part = middle(
         tokens, out_grad, douts, gains, mixed, w_out, up, down
     )
 
     if is_cube():
-        xa, xb, out_sum, block_out = retain_back(
-            rates, lengths, coef_back, a, v_high, gate, kept, grad_mixed, state, part, *block_out
+        xa, xb, out_sum, block_out, up_grad, down_grad = retain_back(
+            decay_rate,
+            lengths,
+            a,
+            v_high,
+            gate,
+            kept,
+            grad_mixed,
+            state,
+            part,
+            *block_out,
+            up_grad,
+            down_grad,
         )
-        block_out = block_out.reshape(tokens.shape)
-        out_sum = out_sum.T
     else:
         xa, xb = plain_backward(gate, kept, grad_mixed)
         out_sum = lax.psum_scatter(part, BLK, scatter_dimension=1, tiled=True)
@@ -2283,16 +2423,26 @@
     input_grad, first_sum, second_sum, gain_sums = close_rows(
         xa, xb, w_first, w_second, one, tokens, grad_hidden, gains, gain_two
     )
-    first_sum, second_sum = first_sum.astype(F32), second_sum.astype(F32)
+    if is_cube():
+        block_out, input_grad, query, key, value, gates, output, up_grad, down_grad = settle(
+            block_out, input_grad, first_sum, second_sum, out_sum, up_grad, down_grad, qk
+        )
+        block_out = block_out.reshape(tokens.shape)
+        input_grad = input_grad.reshape(tokens.shape)
+    else:
+        first_sum, second_sum = first_sum.astype(F32), second_sum.astype(F32)
+        query, key = first_sum[:, :qk], first_sum[:, qk : 2 * qk]
+        value = jnp.concatenate([first_sum[:, 2 * qk :], second_sum[:, :cut_v]], axis=1)
+        gates, output = second_sum[:, cut_v:], out_sum.astype(F32)
     return (
         block_out,
         input_grad,
         gain_sums[0],
-        first_sum[:, :qk],
-        first_sum[:, qk : 2 * qk],
-        jnp.concatenate([first_sum[:, 2 * qk :], second_sum[:, :cut_v]], axis=1),
-        second_sum[:, cut_v:],
-        out_sum.astype(F32),
+        query,
+        key,
+        value,
+        gates,
+        output,
         gain_sums[1],
         up_grad,
         down_grad,

time: 654 us -> 598 us (0.914)
  Pallas kernels: 614 us -> 586 us
  local copies, waits for them, and re-layouts: 20.3 us -> 2.66 us
  other arithmetic: 8.53 us -> 0.59 us
    pallas_call x7 -> x6, Pallas kernels: 614 us -> 579 us  [call(): pl.pallas_call(kernel, out_shape=[like(s, t) for s, t, _ in outs], in_spe...]
    slice x5 -> x0, local copies, waits for them, and re-layouts: 7.25 us -> none  [the longest x2 3.74 us: settle(): away = lax.slice_in_dim(array, half, 2 * half, axis=dim)]
    pallas_call x0 -> x1, Pallas kernels: none -> 7.03 us  [settle(): pl.pallas_call(settle_kernel, out_shape=[like(s, t) for s, t in shapes],...]
  transfers between devices with their start and end apart: 4 -> 0, of which waited for: 0 -> 0; matrix products, arithmetic and copies ran while one was open for 2% -> 0% of each run, Pallas kernels for 27% -> 0%
where the time goes in v4:
time: 598 us; the launch traced here: 590 us
  Pallas kernels  586 us (98%)
    pallas_call x6, Pallas kernels, call(): pl.pallas_call(kernel, out_shape=[like(s, t) for s, t, _ in outs], in_spe...  579 us

profile of v4, /device:TPU:0, one launch (start us, length us, event | category | flops | bytes accessed | tf_op | source)
XLA Modules:
  0.0 590.2 jit_solution(8865415216217205920)
XLA Ops:
  0.6 0.7 stack.9
  1.3 0.7 stack.10
  2.0 0.6 maximum_convert_fusion.gain_ref
  2.5 155.7 %shard_map.212 = (bf16[2,512,2048]{2,1,0:T(8,128)(2,1)}, bf16[2,512,1536]{2,1,0:T(8,128)(2,1)}, bf16[2,512,512]{2,1,0:T(8,128)(2,1)}, f32[2,512,1024]{2,1,0:T(8,...) custom-call(f32[8]{0:T(128)} %rates_ref.3, ...), custom_call_target="tpu_custom_call" | custom-call | flops 12884901888 | bytes 5244976 | tf_op jit(solution)/shard_map/pallas_call | solution.py:1836
  158.3 86.9 %shard_map.213 = (f32[256,2048]{1,0:T(8,128)}, bf16[2048,1024]{1,0:T(8,128)(2,1)}, bf16[1024,2048]{1,0:T(8,128)(2,1)}) custom-call(bf16[2,512,1024]{2,1,0:T(8,128)(2,1)} %get-tuple-element.62.x_ref.mixed_ref, bf16[1024,2048]{1,0:T(8,128)(2,1)} %get-tuple-element.63.w_ref, bf16[256,2048]{1,0:T(8,128)(2,1)} %bitcast.16, ...), custom_call_target="tpu_custom_call" | custom-call | flops 4294967296 | bytes 9437184 | tf_op jit(solution)/shard_map/pallas_call | solution.py:1836
  245.2 80.4 %shard_map.214 = (f32[256,2048]{1,0:T(8,128)}, bf16[256,2048]{1,0:T(8,128)(2,1)}, f32[256,2048]{1,0:T(8,128)}, bf16[256,2048]{1,0:T(8,128)(2,1)}, f32[1,2048]{1,...) custom-call(f32[256,2048]{1,0:T(8,128)} %get-tuple-element.66.hid_ref, ...), custom_call_target="tpu_custom_call" | custom-call | flops 25769803776 | bytes 14745600 | tf_op jit(solution)/shard_map/pallas_call | solution.py:1836
  325.7 85.2 %shard_map.215 = (f32[2,512,1024]{2,1,0:T(8,128)}, bf16[2,8,256,512]{3,2,1,0:T(8,128)(2,1)}, bf16[512,1024]{1,0:T(8,128)(2,1)}, bf16[1024,512]{1,0:T(8,128)(2,1)}) custom-call(bf16[256,2048]{1,0:T(8,128)(2,1)} %get-tuple-element.71.rows_ref, bf16[1024,2048]{1,0:T(8,128)(2,1)} %get-tuple-element.63.w_ref, ...), custom_call_target="tpu_custom_call" | custom-call | flops 8589934592 | bytes 15728640 | tf_op jit(solution)/shard_map/pallas_call | solution.py:1836
  410.8 66.5 %shard_map.216 = (bf16[2,512,1536]{2,1,0:T(8,128)(2,1)}, bf16[2,512,1536]{2,1,0:T(8,128)(2,1)}, bf16[2,256,512]{2,1,0:T(8,128)(2,1)}, bf16[256,2048]{1,0:T(8,128...) custom-call(f32[8]{0:T(128)} %rates_ref.3, s32[2,2]{1,0:T(2,128)} %lengths_ref.3, ...), custom_call_target="tpu_custom_call" | custom-call | flops 4831838208 | bytes 27263024 | tf_op jit(solution)/shard_map/pallas_call | solution.py:1836
  477.3 104.3 %shard_map.217 = (f32[256,2048]{1,0:T(8,128)}, bf16[256,1536]{1,0:T(8,128)(2,1)}, bf16[256,1536]{1,0:T(8,128)(2,1)}, f32[8,256]{1,0:T(8,128)}) custom-call(bf16[1024,1536]{1,0:T(8,128)(2,1)} %bitcast.11, bf16[1024,1536]{1,0:T(8,128)(2,1)} %bitcast.12, bf16[2048,1536]{1,0:T(8,128)(2,1)} %get-tuple-element.84.wa_ref, ...), custom_call_target="tpu_custom_call" | custom-call | flops 25769803776 | bytes 26288128 | tf_op jit(solution)/shard_map/pallas_call | solution.py:1836
  581.6 1.3 fusion
  582.9 7.0 %shard_map.218 = (bf16[256,2048]{1,0:T(8,128)(2,1)}, f32[256,2048]{1,0:T(8,128)}, f32[256,512]{1,0:T(8,128)}, f32[256,512]{1,0:T(8,128)}, f32[256,1024]{1,0:T(8,...) custom-call(bf16[256,2048]{1,0:T(8,128)(2,1)} %get-tuple-element.81.block_in, ...), custom_call_target="tpu_custom_call" | custom-call | tf_op jit(solution)/shard_map/pallas_call | solution.py:1887

commit v5 on v4

--- a/solution.py
+++ b/solution.py
@@ -508,6 +508,7 @@
 
 
 def front_kernel(
+    io,
     rates_ref,
     lengths_ref,
     tok_ref,
@@ -554,9 +555,25 @@
     width = tok_ref.shape[1]
     piece = width // 8
     qk, high = q_hbm.shape[1], high_ref.shape[2]
-    greet(plane=True, line=True, cores=True, across=True)
+    gains[0] = jnp.zeros_like(gains[0])
+    gains[0, 0:2, :] = gain_ref[...]
     line = LineGather(slots, zsend, zrecv)
     slots[z] = tok_ref[...]
+    greet(every=True, line=True, across=True)
+    chip = lax.axis_index("chip")
+    small = [
+        pltpu.make_async_remote_copy(
+            src_ref=gains.at[0],
+            dst_ref=gains.at[p],
+            send_sem=psend.at[0, p - 1],
+            recv_sem=precv.at[0, p - 1],
+            device_id={"chip": chip ^ (p % 4), "core": core ^ (p // 4)},
+            device_id_type=MESH,
+        )
+        for p in range(1, 8)
+    ]
+    for c in small:
+        c.start()
     line.pass_on(0)
     own = pl.ds(0, piece)
     local = [
@@ -574,11 +591,7 @@
     ]
     for c in local:
         c.start()
-    gains[0] = jnp.zeros_like(gains[0])
-    gains[0, 0:2, :] = gain_ref[...]
-    items = [
-        PlaneGather(gains.at[0], lambda p: gains.at[p], True, psend.at[0], precv.at[0])
-    ]
+    items = [None]
     for i, w in enumerate((wa, wb)):
         items.append(
             PlaneGather(
@@ -601,7 +614,6 @@
                 precv.at[3 + i],
             )
         )
-    items[0].start()
     units, cols = up_hbm.shape[1] // 2, down_hbm.shape[1]
     first_half = pl.ds(0, units)
     mine, theirs = (pl.ds(pl.multiple_of(c * units, units), units) for c in (core, 1 - core))
@@ -656,10 +668,8 @@
         item.start()
     for c in give:
         c.start()
-    items[0].near()
-    items[0].far()
-    items[0].corner()
-    items[0].finish()
+    for c in small:
+        c.wait()
     gains_ref[...] = jnp.zeros_like(gains_ref)
     for p in range(8):
         gains_ref[0:1, chunk_of(p, piece)] = gains[p, 0:1, :]
@@ -687,8 +697,15 @@
         douts_ref[0:own_rows, k * 2 * piece : (k + 1) * 2 * piece] = dout_ref[
             :, chip_chunk(k, 2 * piece)
         ]
+    at_end = (z == 0) | (z == line.last)
+    inside = (z > 0) & (z < line.last)
     normalize(z)
     line.take(1, normalize)
+
+    @pl.when(at_end)
+    def _():
+        send_rows[0].start()
+
     for item in items[1:3]:
         item.near()
     for item in items[1:3]:
@@ -696,6 +713,16 @@
     for item in items[3:]:
         item.start()
     line.take(2, normalize)
+    for c in cut:
+        c.wait()
+    for c in give:
+        c.wait()
+
+    @pl.when(at_end)
+    def _():
+        for c in away:
+            c.start()
+
     for item in items[1:3]:
         item.corner()
     for item in items[1:3]:
@@ -737,21 +764,24 @@
         normalize(slot)
         multiply(slot)
 
-    line.take(3, lambda slot: None)
-    for c in cut:
-        c.wait()
-    for c in give:
-        c.wait()
-    for c in away:
-        c.start()
-    send_rows[0].start()
-    line.each(3, both_steps)
+    line.take(3, both_steps)
+
+    @pl.when(inside)
+    def _():
+        for c in away:
+            c.wait_recv()
+        for c in away:
+            c.start()
+        send_rows[0].start()
+
+    io.done("one", "first", "high", "gate")
     for item in items[3:]:
         item.corner()
     for item in items[3:]:
         item.finish()
     line.finish()
     retain_part(
+        io,
         rates_ref,
         lengths_ref,
         first_ref,
@@ -765,11 +795,20 @@
         *state_refs,
     )
     local[5].wait()
-    for c in outs + away:
+    for c in outs:
         c.wait()
 
+    @pl.when(at_end)
+    def _():
+        for c in away:
+            c.wait_recv()
+
+    for c in away:
+        c.wait_send()
+
 
 def add_rows_kernel(
+    io,
     x_ref,
     w_ref,
     tok_ref,
@@ -820,7 +859,9 @@
     line = LineReduce(make, out_ref, held, came, send, recv)
     for item in items:
         item.start()
+    io.ready("x", "w")
     line.step(3)
+    io.start(1)
     for c in local:
         c.start()
     line.step(2)
@@ -830,6 +871,7 @@
         item.far()
     line.step(1)
     line.close()
+    io.ready("tokens")
     for k in range(4):
         cols = pl.ds(k * 2 * width, 2 * width)
         out_ref[:, cols] += tok_ref[:, chip_chunk(k, 2 * width)].astype(F32)
@@ -842,6 +884,7 @@
 
 
 def fan_out_kernel(
+    io,
     rows_ref,
     w_ref,
     mixed_ref,
@@ -907,6 +950,7 @@
             total[p] += dot_tn(ordered[:, cols], mixed)
 
     total[...] = jnp.zeros_like(total)
+    io.ready("w", "mixed")
     multiply(z)
     line.take(1, multiply)
     for g in groups:
@@ -915,15 +959,18 @@
     for g in groups:
         g.first_sums(1)
     line.take(3, multiply)
+    io.done("grad")
     half = part_ref.shape[3]
     for i in range(2):
         part_ref[i] = total[:, :, i * half : (i + 1) * half].astype(BF)
+    io.done("part")
     groups[0].finish(up_ref)
     groups[1].finish(down_ref)
     line.finish()
 
 
 def feed_kernel(
+    io,
     hid_ref,
     douts_ref,
     gain_ref,
@@ -951,8 +998,10 @@
     other, pair = {"core": 1 - core}, {"uly": z ^ 1}
     greet(cores=True, pair=True)
 
-    def group(g):
-        return pl.ds(g * rows, rows)
+    half = rows // 2
+
+    def group(g, part=None):
+        return pl.ds(g * rows, rows) if part is None else pl.ds(g * rows + part * half, half)
 
     def copy(i, src, dst, to):
         return pltpu.make_async_remote_copy(
@@ -964,75 +1013,90 @@
             device_id_type=MESH,
         )
 
+    parts = [pl.ds(part * half, half) for part in range(2)]
+    to_pair = [copy(p, two.at[group(0, p)], two.at[group(2, p)], pair) for p in range(2)]
+    through = [copy(2 + p, two.at[group(2, p)], two.at[group(3, p)], other) for p in range(2)]
+    to_other = copy(4, two.at[group(0)], two.at[group(1)], other)
     step = 32
-
-    @pl.loop(0, rows // step)
-    def _(i):
-        at = pl.ds(pl.multiple_of(i * step, step), step)
-        hat, _scale = normed(hid_ref[at, :])
-        two[at, :] = (hat * gain_ref[1:2, :]).astype(BF)
-
-    to_pair = copy(0, two.at[group(0)], two.at[group(2)], pair)
-    to_other = copy(1, two.at[group(0)], two.at[group(1)], other)
-    through = copy(2, two.at[group(2)], two.at[group(3)], other)
-    to_pair.start()
+    io.ready("hid")
+    io.start(1)
+    for part in range(2):
+
+        @pl.loop(0, half // step)
+        def _(i):
+            at = pl.ds(pl.multiple_of(part * half + i * step, step), step)
+            hat, _scale = normed(hid_ref[at, :])
+            two[at, :] = (hat * gain_ref[1:2, :]).astype(BF)
+
+        to_pair[part].start()
     to_other.start()
 
-    def work(g):
+    def work(g, part=None):
+        at = group(g, part)
+        to = slice(None) if part is None else parts[part]
         tile = 256
 
         @pl.loop(0, hidden // tile)
         def _(n):
             cols = pl.ds(pl.multiple_of(n * tile, tile), tile)
-            upward = jnp.dot(two[group(g), :], ups_ref[:, cols], preferred_element_type=F32)
+            upward = jnp.dot(two[at, :], ups_ref[:, cols], preferred_element_type=F32)
             value, slope = gelu_pair(upward)
-            act[group(g), cols] = value.astype(BF)
-            pulled = dot_nt(douts_ref[group(g), :], downs_ref[cols, :])
-            gu[group(g), cols] = (pulled * slope).astype(BF)
+            act[at, cols] = value.astype(BF)
+            pulled = dot_nt(douts_ref[at, :], downs_ref[cols, :])
+            gu[at, cols] = (pulled * slope).astype(BF)
 
         tile = 512
 
         @pl.loop(0, width // tile)
         def _(n):
             cols = pl.ds(pl.multiple_of(n * tile, tile), tile)
-            back = dot_nt(gu[group(g), :], ups_ref[cols, :])
-            down = jnp.dot(act[group(g), :], downs_ref[:, cols], preferred_element_type=F32)
+            back = dot_nt(gu[at, :], ups_ref[cols, :])
+            down = jnp.dot(act[at, :], downs_ref[:, cols], preferred_element_type=F32)
             if g == 0:
                 sums[0, :, cols] = back
                 sums[1, :, cols] = down
             else:
-                held[g - 1, 0, :, cols] = back.astype(BF)
-                held[g - 1, 1, :, cols] = down.astype(BF)
-
-    returns = [copy(3 + i, held.at[0, i], came.at[3 * i], other) for i in range(2)]
-    returns += [copy(5 + i, held.at[2, i], came.at[1 + 3 * i], other) for i in range(2)]
-    last = copy(7, held.at[1, 0], came.at[2], pair)
-
+                held[g - 1, 0, to, cols] = back.astype(BF)
+                held[g - 1, 1, to, cols] = down.astype(BF)
+
+    own_back = [copy(5 + i, held.at[0, i], came.at[3 * i], other) for i in range(2)]
+    pair_back = [
+        [
+            copy(7 + 2 * p + i, held.at[2, i, parts[p]], came.at[1 + 3 * i, parts[p]], other)
+            for i in range(2)
+        ]
+        for p in range(2)
+    ]
+    last = [copy(11 + p, held.at[1, 0, parts[p]], came.at[2, parts[p]], pair) for p in range(2)]
+
+    io.ready("ups", "downs", "douts")
     work(0)
     to_other.wait_recv()
     work(1)
-    for c in returns[:2]:
+    for c in own_back:
         c.start()
-    to_pair.wait_recv()
-    through.start()
-    work(2)
-    through.wait_recv()
-    work(3)
-    for c in returns[2:]:
-        c.start()
-    for i in range(2):
-        returns[2 + i].wait_recv()
-
-        @pl.loop(0, rows // step)
-        def _(r):
-            at = pl.ds(pl.multiple_of(r * step, step), step)
-            held[1, i, at, :] = (
-                held[1, i, at, :].astype(F32) + came[1 + 3 * i, at, :].astype(F32)
-            ).astype(BF)
-
-        if i == 0:
-            last.start()
+    for p in range(2):
+        to_pair[p].wait_recv()
+        through[p].start()
+        work(2, p)
+        through[p].wait_recv()
+        work(3, p)
+        for c in pair_back[p]:
+            c.start()
+        for i in range(2):
+            pair_back[p][i].wait_recv()
+
+            @pl.loop(0, half // step)
+            def _(r):
+                at = pl.ds(pl.multiple_of(p * half + r * step, step), step)
+                held[1, i, at, :] = (
+                    held[1, i, at, :].astype(F32) + came[1 + 3 * i, at, :].astype(F32)
+                ).astype(BF)
+
+            if i == 0:
+                last[p].start()
     give_ref[...] = held[1, 1]
+    io.done("give")
     tile = 512
 
     @pl.loop(0, width // tile)
@@ -1041,9 +1105,9 @@
         up_grad_ref[n] = dot_tn(two[:, cols], gu[...], BF)
         down_grad_ref[n] = dot_tn(act[...], douts_ref[:, cols], BF)
 
-    for i in range(2):
-        returns[i].wait_recv()
-    last.wait_recv()
+    io.done("up", "down")
+    for c in own_back + last:
+        c.wait_recv()
     gain_grad_ref[...] = jnp.zeros_like(gain_grad_ref)
 
     @pl.loop(0, rows // step)
@@ -1057,7 +1121,7 @@
         rows_ref[at, :] = grad.astype(BF)
         keep_ref[at, :] = hid_ref[at, :] + sums[1, at, :] + came[3, at, :].astype(F32)
 
-    for c in [to_pair, to_other, through, last] + returns:
+    for c in to_pair + through + own_back + pair_back[0] + pair_back[1] + last + [to_other]:
         c.wait_send()
 
 
@@ -1135,6 +1199,7 @@
 
 
 def close_rows_kernel(
+    io,
     xa_ref,
     xb_ref,
     wa_ref,
@@ -1217,7 +1282,10 @@
                 r = r + more[:, cols].astype(F32)
             to[:, cols] = r.astype(BF)
 
+    io.ready("xa", "xb", "wa", "wb")
+    io.start(1)
     line.step(3)
+    io.ready("one")
     for n in range(4):
         for group, x_ref, near, far, got in sets:
             order = (3, group.away[0], group.stay[1], 0)
@@ -1245,6 +1313,7 @@
     line.close()
     step = 32
     gain_sum[...] = jnp.zeros_like(gain_sum)
+    io.ready("tokens", "hid")
 
     @pl.loop(0, 2 * rows // step)
     def _(r):
@@ -1486,6 +1555,7 @@
 
 
 def retain_part(
+    io,
     rates_ref,
     lengths_ref,
     a_ref,
@@ -1565,9 +1635,12 @@
             g = gate_ref[m, at, cols]
             mixed_ref[m, at, cols] = (g * sigmoid(g) * normed(kept)[0]).astype(BF)
 
+        if h == 0:
+            to_other.wait_recv()
+            through.wait_recv()
+            io.done("douts")
+
     states.finish()
-    to_other.wait_recv()
-    through.wait_recv()
     for c in send_rows:
         c.wait_send()
 
@@ -1577,6 +1650,7 @@
 
 
 def retain_back_kernel(
+    io,
     rates_ref,
     lengths_ref,
     a_ref,
@@ -1649,6 +1723,7 @@
         feed_copy(2, swap_up, came_swap_up, {"core": 1 - core}),
         feed_copy(3, swap_down, came_swap_down, {"core": 1 - core}),
     ]
+    io.ready("up", "down")
     for c in across:
         c.start()
     give = pltpu.make_async_remote_copy(
@@ -1678,6 +1753,8 @@
         c.start()
     for group in groups:
         group.start()
+    io.ready("gate", "kept", "grad")
+    io.start(1)
     weights = StateWeights(rates_ref, lengths_ref, length, True)
     states = StateExchange(weights, own, sib, chips, mine, came, final, send, recv)
     parts = length // ROWS
@@ -1705,6 +1782,9 @@
                 gm * hat * (sigma + g * sigma * (1.0 - sigma))
             ).astype(BF)
             pulled[m, at, cols] = norm_back(gm * g * sigma, hat, scale).astype(BF)
+
+        if h == 0:
+            io.ready("a", "high", "state")
 
         @pl.loop(0, 2)
         def _(m):
@@ -1786,6 +1866,7 @@
 
     states.finish()
     give.wait()
+    io.ready("keep")
     quarter = keep_ref.shape[1] // 4
     for k in range(4):
         cols = slice(k * quarter, (k + 1) * quarter)
@@ -1831,14 +1912,78 @@
     return jax.ShapeDtypeStruct(shape, kind)
 
 
+class Late:
+    def __init__(self, name, order=0):
+        self.name, self.order = name, order
+
+
+class Early:
+    def __init__(self, name):
+        self.name = name
+
+
+class Moves:
+    def __init__(self, loads, stores):
+        self.loads, self.stores = loads, stores
+        self.waited, self.begun = set(), set()
+
+    def start(self, order):
+        for copy, at in self.loads.values():
+            if at == order:
+                copy.start()
+
+    def ready(self, *names):
+        for name in names:
+            self.loads[name][0].wait()
+            self.waited.add(name)
+
+    def done(self, *names):
+        for name in names:
+            self.stores[name].start()
+            self.begun.add(name)
+
+    def finish(self):
+        self.done(*[n for n in self.stores if n not in self.begun])
+        self.ready(*[n for n in self.loads if n not in self.waited])
+        for copy in self.stores.values():
+            copy.wait()
+
+
 def call(kernel, number, ins, outs, scratch, flops, *args):
     moved = sum(a.size * a.dtype.itemsize for a in args)
+    late = [i for i, spec in enumerate(ins) if isinstance(spec, Late)]
+    early = [i for i, out in enumerate(outs) if isinstance(out[2], Early)]
+
+    def whole(*refs):
+        refs = list(refs)
+        in_refs, refs = refs[: len(ins)], refs[len(ins) :]
+        out_refs, refs = refs[: len(outs)], refs[len(outs) :]
+        own, refs = refs[: len(scratch)], refs[len(scratch) :]
+        load_sem, store_sem = refs[-2:]
+        loads, stores = {}, {}
+        for n, i in enumerate(late):
+            copy = pltpu.make_async_copy(in_refs[i], refs[n], load_sem.at[n])
+            loads[ins[i].name] = (copy, ins[i].order)
+            in_refs[i] = refs[n]
+        for n, i in enumerate(early):
+            ref = refs[len(late) + n]
+            stores[outs[i][2].name] = pltpu.make_async_copy(ref, out_refs[i], store_sem.at[n])
+            out_refs[i] = ref
+        io = Moves(loads, stores)
+        io.start(0)
+        kernel(io, *in_refs, *out_refs, *own)
+        io.finish()
+
+    extra = [pltpu.VMEM(args[i].shape, args[i].dtype) for i in late]
+    extra += [pltpu.VMEM(outs[i][0], outs[i][1]) for i in early]
     return pl.pallas_call(
-        kernel,
-        out_shape=[like(s, t) for s, t, _ in outs],
-        in_specs=ins,
-        out_specs=[spec for _, _, spec in outs],
-        scratch_shapes=scratch,
+        whole,
+        out_shape=[like(shape, kind) for shape, kind, _ in outs],
+        in_specs=[anywhere() if i in late else spec for i, spec in enumerate(ins)],
+        out_specs=[anywhere() if i in early else out[2] for i, out in enumerate(outs)],
+        scratch_shapes=list(scratch)
+        + extra
+        + [sems(max(len(late), 1)), sems(max(len(early), 1))],
         compiler_params=pltpu.CompilerParams(
             collective_id=number, has_side_effects=True, vmem_limit_bytes=VMEM_LIMIT
         ),
@@ -1903,7 +2048,9 @@
     return call(
         retain_back_kernel,
         6,
-        [smem()] * 2 + [vmem()] * 6 + [anywhere(), vmem(), anywhere(), vmem(), vmem()],
+        [smem()] * 2
+        + [Late("a", 1), Late("high", 1), Late("gate"), Late("kept"), Late("grad"), Late("state", 1)]
+        + [anywhere(), Late("keep", 1), anywhere(), Late("up"), Late("down")],
         [
             ((micro, length, a.shape[2]), BF, vmem()),
             ((micro, length, 3 * vd), BF, vmem()),
@@ -2001,10 +2148,10 @@
         0,
         [smem()] * 2 + [vmem()] * 3 + [anywhere()] * 7,
         [
-            ((micro, wide, width), BF, vmem()),
-            ((micro, wide, na), BF, vmem()),
-            ((micro, wide, high), BF, vmem()),
-            ((micro, wide, nb - high), F32, vmem()),
+            ((micro, wide, width), BF, Early("one")),
+            ((micro, wide, na), BF, Early("first")),
+            ((micro, wide, high), BF, Early("high")),
+            ((micro, wide, nb - high), F32, Early("gate")),
             ((width, na), BF, anywhere()),
             ((width, nb), BF, anywhere()),
             ((no, width), BF, anywhere()),
@@ -2014,7 +2161,7 @@
             ((micro, wide, 2 * high), BF, vmem()),
             ((micro, wide, 2 * high), F32, vmem()),
             (state, BF, vmem()),
-            ((4 * own, width), BF, vmem()),
+            ((4 * own, width), BF, Early("douts")),
         ],
         [
             pltpu.VMEM((count, own, width), BF),
@@ -2064,7 +2211,7 @@
     out = call(
         add_rows_kernel,
         1,
-        [vmem()] * 3 + [anywhere()] * 2,
+        [Late("x"), Late("w"), Late("tokens", 1)] + [anywhere()] * 2,
         [
             ((micro * rows, width), F32, vmem()),
             ((width, units), BF, anywhere()),
@@ -2092,10 +2239,10 @@
     return call(
         fan_out_kernel,
         2,
-        [vmem()] * 3 + [anywhere()] * 2,
+        [vmem(), Late("w"), Late("mixed")] + [anywhere()] * 2,
         [
-            ((micro, count * rows, hidden), F32, vmem()),
-            ((2, 8, width // 8, hidden // 2), BF, vmem()),
+            ((micro, count * rows, hidden), F32, Early("grad")),
+            ((2, 8, width // 8, hidden // 2), BF, Early("part")),
             (up_shape, BF, vmem()),
             (down_shape, BF, vmem()),
         ],
@@ -2128,15 +2275,15 @@
     return call(
         feed_kernel,
         4,
-        [vmem()] * 5,
+        [Late("hid"), Late("douts", 1), vmem(), Late("ups", 1), Late("downs", 1)],
         [
             ((own, width), F32, vmem()),
-            ((own, width), BF, vmem()),
+            ((own, width), BF, Early("give")),
             ((own, width), F32, vmem()),
             ((own, width), BF, vmem()),
             ((1, width), F32, vmem()),
-            ((4, width // 4, units), BF, vmem()),
-            ((4, units, width // 4), BF, vmem()),
+            ((4, width // 4, units), BF, Early("up")),
+            ((4, units, width // 4), BF, Early("down")),
         ],
         [
             pltpu.VMEM((4 * own, width), BF),
@@ -2145,8 +2292,8 @@
             pltpu.VMEM((2, own, width), F32),
             pltpu.VMEM((3, 2, own, width), BF),
             pltpu.VMEM((5, own, width), BF),
-            sems(8),
-            sems(8),
+            sems(13),
+            sems(13),
         ],
         2 * 6 * 4 * own * units * width,
         hidden,
@@ -2227,7 +2374,8 @@
     out = call(
         close_rows_kernel,
         3,
-        [vmem()] * 9,
+        [Late("xa"), Late("xb"), Late("wa"), Late("wb"), Late("one", 1), Late("tokens", 1)]
+        + [Late("hid", 1), vmem(), vmem()],
         [
             ((micro * rows, width), F32, vmem()),
             ((piece, na), BF, vmem()),

time: 598 us -> 558 us (0.933); the launches traced: 590 us -> 557 us
  Pallas kernels: 586 us -> 552 us
    pallas_call x6, Pallas kernels: 579 us -> 545 us  [call(): pl.pallas_call(whole, out_shape=[like(shape, kind) for shape, kind, _ in...]
where the time goes in v5:
time: 558 us; the launch traced here: 557 us
  Pallas kernels  552 us (99%)
    pallas_call x6, Pallas kernels, call(): pl.pallas_call(whole, out_shape=[like(shape, kind) for shape, kind, _ in...  545 us

profile of v5, /device:TPU:0, one launch (start us, length us, event | category | flops | bytes accessed | tf_op | source)
XLA Modules:
  0.0 556.5 jit_solution(7894802507471455480)
XLA Ops:
  0.6 0.7 stack.9
  1.3 0.7 stack.10
  2.0 0.6 maximum_convert_fusion.refs_4_
  2.5 156.0 %shard_map.212 = (bf16[2,512,2048]{2,1,0:T(8,128)(2,1)}, bf16[2,512,1536]{2,1,0:T(8,128)(2,1)}, bf16[2,512,512]{2,1,0:T(8,128)(2,1)}, f32[2,512,1024]{2,1,0:T(8,...) custom-call(f32[8]{0:T(128)} %refs_0_.3, ...), custom_call_target="tpu_custom_call" | custom-call | flops 12884901888 | bytes 5244976 | tf_op jit(solution)/shard_map/pallas_call | solution.py:1979
  158.5 82.4 %shard_map.213 = (f32[256,2048]{1,0:T(8,128)}, bf16[2048,1024]{1,0:T(8,128)(2,1)}, bf16[1024,2048]{1,0:T(8,128)(2,1)}) custom-call(bf16[2,512,1024]{2,1,0:T(8,128)(2,1)} %get-tuple-element.62.refs_0_.refs_2_, bf16[1024,2048]{1,0:T(8,128)(2,1)} %get-tuple-element.63.refs_1_, bf16[256,2048]{1,0:T(8,128)(2,1)} %bitcast.16, ...), custom_call_target="tpu_custom_call" | custom-call | flops 4294967296 | bytes 9437184 | tf_op jit(solution)/shard_map/pallas_call | solution.py:1979
  241.0 65.2 %shard_map.214 = (f32[256,2048]{1,0:T(8,128)}, bf16[256,2048]{1,0:T(8,128)(2,1)}, f32[256,2048]{1,0:T(8,128)}, bf16[256,2048]{1,0:T(8,128)(2,1)}, f32[1,2048]{1,...) custom-call(f32[256,2048]{1,0:T(8,128)} %get-tuple-element.66.refs_0_, ...), custom_call_target="tpu_custom_call" | custom-call | flops 25769803776 | bytes 14745600 | tf_op jit(solution)/shard_map/pallas_call | solution.py:1979
  306.2 80.2 %shard_map.215 = (f32[2,512,1024]{2,1,0:T(8,128)}, bf16[2,8,256,512]{3,2,1,0:T(8,128)(2,1)}, bf16[512,1024]{1,0:T(8,128)(2,1)}, bf16[1024,512]{1,0:T(8,128)(2,1)}) custom-call(bf16[256,2048]{1,0:T(8,128)(2,1)} %get-tuple-element.71.refs_0_, bf16[1024,2048]{1,0:T(8,128)(2,1)} %get-tuple-element.63.refs_1_, ...), custom_call_target="tpu_custom_call" | custom-call | flops 8589934592 | bytes 15728640 | tf_op jit(solution)/shard_map/pallas_call | solution.py:1979
  386.4 60.8 %shard_map.216 = (bf16[2,512,1536]{2,1,0:T(8,128)(2,1)}, bf16[2,512,1536]{2,1,0:T(8,128)(2,1)}, bf16[2,256,512]{2,1,0:T(8,128)(2,1)}, bf16[256,2048]{1,0:T(8,128...) custom-call(f32[8]{0:T(128)} %refs_0_.3, s32[2,2]{1,0:T(2,128)} %refs_1_.3, ...), custom_call_target="tpu_custom_call" | custom-call | flops 4831838208 | bytes 27263024 | tf_op jit(solution)/shard_map/pallas_call | solution.py:1979
  447.2 100.8 %shard_map.217 = (f32[256,2048]{1,0:T(8,128)}, bf16[256,1536]{1,0:T(8,128)(2,1)}, bf16[256,1536]{1,0:T(8,128)(2,1)}, f32[8,256]{1,0:T(8,128)}) custom-call(bf16[1024,1536]{1,0:T(8,128)(2,1)} %bitcast.11, bf16[1024,1536]{1,0:T(8,128)(2,1)} %bitcast.12, bf16[2048,1536]{1,0:T(8,128)(2,1)} %get-tuple-element.84.refs_2_, ...), custom_call_target="tpu_custom_call" | custom-call | flops 25769803776 | bytes 26288128 | tf_op jit(solution)/shard_map/pallas_call | solution.py:1979
  548.0 1.3 fusion
  549.3 7.0 %shard_map.218 = (bf16[256,2048]{1,0:T(8,128)(2,1)}, f32[256,2048]{1,0:T(8,128)}, f32[256,512]{1,0:T(8,128)}, f32[256,512]{1,0:T(8,128)}, f32[256,1024]{1,0:T(8,...) custom-call(bf16[256,2048]{1,0:T(8,128)(2,1)} %get-tuple-element.81.block_in, ...), custom_call_target="tpu_custom_call" | custom-call | tf_op jit(solution)/shard_map/pallas_call | solution.py:2032

commit v6 on v5

--- a/solution.py
+++ b/solution.py
@@ -467,9 +467,11 @@
 
                 self.copy(right, d).start()
 
+    def own(self):
+        self.make(self.z, self.out)
+
     def close(self):
         z, last = self.z, self.last
-        self.make(z, self.out)
 
         @pl.when(z > 0)
         def _():
@@ -548,6 +550,9 @@
     dsend,
     drecv,
     lsem,
+    stage_out,
+    stage_up,
+    stage_down,
     *state_refs,
 ):
     core, z = lax.axis_index("core"), lax.axis_index("uly")
@@ -585,7 +590,7 @@
                 (v_hbm.at[:, pl.ds(0, high)], wa.at[own, pl.ds(2 * qk, high)]),
                 (v_hbm.at[:, pl.ds(high, high)], wb.at[own, pl.ds(0, high)]),
                 (g_hbm, wb.at[own, pl.ds(high, g_hbm.shape[1])]),
-                (out_hbm, w_out_hbm.at[:, own]),
+                (out_hbm, stage_out),
             )
         )
     ]
@@ -629,9 +634,15 @@
             device_id_type=MESH,
         )
 
+    stage = [
+        local[5],
+        pltpu.make_async_copy(up_hbm.at[:, mine], stage_up, lsem.at[6]),
+        pltpu.make_async_copy(down_hbm.at[mine], stage_down, lsem.at[7]),
+    ]
     cut = [
-        pltpu.make_async_copy(up_hbm.at[:, mine], up_own_hbm.at[here, first_half], lsem.at[6]),
-        pltpu.make_async_copy(down_hbm.at[mine], down_own_hbm.at[first_half, here], lsem.at[7]),
+        pltpu.make_async_copy(stage_out, w_out_hbm.at[:, own], lsem.at[10]),
+        pltpu.make_async_copy(stage_up, up_own_hbm.at[here, first_half], lsem.at[11]),
+        pltpu.make_async_copy(stage_down, down_own_hbm.at[first_half, here], lsem.at[12]),
     ]
     give = [
         remote(0, up_hbm.at[:, theirs], up_own_hbm.at[here, first_half], {"core": 1 - core}),
@@ -660,7 +671,7 @@
         rows_to(1, 0, 1, {"core": 1 - core}),
         rows_to(2, 2, 3, {"core": 1 - core}),
     ]
-    for c in cut:
+    for c in stage[1:]:
         c.start()
     for c in local[:5]:
         c.wait()
@@ -693,6 +704,10 @@
                         (src - mean) * scale * gains[p, 0:1, :]
                     ).astype(BF)
 
+    for c in stage:
+        c.wait()
+    for c in cut:
+        c.start()
     for k in range(4):
         douts_ref[0:own_rows, k * 2 * piece : (k + 1) * 2 * piece] = dout_ref[
             :, chip_chunk(k, 2 * piece)
@@ -770,9 +785,9 @@
     def _():
         for c in away:
             c.wait_recv()
+        send_rows[0].start()
         for c in away:
             c.start()
-        send_rows[0].start()
 
     io.done("one", "first", "high", "gate")
     for item in items[3:]:
@@ -794,7 +809,6 @@
         send_rows,
         *state_refs,
     )
-    local[5].wait()
     for c in outs:
         c.wait()
 
@@ -824,6 +838,8 @@
     psend,
     precv,
     lsem,
+    stage_up,
+    stage_down,
 ):
     rows = out_ref.shape[0] // 2
     width = out_ref.shape[1] // 8
@@ -840,9 +856,13 @@
         PlaneGather(up_hbm, up_at, True, psend.at[0], precv.at[0], False),
         PlaneGather(down_hbm, down_at, False, psend.at[1], precv.at[1], False),
     ]
+    stage = [
+        pltpu.make_async_copy(up_hbm, stage_up, lsem.at[2]),
+        pltpu.make_async_copy(down_hbm, stage_down, lsem.at[3]),
+    ]
     local = [
-        pltpu.make_async_copy(up_hbm, up_at(0), lsem.at[0]),
-        pltpu.make_async_copy(down_hbm, down_at(0), lsem.at[1]),
+        pltpu.make_async_copy(stage_up, up_at(0), lsem.at[0]),
+        pltpu.make_async_copy(stage_down, down_at(0), lsem.at[1]),
     ]
 
     def make(a, to):
@@ -862,14 +882,19 @@
     io.ready("x", "w")
     line.step(3)
     io.start(1)
+    for c in stage:
+        c.start()
+    line.step(2)
+    for c in stage:
+        c.wait()
     for c in local:
         c.start()
-    line.step(2)
     for item in items:
         item.near()
     for item in items:
         item.far()
     line.step(1)
+    line.own()
     line.close()
     io.ready("tokens")
     for k in range(4):
@@ -1221,7 +1246,6 @@
     far_b,
     came_a,
     came_b,
-    gain_sum,
     small,
     small_came,
     small_line,
@@ -1248,10 +1272,12 @@
         @pl.loop(0, 8)
         def _(p):
             part = pl.ds(pl.multiple_of(p * width, width), width)
-            to[:, chunk_of(p, width)] = (
-                dot_nt(xa, wa_ref[part, :]) + dot_nt(xb, wb_ref[part, :])
-            ).astype(to.dtype)
-
+            r = dot_nt(xa, wa_ref[part, :]) + dot_nt(xb, wb_ref[part, :])
+            to[:, chunk_of(p, width)] = r.astype(to.dtype)
+            ones = jnp.concatenate([one_ref[i, part] for i in at], axis=0)
+            small[p, 0:1, :] += jnp.sum(r * ones.astype(F32), axis=0, keepdims=True)
+
+    small[...] = jnp.zeros_like(small)
     line = LineReduce(make, out_ref, held, came, send, recv)
     sets = []
     for i, (x_ref, near, far, got, x_first) in enumerate(
@@ -1282,10 +1308,9 @@
                 r = r + more[:, cols].astype(F32)
             to[:, cols] = r.astype(BF)
 
-    io.ready("xa", "xb", "wa", "wb")
+    io.ready("xa", "xb", "wa", "wb", "one")
     io.start(1)
     line.step(3)
-    io.ready("one")
     for n in range(4):
         for group, x_ref, near, far, got in sets:
             order = (3, group.away[0], group.stay[1], 0)
@@ -1308,28 +1333,9 @@
     add_near(2)
     add_near(3)
     line.step(1)
-    for group, *_ in sets:
-        group.first_sums(0)
-    line.close()
-    step = 32
-    gain_sum[...] = jnp.zeros_like(gain_sum)
-    io.ready("tokens", "hid")
-
-    @pl.loop(0, 2 * rows // step)
-    def _(r):
-        at = pl.ds(pl.multiple_of(r * step, step), step)
-        hat, scale = normed(tok_ref[at, :].astype(F32))
-        grad = out_ref[at, :]
-        gain_sum[...] += jnp.sum(grad * hat, axis=0, keepdims=True)
-        out_ref[at, :] = norm_back(grad * gain_ref[0:1, :], hat, scale)
-        for k in range(4):
-            out_ref[at, chip_chunk(k, 2 * width)] += hid_ref[
-                at, k * 2 * width : (k + 1) * 2 * width
-            ]
-
-    small[...] = jnp.zeros_like(small)
+    line.own()
     for p in range(8):
-        small[p, 0:1, :] = gain_sum[:, chunk_of(p, width)]
+        small[p, 0:1, :] = small[p, 0:1, :] / gain_ref[0:1, chunk_of(p, width)]
         small[p, 1:2, :] = gain_two_ref[:, chip_order(p, width)]
 
     def pass_small(i, src, dst, to):
@@ -1354,6 +1360,8 @@
     for c in sent:
         c.start()
     for group, *_ in sets:
+        group.first_sums(0)
+    for group, *_ in sets:
         group.first_sums(1)
     total = small[0]
     for p in range(1, 8):
@@ -1365,6 +1373,20 @@
     ]
     for c in last:
         c.start()
+    io.ready("tokens", "hid")
+    line.close()
+    step = 32
+
+    @pl.loop(0, 2 * rows // step)
+    def _(r):
+        at = pl.ds(pl.multiple_of(r * step, step), step)
+        hat, scale = normed(tok_ref[at, :].astype(F32))
+        out_ref[at, :] = norm_back(out_ref[at, :] * gain_ref[0:1, :], hat, scale)
+        for k in range(4):
+            out_ref[at, chip_chunk(k, 2 * width)] += hid_ref[
+                at, k * 2 * width : (k + 1) * 2 * width
+            ]
+
     for (group, *_), out in zip(sets, (sum_a_ref, sum_b_ref)):
         group.finish(out)
     for k in range(1, 4):
@@ -1616,8 +1638,6 @@
     states.near()
     local(1)
     states.far()
-    to_pair.wait_recv()
-    through.start()
     states.settle()
     for h in range(2):
 
@@ -1635,12 +1655,12 @@
             g = gate_ref[m, at, cols]
             mixed_ref[m, at, cols] = (g * sigmoid(g) * normed(kept)[0]).astype(BF)
 
-        if h == 0:
-            to_other.wait_recv()
-            through.wait_recv()
-            io.done("douts")
-
     states.finish()
+    to_pair.wait_recv()
+    through.start()
+    to_other.wait_recv()
+    through.wait_recv()
+    io.done("douts")
     for c in send_rows:
         c.wait_send()
 
@@ -2176,7 +2196,10 @@
             sems(4),
             sems(3),
             sems(3),
-            sems(10),
+            sems(13),
+            pltpu.VMEM(out_weight.shape, BF),
+            pltpu.VMEM((up_weight.shape[0], units // 2), BF),
+            pltpu.VMEM((units // 2, down_weight.shape[1]), BF),
         ]
         + state_scratch(state),
         2 * micro * wide * width * (na + nb),
@@ -2219,7 +2242,7 @@
         ],
         line_scratch(count, micro * rows, width)
         + [sems(2, count - 1)] * 2
-        + [sems(2, 3), sems(2, 3), sems(2)],
+        + [sems(2, 3), sems(2, 3), sems(4), pltpu.VMEM(up.shape, BF), pltpu.VMEM(down.shape, BF)],
         2 * micro * wide * hidden * width,
         mixed,
         w_out,
@@ -2374,7 +2397,7 @@
     out = call(
         close_rows_kernel,
         3,
-        [Late("xa"), Late("xb"), Late("wa"), Late("wb"), Late("one", 1), Late("tokens", 1)]
+        [Late("xa"), Late("xb"), Late("wa"), Late("wb"), Late("one"), Late("tokens", 1)]
         + [Late("hid", 1), vmem(), vmem()],
         [
             ((micro * rows, width), F32, vmem()),
@@ -2390,7 +2413,6 @@
             pltpu.VMEM((2, piece, nb), BF),
             pltpu.VMEM((7, piece, na), BF),
             pltpu.VMEM((7, piece, nb), BF),
-            pltpu.VMEM((1, width), F32),
             pltpu.VMEM((8, 8, piece), F32),
             pltpu.VMEM((8, 8, piece), F32),
             pltpu.VMEM((4, 8, piece), F32),

time: 558 us -> 549 us (0.984)
  Pallas kernels: 552 us -> 543 us
    pallas_call x6, Pallas kernels: 545 us -> 536 us  [call(): pl.pallas_call(whole, out_shape=[like(shape, kind) for shape, kind, _ in...]
where the time goes in v6:
time: 549 us; the launch traced here: 547 us
  Pallas kernels  543 us (99%)
    pallas_call x6, Pallas kernels, call(): pl.pallas_call(whole, out_shape=[like(shape, kind) for shape, kind, _ in...  536 us

profile of v6, /device:TPU:0, one launch (start us, length us, event | category | flops | bytes accessed | tf_op | source)
XLA Modules:
  0.0 547.1 jit_solution(2774427834491635472)
XLA Ops:
  0.6 0.7 stack.9
  1.3 0.7 stack.10
  2.0 0.6 maximum_convert_fusion.refs_4_
  2.5 151.0 %shard_map.212 = (bf16[2,512,2048]{2,1,0:T(8,128)(2,1)}, bf16[2,512,1536]{2,1,0:T(8,128)(2,1)}, bf16[2,512,512]{2,1,0:T(8,128)(2,1)}, f32[2,512,1024]{2,1,0:T(8,...) custom-call(f32[8]{0:T(128)} %refs_0_.3, ...), custom_call_target="tpu_custom_call" | custom-call | flops 12884901888 | bytes 5244976 | tf_op jit(solution)/shard_map/pallas_call | solution.py:1999
  153.6 82.4 %shard_map.213 = (f32[256,2048]{1,0:T(8,128)}, bf16[2048,1024]{1,0:T(8,128)(2,1)}, bf16[1024,2048]{1,0:T(8,128)(2,1)}) custom-call(bf16[2,512,1024]{2,1,0:T(8,128)(2,1)} %get-tuple-element.62.refs_0_.refs_2_, bf16[1024,2048]{1,0:T(8,128)(2,1)} %get-tuple-element.63.refs_1_, bf16[256,2048]{1,0:T(8,128)(2,1)} %bitcast.16, ...), custom_call_target="tpu_custom_call" | custom-call | flops 4294967296 | bytes 9437184 | tf_op jit(solution)/shard_map/pallas_call | solution.py:1999
  236.0 65.2 %shard_map.214 = (f32[256,2048]{1,0:T(8,128)}, bf16[256,2048]{1,0:T(8,128)(2,1)}, f32[256,2048]{1,0:T(8,128)}, bf16[256,2048]{1,0:T(8,128)(2,1)}, f32[1,2048]{1,...) custom-call(f32[256,2048]{1,0:T(8,128)} %get-tuple-element.66.refs_0_, ...), custom_call_target="tpu_custom_call" | custom-call | flops 25769803776 | bytes 14745600 | tf_op jit(solution)/shard_map/pallas_call | solution.py:1999
  301.3 80.2 %shard_map.215 = (f32[2,512,1024]{2,1,0:T(8,128)}, bf16[2,8,256,512]{3,2,1,0:T(8,128)(2,1)}, bf16[512,1024]{1,0:T(8,128)(2,1)}, bf16[1024,512]{1,0:T(8,128)(2,1)}) custom-call(bf16[256,2048]{1,0:T(8,128)(2,1)} %get-tuple-element.71.refs_0_, bf16[1024,2048]{1,0:T(8,128)(2,1)} %get-tuple-element.63.refs_1_, ...), custom_call_target="tpu_custom_call" | custom-call | flops 8589934592 | bytes 15728640 | tf_op jit(solution)/shard_map/pallas_call | solution.py:1999
  381.5 60.8 %shard_map.216 = (bf16[2,512,1536]{2,1,0:T(8,128)(2,1)}, bf16[2,512,1536]{2,1,0:T(8,128)(2,1)}, bf16[2,256,512]{2,1,0:T(8,128)(2,1)}, bf16[256,2048]{1,0:T(8,128...) custom-call(f32[8]{0:T(128)} %refs_0_.3, s32[2,2]{1,0:T(2,128)} %refs_1_.3, ...), custom_call_target="tpu_custom_call" | custom-call | flops 4831838208 | bytes 27263024 | tf_op jit(solution)/shard_map/pallas_call | solution.py:1999
  442.3 96.2 %shard_map.217 = (f32[256,2048]{1,0:T(8,128)}, bf16[256,1536]{1,0:T(8,128)(2,1)}, bf16[256,1536]{1,0:T(8,128)(2,1)}, f32[8,256]{1,0:T(8,128)}) custom-call(bf16[1024,1536]{1,0:T(8,128)(2,1)} %bitcast.11, bf16[1024,1536]{1,0:T(8,128)(2,1)} %bitcast.12, bf16[2048,1536]{1,0:T(8,128)(2,1)} %get-tuple-element.84.refs_2_, ...), custom_call_target="tpu_custom_call" | custom-call | flops 25769803776 | bytes 26288128 | tf_op jit(solution)/shard_map/pallas_call | solution.py:1999
  538.5 1.3 fusion
  539.8 7.0 %shard_map.218 = (bf16[256,2048]{1,0:T(8,128)(2,1)}, f32[256,2048]{1,0:T(8,128)}, f32[256,512]{1,0:T(8,128)}, f32[256,512]{1,0:T(8,128)}, f32[256,1024]{1,0:T(8,...) custom-call(bf16[256,2048]{1,0:T(8,128)(2,1)} %get-tuple-element.81.block_in, ...), custom_call_target="tpu_custom_call" | custom-call | tf_op jit(solution)/shard_map/pallas_call | solution.py:2052

commit v7 on v6

--- a/solution.py
+++ b/solution.py
@@ -738,6 +738,10 @@
         for c in away:
             c.start()
 
+    @pl.when(inside)
+    def _():
+        send_rows[0].start()
+
     for item in items[1:3]:
         item.corner()
     for item in items[1:3]:
@@ -785,7 +789,6 @@
     def _():
         for c in away:
             c.wait_recv()
-        send_rows[0].start()
         for c in away:
             c.start()
 

time: 549 us -> 538 us (0.980)
  Pallas kernels: 543 us -> 529 us
    pallas_call x6, Pallas kernels: 536 us -> 522 us  [call(): pl.pallas_call(whole, out_shape=[like(shape, kind) for shape, kind, _ in...]
where the time goes in v7:
time: 538 us; the launch traced here: 533 us
  Pallas kernels  529 us (98%)
    pallas_call x6, Pallas kernels, call(): pl.pallas_call(whole, out_shape=[like(shape, kind) for shape, kind, _ in...  522 us

profile of v7, /device:TPU:0, one launch (start us, length us, event | category | flops | bytes accessed | tf_op | source)
XLA Modules:
  0.0 532.8 jit_solution(1183174110415413577)
XLA Ops:
  0.6 0.7 stack.9
  1.3 0.7 stack.10
  2.0 0.6 maximum_convert_fusion.refs_4_
  2.5 141.5 %shard_map.212 = (bf16[2,512,2048]{2,1,0:T(8,128)(2,1)}, bf16[2,512,1536]{2,1,0:T(8,128)(2,1)}, bf16[2,512,512]{2,1,0:T(8,128)(2,1)}, f32[2,512,1024]{2,1,0:T(8,...) custom-call(f32[8]{0:T(128)} %refs_0_.3, ...), custom_call_target="tpu_custom_call" | custom-call | flops 12884901888 | bytes 5244976 | tf_op jit(solution)/shard_map/pallas_call | solution.py:2002
  144.0 78.6 %shard_map.213 = (f32[256,2048]{1,0:T(8,128)}, bf16[2048,1024]{1,0:T(8,128)(2,1)}, bf16[1024,2048]{1,0:T(8,128)(2,1)}) custom-call(bf16[2,512,1024]{2,1,0:T(8,128)(2,1)} %get-tuple-element.62.refs_0_.refs_2_, bf16[1024,2048]{1,0:T(8,128)(2,1)} %get-tuple-element.63.refs_1_, bf16[256,2048]{1,0:T(8,128)(2,1)} %bitcast.16, ...), custom_call_target="tpu_custom_call" | custom-call | flops 4294967296 | bytes 9437184 | tf_op jit(solution)/shard_map/pallas_call | solution.py:2002
  222.7 62.7 %shard_map.214 = (f32[256,2048]{1,0:T(8,128)}, bf16[256,2048]{1,0:T(8,128)(2,1)}, f32[256,2048]{1,0:T(8,128)}, bf16[256,2048]{1,0:T(8,128)(2,1)}, f32[1,2048]{1,...) custom-call(f32[256,2048]{1,0:T(8,128)} %get-tuple-element.66.refs_0_, ...), custom_call_target="tpu_custom_call" | custom-call | flops 25769803776 | bytes 14745600 | tf_op jit(solution)/shard_map/pallas_call | solution.py:2002
  285.4 81.3 %shard_map.215 = (f32[2,512,1024]{2,1,0:T(8,128)}, bf16[2,8,256,512]{3,2,1,0:T(8,128)(2,1)}, bf16[512,1024]{1,0:T(8,128)(2,1)}, bf16[1024,512]{1,0:T(8,128)(2,1)}) custom-call(bf16[256,2048]{1,0:T(8,128)(2,1)} %get-tuple-element.71.refs_0_, bf16[1024,2048]{1,0:T(8,128)(2,1)} %get-tuple-element.63.refs_1_, ...), custom_call_target="tpu_custom_call" | custom-call | flops 8589934592 | bytes 15728640 | tf_op jit(solution)/shard_map/pallas_call | solution.py:2002
  366.6 61.4 %shard_map.216 = (bf16[2,512,1536]{2,1,0:T(8,128)(2,1)}, bf16[2,512,1536]{2,1,0:T(8,128)(2,1)}, bf16[2,256,512]{2,1,0:T(8,128)(2,1)}, bf16[256,2048]{1,0:T(8,128...) custom-call(f32[8]{0:T(128)} %refs_0_.3, s32[2,2]{1,0:T(2,128)} %refs_1_.3, ...), custom_call_target="tpu_custom_call" | custom-call | flops 4831838208 | bytes 27263024 | tf_op jit(solution)/shard_map/pallas_call | solution.py:2002
  428.1 96.2 %shard_map.217 = (f32[256,2048]{1,0:T(8,128)}, bf16[256,1536]{1,0:T(8,128)(2,1)}, bf16[256,1536]{1,0:T(8,128)(2,1)}, f32[8,256]{1,0:T(8,128)}) custom-call(bf16[1024,1536]{1,0:T(8,128)(2,1)} %bitcast.11, bf16[1024,1536]{1,0:T(8,128)(2,1)} %bitcast.12, bf16[2048,1536]{1,0:T(8,128)(2,1)} %get-tuple-element.84.refs_2_, ...), custom_call_target="tpu_custom_call" | custom-call | flops 25769803776 | bytes 26288128 | tf_op jit(solution)/shard_map/pallas_call | solution.py:2002
  524.3 1.3 fusion
  525.6 7.0 %shard_map.218 = (bf16[256,2048]{1,0:T(8,128)(2,1)}, f32[256,2048]{1,0:T(8,128)}, f32[256,512]{1,0:T(8,128)}, f32[256,512]{1,0:T(8,128)}, f32[256,1024]{1,0:T(8,...) custom-call(bf16[256,2048]{1,0:T(8,128)(2,1)} %get-tuple-element.81.block_in, ...), custom_call_target="tpu_custom_call" | custom-call | tf_op jit(solution)/shard_map/pallas_call | solution.py:2055

commit v8 on v7

--- a/solution.py
+++ b/solution.py
@@ -1658,6 +1658,7 @@
             g = gate_ref[m, at, cols]
             mixed_ref[m, at, cols] = (g * sigmoid(g) * normed(kept)[0]).astype(BF)
 
+    io.done("mixed", "kept")
     states.finish()
     to_pair.wait_recv()
     through.start()
@@ -1887,6 +1888,7 @@
             else:
                 xa_ref[m, at, 2 * qk :] = gv
 
+    io.done("xa", "xb")
     states.finish()
     give.wait()
     io.ready("keep")
@@ -2075,8 +2077,8 @@
         + [Late("a", 1), Late("high", 1), Late("gate"), Late("kept"), Late("grad"), Late("state", 1)]
         + [anywhere(), Late("keep", 1), anywhere(), Late("up"), Late("down")],
         [
-            ((micro, length, a.shape[2]), BF, vmem()),
-            ((micro, length, 3 * vd), BF, vmem()),
+            ((micro, length, a.shape[2]), BF, Early("xa")),
+            ((micro, length, 3 * vd), BF, Early("xb")),
             ((2, *part.shape[2:]), BF, vmem()),
             (give.shape, BF, vmem()),
             ((rows, 2 * units), F32, vmem()),
@@ -2181,8 +2183,8 @@
             ((8, width), F32, vmem()),
             ((2 * piece, units), BF, anywhere()),
             ((units, 2 * piece), BF, anywhere()),
-            ((micro, wide, 2 * high), BF, vmem()),
-            ((micro, wide, 2 * high), F32, vmem()),
+            ((micro, wide, 2 * high), BF, Early("mixed")),
+            ((micro, wide, 2 * high), F32, Early("kept")),
             (state, BF, vmem()),
             ((4 * own, width), BF, Early("douts")),
         ],

time: 538 us -> 537 us (level)
  no operation moved by 1% of the time
where the time goes in v8:
time: 537 us; the launch traced here: 532 us
  Pallas kernels  528 us (98%)
    pallas_call x6, Pallas kernels, call(): pl.pallas_call(whole, out_shape=[like(shape, kind) for shape, kind, _ in...  521 us

profile of v8, /device:TPU:0, one launch (start us, length us, event | category | flops | bytes accessed | tf_op | source)
XLA Modules:
  0.0 531.8 jit_solution(9110528431169960044)
XLA Ops:
  0.6 0.7 stack.9
  1.3 0.7 stack.10
  2.0 0.6 maximum_convert_fusion.refs_4_
  2.5 139.5 %shard_map.212 = (bf16[2,512,2048]{2,1,0:T(8,128)(2,1)}, bf16[2,512,1536]{2,1,0:T(8,128)(2,1)}, bf16[2,512,512]{2,1,0:T(8,128)(2,1)}, f32[2,512,1024]{2,1,0:T(8,...) custom-call(f32[8]{0:T(128)} %refs_0_.3, ...), custom_call_target="tpu_custom_call" | custom-call | flops 12884901888 | bytes 5244976 | tf_op jit(solution)/shard_map/pallas_call | solution.py:2004
  142.1 80.5 %shard_map.213 = (f32[256,2048]{1,0:T(8,128)}, bf16[2048,1024]{1,0:T(8,128)(2,1)}, bf16[1024,2048]{1,0:T(8,128)(2,1)}) custom-call(bf16[2,512,1024]{2,1,0:T(8,128)(2,1)} %get-tuple-element.62.refs_0_.refs_2_, bf16[1024,2048]{1,0:T(8,128)(2,1)} %get-tuple-element.63.refs_1_, bf16[256,2048]{1,0:T(8,128)(2,1)} %bitcast.16, ...), custom_call_target="tpu_custom_call" | custom-call | flops 4294967296 | bytes 9437184 | tf_op jit(solution)/shard_map/pallas_call | solution.py:2004
  222.6 63.2 %shard_map.214 = (f32[256,2048]{1,0:T(8,128)}, bf16[256,2048]{1,0:T(8,128)(2,1)}, f32[256,2048]{1,0:T(8,128)}, bf16[256,2048]{1,0:T(8,128)(2,1)}, f32[1,2048]{1,...) custom-call(f32[256,2048]{1,0:T(8,128)} %get-tuple-element.66.refs_0_, ...), custom_call_target="tpu_custom_call" | custom-call | flops 25769803776 | bytes 14745600 | tf_op jit(solution)/shard_map/pallas_call | solution.py:2004
  285.8 80.9 %shard_map.215 = (f32[2,512,1024]{2,1,0:T(8,128)}, bf16[2,8,256,512]{3,2,1,0:T(8,128)(2,1)}, bf16[512,1024]{1,0:T(8,128)(2,1)}, bf16[1024,512]{1,0:T(8,128)(2,1)}) custom-call(bf16[256,2048]{1,0:T(8,128)(2,1)} %get-tuple-element.71.refs_0_, bf16[1024,2048]{1,0:T(8,128)(2,1)} %get-tuple-element.63.refs_1_, ...), custom_call_target="tpu_custom_call" | custom-call | flops 8589934592 | bytes 15728640 | tf_op jit(solution)/shard_map/pallas_call | solution.py:2004
  366.6 59.5 %shard_map.216 = (bf16[2,512,1536]{2,1,0:T(8,128)(2,1)}, bf16[2,512,1536]{2,1,0:T(8,128)(2,1)}, bf16[2,256,512]{2,1,0:T(8,128)(2,1)}, bf16[256,2048]{1,0:T(8,128...) custom-call(f32[8]{0:T(128)} %refs_0_.3, s32[2,2]{1,0:T(2,128)} %refs_1_.3, ...), custom_call_target="tpu_custom_call" | custom-call | flops 4831838208 | bytes 27263024 | tf_op jit(solution)/shard_map/pallas_call | solution.py:2004
  426.2 97.0 %shard_map.217 = (f32[256,2048]{1,0:T(8,128)}, bf16[256,1536]{1,0:T(8,128)(2,1)}, bf16[256,1536]{1,0:T(8,128)(2,1)}, f32[8,256]{1,0:T(8,128)}) custom-call(bf16[1024,1536]{1,0:T(8,128)(2,1)} %bitcast.11, bf16[1024,1536]{1,0:T(8,128)(2,1)} %bitcast.12, bf16[2048,1536]{1,0:T(8,128)(2,1)} %get-tuple-element.84.refs_2_, ...), custom_call_target="tpu_custom_call" | custom-call | flops 25769803776 | bytes 26288128 | tf_op jit(solution)/shard_map/pallas_call | solution.py:2004
  523.2 1.3 fusion
  524.5 7.0 %shard_map.218 = (bf16[256,2048]{1,0:T(8,128)(2,1)}, f32[256,2048]{1,0:T(8,128)}, f32[256,512]{1,0:T(8,128)}, f32[256,512]{1,0:T(8,128)}, f32[256,1024]{1,0:T(8,...) custom-call(bf16[256,2048]{1,0:T(8,128)(2,1)} %get-tuple-element.81.block_in, ...), custom_call_target="tpu_custom_call" | custom-call | tf_op jit(solution)/shard_map/pallas_call | solution.py:2057
